TPU v7x, 512 devices: a whole 4x4x16 slice. The times are simulated.
512 devices in a mesh: expert: 64 (over x, z), tensor: 8 (over y, core).
Axes of the slice: x: 4, y: 4, z: 16, core: 2. Of those that a mesh axis runs over, the one named last changes fastest.
Arguments:
- context: bfloat16 [2048, 3072], P('expert', 'tensor'), may hold values from -6 to 6
- out_weight: bfloat16 [3072, 3072], P('tensor', 'expert'), may hold values from -0.109375 to 0.109375
- residual: bfloat16 [2048, 3072], P(('expert', 'tensor')), may hold values from -6 to 6
- norm_gain: bfloat16 [3072], replicated, may hold values from 0.099609375 to 1.8984375
- router_weight: bfloat16 [3072, 16], replicated, may hold values from -0.109375 to 0.109375
- gate_weight: bfloat16 [3072, 131072], P(None, ('expert', 'tensor')), may hold values from -0.109375 to 0.109375
- up_weight: bfloat16 [3072, 131072], P(None, ('expert', 'tensor')), may hold values from -0.109375 to 0.109375
- down_weight: bfloat16 [131072, 3072], P(('expert', 'tensor')), may hold values from -0.0625 to 0.0625
- expert_ids: int32 [2048, 4], P(('expert', 'tensor')), may hold values from 0 to 15, all different within a row; in each aligned block of 4 rows (0 to 3, 4 to 7, ...) at most 2 rows name the same one
Outputs:
- hidden_state: bfloat16 [2048, 3072], P(('expert', 'tensor'))
- expert_mix: bfloat16 [2048, 3072], P(('expert', 'tensor'))
Inputs may be any that keep to these rules, and one draw needn't show every extreme that they name: `expert_ids`: each row names 4 different experts; among the 4 rows of one device no expert is named more than 2 times.
All inputs are finite; a program needn't handle non-finite values.
Results may differ from a plain program's by a relative error of at most 0.013.
Values may be sent and summed in bfloat16 or wider, within the bound.
No kernel may reach another device: no remote copies, remote signals or barrier semaphores. Data moves between devices by JAX's collectives and lax.ppermute only.
A program may use at most 128 MiB of HBM per device.

v0:
```python
import jax
import jax.numpy as jnp
from jax import lax
from jax.sharding import PartitionSpec as P

CAP = 2


norm_epsilon = 1e-05


def layer_norm(state, norm_gain):
    values = state.astype(jnp.float32)
    row_mean = jnp.mean(values, axis=-1, keepdims=True)
    centred = values - row_mean
    variance = jnp.mean(centred * centred, axis=-1, keepdims=True)
    return (centred * lax.rsqrt(variance + norm_epsilon) * norm_gain.astype(jnp.float32)).astype(
        jnp.bfloat16
    )


def swiglu_part(row_block, gate_weight, up_weight, down_weight):
    gate_value = jnp.dot(row_block, gate_weight, preferred_element_type=jnp.float32)
    up_value = jnp.dot(row_block, up_weight, preferred_element_type=jnp.float32)
    hidden = (jax.nn.silu(gate_value) * up_value).astype(jnp.bfloat16)
    return jnp.dot(hidden, down_weight, preferred_element_type=jnp.float32).astype(jnp.bfloat16)


def on_device(
    context,
    out_weight,
    residual,
    norm_gain,
    router_weight,
    gate_weight,
    up_weight,
    down_weight,
    expert_ids,
):
    n_expert = lax.axis_size("expert")
    model_width = residual.shape[1]
    experts = router_weight.shape[1]
    wide_weight = lax.all_gather(out_weight, "expert", axis=1, tiled=True)
    attention_sum = lax.psum_scatter(
        jnp.dot(context, wide_weight, preferred_element_type=jnp.float32),
        "tensor",
        scatter_dimension=0,
        tiled=True,
    )
    hidden_state = (residual.astype(jnp.float32) + attention_sum).astype(jnp.bfloat16)
    normed = layer_norm(hidden_state, norm_gain)
    logits = jnp.dot(normed, router_weight, preferred_element_type=jnp.float32)
    matches = expert_ids[:, :, None] == jnp.arange(experts, dtype=jnp.int32)[None, None, :]
    picked = jnp.sum(jnp.where(matches, logits[:, None, :], 0.0), axis=2)
    scores = jnp.exp(picked)
    route_weight = scores / jnp.sum(scores, axis=1, keepdims=True)
    onehot = matches.astype(jnp.int32)
    present = jnp.sum(onehot, axis=1)
    before = jnp.cumsum(present, axis=0) - present
    slot_rank = jnp.sum(onehot * before[:, None, :], axis=2)
    cell_index = expert_ids * CAP + slot_rank
    assign = jnp.any(
        cell_index[:, :, None] == jnp.arange(experts * CAP, dtype=jnp.int32)[None, None, :], axis=1
    )
    send_rows = jnp.dot(
        assign.astype(jnp.bfloat16).T, normed, preferred_element_type=jnp.float32
    ).astype(jnp.bfloat16)
    send_rows = send_rows.reshape(experts, CAP, model_width)
    group_size = n_expert // experts
    outgoing = jnp.repeat(send_rows, group_size, axis=0)
    landed = lax.all_to_all(outgoing, "expert", split_axis=0, concat_axis=0, tiled=True)
    arrived = lax.all_gather(landed[None], "tensor", axis=0, tiled=True)
    arrived_shape = arrived.shape
    slot_rows = arrived.reshape(-1, model_width)
    row_total = slot_rows.shape[0]
    block_span = 512
    blocked = slot_rows.reshape(row_total // block_span, block_span, model_width)

    def span_part(row_block):
        return swiglu_part(row_block, gate_weight, up_weight, down_weight)

    partial_value = lax.map(span_part, blocked).reshape(row_total, model_width)
    partial_value = partial_value.reshape(arrived_shape)
    returned = lax.all_to_all(
        lax.all_to_all(partial_value, "expert", split_axis=1, concat_axis=1, tiled=True),
        "tensor",
        split_axis=0,
        concat_axis=0,
        tiled=True,
    )
    summed = returned.astype(jnp.float32).reshape(-1, experts, group_size, CAP, model_width)
    summed = jnp.sum(summed, axis=(0, 2)).reshape(experts * CAP, model_width)
    chosen = summed[cell_index]
    expert_mix = jnp.sum(route_weight[:, :, None] * chosen, axis=1).astype(jnp.bfloat16)
    return (hidden_state, expert_mix)


def solution(mesh):
    placed = (
        P("expert", "tensor"),
        P("tensor", "expert"),
        P(("expert", "tensor"), None),
        P(),
        P(),
        P(None, ("expert", "tensor")),
        P(None, ("expert", "tensor")),
        P(("expert", "tensor"), None),
        P(("expert", "tensor"), None),
    )
    return jax.shard_map(
        on_device,
        mesh=mesh,
        in_specs=placed,
        out_specs=(P(("expert", "tensor"), None), P(("expert", "tensor"), None)),
        check_vma=False,
    )
```

profile of v0, /device:TPU:6, one launch (start us, length us, event | category | flops | bytes accessed | tf_op | source)
XLA Modules:
  0.0 778.1 jit_solution(11295594086046768477)
XLA Ops:
  7.2 0.0 copy-start
  7.2 0.0 copy-start.2
  7.2 0.0 copy-start.4
  7.2 0.0 copy-start.3
  7.2 0.0 all-gather.4.cloned.1.call-start
  7.3 0.7 all-gather.4.cloned.1.call-update
  7.9 0.0 all-reduce.3.cloned.1.call-start
  8.0 0.8 convert_reduce_fusion.2
  8.8 0.9 select_reduce_fusion
  9.7 146.3 %all-gather.4.cloned.1.call-done = bf16[384,3072]{0,1:T(8,128)(2,1)} async-done(((bf16[384,48]{0,1:T(8,128)(2,1)}), bf16[384,3072]{0,1:T(8,128)(2,1)}) %all-gather.4.cloned.1.call-update) | async-done | bytes 2359312 | tf_op jit(solution)/shard_map/all_gather | solution.py:43
  156.0 3.3 fusion.37
  159.2 0.0 all-reduce.3.cloned.1.call-update
  159.3 0.0 all-gather.6.cloned.1.call-start
  159.3 0.0 copy-done.2
  159.3 0.0 copy-done.4
  159.4 1.3 dynamic-slice
  161.3 0.1 fusion.32
  161.4 70.6 %all-reduce.3.cloned.1.call-done = f32[32,3072]{1,0:T(8,128)} async-done(((f32[32,3072]{1,0:T(8,128)}), f32[32,3072]{1,0:T(8,128)}) %all-reduce.3.cloned.1.call-update) | async-done | bytes 393232
  231.9 0.0 copy-done.3
  231.9 1.0 convert_reduce_fusion.1
  233.0 0.0 copy-start.1
  233.0 0.2 fusion.28
  233.2 0.3 convolution_convert_fusion.1
  233.5 0.1 reshape.59
  233.6 0.4 broadcast_in_dim.42
  234.0 55.4 %all_to_all.15 = bf16[64,2,3072]{2,1,0:T(2,128)(2,1)} all-to-all(bf16[64,2,3072]{2,1,0:T(2,128)(2,1)S(1)} %bitcast.38), channel_id=1, replica_groups=mesh['expert'=64,'tensor'=8] {'expert'}, dimensions={0} | all-to-all | bytes 1572864 | tf_op jit(solution)/shard_map/all_to_all | solution.py:71
  289.4 0.0 all-gather.6.cloned.1.call-update
  289.4 0.0 copy-start.5
  289.4 42.5 %all-gather.6.cloned.1.call-done = bf16[512,2,3072]{2,1,0:T(2,128)(2,1)} async-done(((bf16[64,2,3072]{2,1,0:T(2,128)(2,1)}), bf16[512,2,3072]{2,1,0:T(2,128)(2,1)}) %all-gather.6.cloned.1.call-update) | async-done | bytes 6291472 | tf_op jit(solution)/shard_map/all_gather | solution.py:72
  331.9 13.6 %reshape_reshape.6 = bf16[2,512,3072]{2,1,0:T(8,128)(2,1)} reshape(bf16[512,2,3072]{2,1,0:T(2,128)(2,1)} %all-gather.6.cloned.1.call-done) | data formatting | bytes 12582912 | tf_op jit(solution)/shard_map/reshape;reshape | solution.py:77
  345.5 0.0 copy-done.5
  345.5 21.6 %while.10 = (s32[]{:T(128)}, bf16[2,512,3072]{2,1,0:T(8,128)(2,1)}, bf16[2,512,3072]{2,1,0:T(8,128)(2,1)}, bf16[3072,256]{1,0:T(8,128)(2,1)S(1)}, bf16[3072,256]...) while((s32[]{:T(128)}, bf16[2,512,3072]{2,1,0:T(8,128)(2,1)}, bf16[2,512,3072]{2,1,0:T(8,128)(2,1)}, ...), condition=%wide.region_10.11_spmd, body=%wide.region_9.10_spmd.sunk | while | flops 2418278400 | bytes 15205965 | solution.py:82
  345.5 2.9 fusion.57
  348.4 7.9 %fusion.58 = bf16[2,512,3072]{2,1,0:T(8,128)(2,1)} fusion(bf16[2,512,3072]{2,1,0:T(8,128)(2,1)} %get-tuple-element.96, s32[]{:T(128)} %get-tuple-element.95, bf16[256,3072]{1,0:T(8,128)(2,1)} %get-tuple-element.107, bf16[3072,256]{1,0:T(8,128)(2,1)} %get-tuple-element.106, bf16[2,512,3072]{2,1,0:T(8,128)(2,1)} %get-tuple-element.104, ...), kind=kOutput, calls=%fused_computation.3.clone.1 | convolution fusion | flops 1612972032 | bytes 9962496 | tf_op jit(solution)/shard_map/while/body/eval_jaxpr/dot_general | solution.py:26
  356.4 2.9 fusion.57
  359.3 7.9 %fusion.58 = bf16[2,512,3072]{2,1,0:T(8,128)(2,1)} fusion(bf16[2,512,3072]{2,1,0:T(8,128)(2,1)} %get-tuple-element.96, s32[]{:T(128)} %get-tuple-element.95, bf16[256,3072]{1,0:T(8,128)(2,1)} %get-tuple-element.107, bf16[3072,256]{1,0:T(8,128)(2,1)} %get-tuple-element.106, bf16[2,512,3072]{2,1,0:T(8,128)(2,1)} %get-tuple-element.104, ...), kind=kOutput, calls=%fused_computation.3.clone.1 | convolution fusion | flops 1612972032 | bytes 9962496 | tf_op jit(solution)/shard_map/while/body/eval_jaxpr/dot_general | solution.py:26
  367.1 13.1 %reshape_reshape.7 = bf16[8,64,2,3072]{3,2,1,0:T(2,128)(2,1)} reshape(bf16[2,512,3072]{2,1,0:T(8,128)(2,1)} %get-tuple-element.34) | data formatting | bytes 12582912 | tf_op jit(solution)/shard_map/reshape;reshape | solution.py:83
  380.2 7.1 copy.17
  387.4 291.5 %all_to_all.16 = bf16[8,64,2,3072]{3,2,0,1:T(2,128)(2,1)S(1)} all-to-all(bf16[8,64,2,3072]{3,2,0,1:T(2,128)(2,1)S(1)} %copy.17), channel_id=1, replica_groups=mesh['expert'=64,'tensor'=8] {'expert'}, dimensions={1} | all-to-all | bytes 12582912 | tf_op jit(solution)/shard_map/all_to_all | solution.py:85
  678.9 5.4 copy.18
  684.3 4.9 all-to-all-start.2
  689.2 0.1 reshape.64
  689.3 0.0 copy-done.1
  689.3 0.0 copy-done
  689.3 0.2 fusion.34
  689.5 0.2 select_reduce_fusion.1
  689.7 0.1 exponential_reduce_fusion
  689.8 0.1 exponential_divide_fusion
  689.9 71.3 %all-to-all-done.2 = bf16[8,64,2,3072]{3,2,1,0:T(2,128)(2,1)} async-done(((bf16[8,64,2,3072]{3,2,1,0:T(2,128)(2,1)}), bf16[8,64,2,3072]{3,2,1,0:T(2,128)(2,1)}, u32[]{:S(2)}, u32[]{:S(2)}) %all-to-all-start.2) | async-done | bytes 6291488 | tf_op jit(solution)/shard_map/all_to_all | solution.py:84
  761.2 8.1 %convert_reduce_fusion = f32[64,2,3072]{2,1,0:T(2,128)S(1)} fusion(bf16[8,64,2,3072]{3,2,1,0:T(2,128)(2,1)} %all-to-all-done.2), kind=kLoop, calls=%fused_computation.21 | loop fusion | flops 5898240 | bytes 7864320 | tf_op jit(solution)/shard_map/reduce_sum | solution.py:92
  769.2 0.5 bitcast_reduce_fusion
  769.8 0.3 reshape.61
  770.1 0.6 gather_fusion
  770.7 0.1 reshape.63
  770.8 0.8 multiply_reduce_fusion
  (8 shorter events, 0.1 us)
Async XLA Ops:
  7.2 682.1 %copy-start = (bf16[3072,16]{0,1:T(8,128)(2,1)S(1)}, bf16[3072,16]{0,1:T(8,128)(2,1)}, u32[]{:S(2)}) copy-start(bf16[3072,16]{0,1:T(8,128)(2,1)} %param.15) | copy-start | bytes 294916
  7.2 152.1 %copy-start.2 = (s32[4,4]{1,0:T(4,128)S(1)}, s32[4,4]{1,0:T(4,128)}, u32[]{:S(2)}) copy-start(s32[4,4]{1,0:T(4,128)} %param.19) | copy-start | bytes 196
  7.2 152.1 %copy-start.4 = (bf16[3072]{0:T(1024)(128)(2,1)S(1)}, bf16[3072]{0:T(1024)(128)(2,1)}, u32[]{:S(2)}) copy-start(bf16[3072]{0:T(1024)(128)(2,1)} %param.14) | copy-start | bytes 18436
  7.2 224.7 %copy-start.3 = (bf16[4,3072]{1,0:T(4,128)(2,1)S(1)}, bf16[4,3072]{1,0:T(4,128)(2,1)}, u32[]{:S(2)}) copy-start(bf16[4,3072]{1,0:T(4,128)(2,1)} %param.13) | copy-start | bytes 73732
  7.2 148.8 %all-gather.4.cloned.1.call-start = ((), (), s32[]{:S(2)}) async-start(), calls=%async_computation.3 | async-start | bytes 2396160 | tf_op jit(solution)/shard_map/all_gather | solution.py:43
  7.9 224.0 %all-reduce.3.cloned.1.call-start = ((), (), s32[]{:S(2)}) async-start(), calls=%async_computation.5 | async-start | bytes 786432
  159.3 172.7 %all-gather.6.cloned.1.call-start = ((), (), s32[]{:S(2)}) async-start(), calls=%async_computation.4 | async-start | bytes 7077888 | tf_op jit(solution)/shard_map/all_gather | solution.py:72
  233.0 456.3 %copy-start.1 = (bf16[4,3072]{1,0:T(4,128)(2,1)}, bf16[4,3072]{1,0:T(4,128)(2,1)S(1)}, u32[]{:S(2)}) copy-start(bf16[4,3072]{1,0:T(4,128)(2,1)S(1)} %get-tuple-element.50) | copy-start | bytes 73732
  289.4 56.1 %copy-start.5 = (bf16[3072,256]{1,0:T(8,128)(2,1)S(1)}, bf16[3072,256]{1,0:T(8,128)(2,1)}, u32[]{:S(2)}) copy-start(bf16[3072,256]{1,0:T(8,128)(2,1)} %param.16) | copy-start | bytes 4718596
  684.3 76.9 %all-to-all-start.2 = ((bf16[8,64,2,3072]{3,2,1,0:T(2,128)(2,1)}), bf16[8,64,2,3072]{3,2,1,0:T(2,128)(2,1)}, u32[]{:S(2)}, u32[]{:S(2)}) async-start(bf16[8,64,2,3072]{3,2,1,0:T(2,128)(2,1)} %copy.18), calls=%async_computation.2 | async-start | bytes 12582912 | tf_op jit(solution)/shard_map/all_to_all | solution.py:84
Sparse Core Ops, SparseCore 0:
  11.0 144.9 all-gather.3
  159.4 72.5 all-reduce.2
  289.5 42.3 all-gather.5
where the time goes:
time: 781 us; the launch traced here: 778 us
  blocking collectives  347 us (44%)
  waiting for transfers between devices  331 us (42%)
  local copies, waits for them, and re-layouts  42 us (5%)
  matrix products  25.3 us (3%)
  between operations  14.6 us (2%)
  other arithmetic  12.8 us (2%)
    all_to_all x1, blocking collectives, on_device(): lax.all_to_all(partial_value, 'expert', split_axis=1, concat_axis=1, tile...  292 us
    all_gather x1, waiting for transfers between devices, on_device(): wide_weight = lax.all_gather(out_weight, 'expert', axis=1, tiled=True)  146 us
    all_to_all x1, waiting for transfers between devices, on_device(): lax.all_to_all(lax.all_to_all(partial_value, 'expert', split_axis=1, conc...  71.3 us
    unnamed x4, waiting for transfers between devices  71.3 us
    all_to_all x1, blocking collectives, on_device(): lax.all_to_all(outgoing, 'expert', split_axis=0, concat_axis=0, tiled=True)  55.4 us
    all_gather x1, waiting for transfers between devices, on_device(): arrived = lax.all_gather(landed[None], 'tensor', axis=0, tiled=True)  42.5 us
    another operation x2, local copies, waits for them, and re-layouts, on_device(): partial_value = partial_value.reshape(arrived_shape)  20.2 us
    dot_general x2, matrix products, swiglu_part(): jnp.dot(hidden, down_weight, preferred_element_type=jnp.float32)  15.8 us
  transfers between devices with their start and end apart: 4, of which 4 were waited for; matrix products, arithmetic and copies ran while one was open for 0% of the time, Pallas kernels for 0%

commit v1 on v0

v1 whole, which is shorter than its diff:
```python
import jax
import jax.numpy as jnp
import numpy as np
from jax import lax
from jax.sharding import Mesh, PartitionSpec as P

CAP = 2
AXES = ("X", "B", "I", "Y", "C")
SIZES = (4, 4, 4, 4, 2)
EXPERT = ("X", "B", "I")
TENSOR = ("Y", "C")

norm_epsilon = 1e-05


def layer_norm(state, norm_gain):
    values = state.astype(jnp.float32)
    row_mean = jnp.mean(values, axis=-1, keepdims=True)
    centred = values - row_mean
    variance = jnp.mean(centred * centred, axis=-1, keepdims=True)
    return (centred * lax.rsqrt(variance + norm_epsilon) * norm_gain.astype(jnp.float32)).astype(
        jnp.bfloat16
    )


def swap(value, axes):
    return lax.all_to_all(value, axes, split_axis=0, concat_axis=0, tiled=True)


def attention_rows(context, out_weight):
    tokens = lax.all_gather(context, "X", axis=0, tiled=True)
    columns = lax.all_gather(out_weight.T, ("B", "I"), axis=0, tiled=True)
    partial_sum = lax.dot_general(
        tokens, columns, (((1,), (1,)), ((), ())), preferred_element_type=jnp.float32
    ).astype(jnp.bfloat16)
    width = columns.shape[0]
    pieces = swap(partial_sum.reshape(32, -1, width), ("X", "Y", "C"))
    pieces = pieces.reshape(4, 8, -1, width).astype(jnp.float32)
    return jnp.transpose(jnp.sum(pieces, axis=1), (1, 0, 2)).reshape(-1, 4 * width)


def both_cores(rows, weights, partner):
    total = None
    for gate, up, down in (weights, partner):
        gate_value = jnp.dot(rows, gate, preferred_element_type=jnp.float32)
        up_value = jnp.dot(rows, up, preferred_element_type=jnp.float32)
        hidden = (jax.nn.silu(gate_value) * up_value).astype(jnp.bfloat16)
        part = jnp.dot(hidden, down, preferred_element_type=jnp.float32)
        total = part if total is None else total + part
    return total.astype(jnp.bfloat16)


def on_device(
    context,
    out_weight,
    residual,
    norm_gain,
    router_weight,
    gate_weight,
    up_weight,
    down_weight,
    expert_ids,
):
    width = residual.shape[1]
    experts = router_weight.shape[1]
    weights = (gate_weight, up_weight, down_weight)
    partner = tuple(lax.ppermute(w, "C", [(0, 1), (1, 0)]) for w in weights)
    attention_sum = attention_rows(context, out_weight)
    hidden_state = (residual.astype(jnp.float32) + attention_sum).astype(jnp.bfloat16)
    normed = layer_norm(hidden_state, norm_gain)
    logits = jnp.dot(normed, router_weight, preferred_element_type=jnp.float32)
    matches = expert_ids[:, :, None] == jnp.arange(experts, dtype=jnp.int32)[None, None, :]
    picked = jnp.sum(jnp.where(matches, logits[:, None, :], 0.0), axis=2)
    scores = jnp.exp(picked)
    route_weight = scores / jnp.sum(scores, axis=1, keepdims=True)
    onehot = matches.astype(jnp.int32)
    present = jnp.sum(onehot, axis=1)
    before = jnp.cumsum(present, axis=0) - present
    slot_rank = jnp.sum(onehot * before[:, None, :], axis=2)
    cell_index = expert_ids * CAP + slot_rank
    cells = cell_index[:, :, None] == jnp.arange(experts * CAP, dtype=jnp.int32)[None, None, :]
    assign = jnp.any(cells, axis=1)
    send_rows = jnp.dot(
        assign.astype(jnp.bfloat16).T, normed, preferred_element_type=jnp.float32
    ).astype(jnp.bfloat16)

    at_x = swap(send_rows.reshape(4, 4 * CAP, width), "X")
    by_z = jnp.transpose(at_x.reshape(4, 4, CAP, width), (1, 0, 2, 3)).reshape(16, CAP, width)
    at_z = swap(by_z, ("B", "I")).reshape(16 * CAP, width)
    block_rows = lax.all_gather(at_z, "I", axis=0, tiled=True)
    rows = lax.all_gather(block_rows, "Y", axis=0, tiled=True)

    partial_value = both_cores(rows, weights, partner)

    def summed(value, axes, parts):
        got = swap(value.reshape(parts, -1, width), axes)
        return jnp.sum(got.astype(jnp.float32), axis=0).astype(jnp.bfloat16)

    over_y = summed(partial_value, "Y", 4)
    over_block = summed(over_y, "I", 4)
    back_z = swap(over_block.reshape(16, CAP, width), ("B", "I"))
    back_x = jnp.transpose(back_z.reshape(4, 4, CAP, width), (1, 0, 2, 3)).reshape(4, 4 * CAP, width)
    chosen = swap(back_x, "X").reshape(experts * CAP, width)
    cell_weight = jnp.sum(jnp.where(cells, route_weight[:, :, None], 0.0), axis=1)
    expert_mix = jnp.dot(
        cell_weight, chosen.astype(jnp.float32), precision=lax.Precision.HIGHEST
    ).astype(jnp.bfloat16)
    return (hidden_state, expert_mix)


def solution(mesh):
    fine = Mesh(np.asarray(mesh.devices).reshape(SIZES), AXES)
    whole = EXPERT + TENSOR
    placed = (
        P(EXPERT, TENSOR),
        P(TENSOR, EXPERT),
        P(whole, None),
        P(),
        P(),
        P(None, whole),
        P(None, whole),
        P(whole, None),
        P(whole, None),
    )
    return jax.shard_map(
        on_device,
        mesh=fine,
        in_specs=placed,
        out_specs=(P(whole, None), P(whole, None)),
        check_vma=False,
    )
```

time: 781 us -> 303 us (0.39)
  waiting for transfers between devices: 331 us -> 58.3 us
  blocking collectives: 347 us -> 167 us
  local copies, waits for them, and re-layouts: 42 us -> 2.69 us
  starting transfers between devices: 5.04 us -> 29.7 us
  other arithmetic: 12.8 us -> 3.12 us
    all_to_all x2 -> x4, blocking collectives: 347 us -> 97 us  [swap(): return lax.all_to_all(value, axes, split_axis=0, concat_axis=0, tiled=True)]
    all_gather x2 -> x1, waiting for transfers between devices: 189 us -> 33 us  [on_device(): rows = lax.all_gather(block_rows, 'Y', axis=0, tiled=True)]
    unnamed x4 -> x1, waiting for transfers between devices: 71.3 us -> 0.02 us
    all_gather x0 -> x3, blocking collectives: none -> 69.6 us  [the longest x1 36.1 us: attention_rows(): columns = lax.all_gather(out_weight.T, ('B', 'I'), axis=0, tiled=True)]
    all_to_all x1 -> x3, waiting for transfers between devices: 71.3 us -> 25.2 us  [swap(): return lax.all_to_all(value, axes, split_axis=0, concat_axis=0, tiled=True)]
    another operation x3 -> x0, local copies, waits for them, and re-layouts: 33.9 us -> none  [the longest x2 20.2 us: on_device(): partial_value = partial_value.reshape(arrived_shape)]
    all_to_all x1 -> x3, starting transfers between devices: 4.92 us -> 23.4 us  [swap(): return lax.all_to_all(value, axes, split_axis=0, concat_axis=0, tiled=True)]
    dot_general x5 -> x6, matrix products: 24.8 us -> 25.7 us  [the longest x2 17.1 us: both_cores(): part = jnp.dot(hidden, down, preferred_element_type=jnp.float32)]
  transfers between devices with their start and end apart: 4 -> 7, of which waited for: 4 -> 4; matrix products, arithmetic and copies ran while one was open for 0% -> 6% of each run, Pallas kernels for 0% -> 0%
where the time goes in v1:
time: 303 us; the launch traced here: 301 us
  blocking collectives  167 us (55%)
  waiting for transfers between devices  58.3 us (19%)
  starting transfers between devices  29.7 us (10%)
  matrix products  26.2 us (9%)
  between operations  14.2 us (5%)
  other arithmetic  3.12 us (1%)
    all_to_all x4, blocking collectives, swap(): return lax.all_to_all(value, axes, split_axis=0, concat_axis=0, tiled=True)  97 us
    all_gather x1, blocking collectives, attention_rows(): columns = lax.all_gather(out_weight.T, ('B', 'I'), axis=0, tiled=True)  36.1 us
    all_gather x1, waiting for transfers between devices, on_device(): rows = lax.all_gather(block_rows, 'Y', axis=0, tiled=True)  33 us
    all_to_all x3, waiting for transfers between devices, swap(): return lax.all_to_all(value, axes, split_axis=0, concat_axis=0, tiled=True)  25.2 us
    all_to_all x3, starting transfers between devices, swap(): return lax.all_to_all(value, axes, split_axis=0, concat_axis=0, tiled=True)  23.4 us
    all_gather x1, blocking collectives, on_device(): block_rows = lax.all_gather(at_z, 'I', axis=0, tiled=True)  18.5 us
    dot_general x2, matrix products, both_cores(): part = jnp.dot(hidden, down, preferred_element_type=jnp.float32)  17.1 us
    all_gather x1, blocking collectives, attention_rows(): tokens = lax.all_gather(context, 'X', axis=0, tiled=True)  15 us
  transfers between devices with their start and end apart: 7, of which 4 were waited for; matrix products, arithmetic and copies ran while one was open for 6% of the time, Pallas kernels for 0%

profile of v1, /device:TPU:6, one launch (start us, length us, event | category | flops | bytes accessed | tf_op | source)
XLA Modules:
  0.0 300.7 jit_solution(4838374026135812249)
XLA Ops:
  7.2 0.0 copy-start
  7.2 0.0 copy-start.3
  7.2 0.0 copy-start.5
  7.2 0.0 copy-start.4
  7.2 15.0 %all_gather.12 = bf16[128,384]{1,0:T(8,128)(2,1)S(1)} all-gather(bf16[32,384]{1,0:T(8,128)(2,1)} %param.9), channel_id=1, replica_groups=mesh['X'=4,'B'=4,'I'=4,'Y'=4,'C'=2] {'X'}, dimensions={0}, use_global_device_ids=true | all-gather | bytes 122880 | tf_op jit(solution)/shard_map/all_gather | solution.py:31
  22.2 36.1 %all_gather.13 = bf16[768,384]{1,0:T(8,128)(2,1)S(1)} all-gather(bf16[48,384]{1,0:T(8,128)(2,1)} %bitcast.44), channel_id=1, replica_groups=mesh['X'=4,'B'=4,'I'=4,'Y'=4,'C'=2] {'B','I'}, dimensions={0}, use_global_device_ids=true | all-gather | bytes 626688 | tf_op jit(solution)/shard_map/all_gather | solution.py:32
  58.3 0.3 convolution_convert_fusion.2
  58.6 0.7 reshape.87
  59.3 7.3 %all-to-all-start = ((bf16[32,4,768]{2,1,0:T(4,128)(2,1)}), bf16[32,4,768]{2,1,0:T(4,128)(2,1)S(1)}, u32[]{:S(2)}, u32[]{:S(2)}) async-start(bf16[32,4,768]{2,1,0:T(4,128)(2,1)} %reshape.87), calls=%async_computation | async-start | bytes 393216 | tf_op jit(solution)/shard_map/all_to_all | solution.py:27
  66.7 0.0 all-gather.2.cloned.1.call-start
  66.7 0.0 copy-done.3
  66.7 0.1 convert_reduce_fusion.2
  66.9 0.2 select_reduce_fusion.2
  67.1 0.0 copy-done.5
  67.1 0.1 fusion.16
  67.2 5.9 %all-to-all-done = bf16[32,4,768]{2,1,0:T(4,128)(2,1)S(1)} async-done(((bf16[32,4,768]{2,1,0:T(4,128)(2,1)}), bf16[32,4,768]{2,1,0:T(4,128)(2,1)S(1)}, u32[]{:S(2)}, u32[]{:S(2)}) %all-to-all-start) | async-done | bytes 196640 | tf_op jit(solution)/shard_map/all_to_all | solution.py:27
  73.1 0.1 convert_reduce_fusion
  73.2 0.0 copy-done.4
  73.2 0.1 convert_reduce_fusion.1
  73.3 0.0 copy-start.2
  73.3 0.2 fusion.13
  73.5 0.3 fusion
  73.8 9.1 %all_to_all.35 = bf16[4,8,3072]{2,1,0:T(8,128)(2,1)S(1)} all-to-all(bf16[4,8,3072]{2,1,0:T(8,128)(2,1)S(1)} %fusion), channel_id=1, replica_groups=mesh['X'=4,'B'=4,'I'=4,'Y'=4,'C'=2] {'X'}, dimensions={0} | all-to-all | bytes 393216 | tf_op jit(solution)/shard_map/all_to_all | solution.py:27
  82.9 0.2 copy.19
  83.1 0.2 copy.20
  83.2 22.6 %all_to_all.36 = bf16[16,2,3072]{2,1,0:T(2,128)(2,1)S(1)} all-to-all(bf16[16,2,3072]{2,1,0:T(2,128)(2,1)S(1)} %bitcast.41), channel_id=1, replica_groups=mesh['X'=4,'B'=4,'I'=4,'Y'=4,'C'=2] {'B','I'}, dimensions={0} | all-to-all | bytes 393216 | tf_op jit(solution)/shard_map/all_to_all | solution.py:27
  105.9 0.1 reshape.92
  105.9 18.5 %all_gather.14 = bf16[128,3072]{1,0:T(8,128)(2,1)} all-gather(bf16[32,3072]{1,0:T(8,128)(2,1)S(1)} %reshape.92), channel_id=1, replica_groups=mesh['X'=4,'B'=4,'I'=4,'Y'=4,'C'=2] {'I'}, dimensions={0}, use_global_device_ids=true | all-gather | bytes 983040 | tf_op jit(solution)/shard_map/all_gather | solution.py:90
  124.5 0.0 all-gather.2.cloned.1.call-update
  124.5 1.9 collective-permute-start
  126.4 2.4 collective-permute-start.1
  128.8 1.9 collective-permute-start.2
  130.8 33.0 %all-gather.2.cloned.1.call-done = bf16[512,3072]{1,0:T(8,128)(2,1)} async-done(((bf16[128,3072]{1,0:T(8,128)(2,1)}), bf16[512,3072]{1,0:T(8,128)(2,1)}) %all-gather.2.cloned.1.call-update) | async-done | bytes 3145744 | tf_op jit(solution)/shard_map/all_gather | solution.py:91
  163.8 0.0 copy-start.1
  163.8 4.3 %fusion.24 = f32[512,256]{1,0:T(8,128)} fusion(bf16[512,3072]{1,0:T(8,128)(2,1)} %all-gather.2.cloned.1.call-done, bf16[3072,256]{1,0:T(8,128)(2,1)} %param.14), kind=kOutput, calls=%fused_computation.42 | convolution fusion | flops 805306368 | bytes 5242880 | tf_op jit(solution)/shard_map/dot_general | solution.py:45
  168.1 0.0 collective-permute-done
  168.1 0.0 copy-done.1
  168.1 3.2 %fusion.25 = f32[512,256]{1,0:T(8,128)} fusion(bf16[512,3072]{1,0:T(8,128)(2,1)S(1)} %copy-done.1, bf16[3072,256]{1,0:T(8,128)(2,1)} %collective-permute-done), kind=kOutput, calls=%fused_computation.43 | convolution fusion | flops 805306368 | bytes 5242880 | tf_op jit(solution)/shard_map/dot_general | solution.py:45
  171.3 8.1 %fusion.2 = f32[512,3072]{1,0:T(8,128)} fusion(bf16[256,3072]{1,0:T(8,128)(2,1)} %param.16, bf16[512,3072]{1,0:T(8,128)(2,1)S(1)} %copy-done.1, bf16[3072,256]{1,0:T(8,128)(2,1)} %param.15, f32[512,256]{1,0:T(8,128)} %fusion.24), kind=kOutput, calls=%fused_computation.6 | convolution fusion | flops 1611399168 | bytes 13107200 | tf_op jit(solution)/shard_map/dot_general | solution.py:48
  179.4 0.0 collective-permute-done.1
  179.4 0.0 collective-permute-done.2
  179.4 9.0 %add_convert_fusion = bf16[512,3072]{1,0:T(8,128)(2,1)} fusion(f32[512,3072]{1,0:T(8,128)} %fusion.2, bf16[256,3072]{1,0:T(8,128)(2,1)} %collective-permute-done.2, f32[512,256]{1,0:T(8,128)} %fusion.25, bf16[512,3072]{1,0:T(8,128)(2,1)S(1)} %copy-done.1, bf16[3072,256]{1,0:T(8,128)(2,1)} %collective-permute-done.1), kind=kOutput, calls=%fused_computation | convolution fusion | flops 1614544896 | bytes 16252928 | tf_op jit(solution)/shard_map/dot_general | solution.py:48
  188.4 41.5 %all_to_all.37 = bf16[4,128,3072]{2,1,0:T(8,128)(2,1)S(1)} all-to-all(bf16[4,128,3072]{2,1,0:T(8,128)(2,1)} %bitcast.37), channel_id=1, replica_groups=mesh['X'=4,'B'=4,'I'=4,'Y'=4,'C'=2] {'Y'}, dimensions={0} | all-to-all | bytes 6291456 | tf_op jit(solution)/shard_map/all_to_all | solution.py:27
  229.9 1.6 reduce_sum.104
  231.6 23.7 %all_to_all.38 = bf16[4,32,3072]{2,1,0:T(8,128)(2,1)S(1)} all-to-all(bf16[4,32,3072]{2,1,0:T(8,128)(2,1)} %bitcast.38), channel_id=1, replica_groups=mesh['X'=4,'B'=4,'I'=4,'Y'=4,'C'=2] {'I'}, dimensions={0} | all-to-all | bytes 1572864 | tf_op jit(solution)/shard_map/all_to_all | solution.py:27
  255.3 0.2 reduce_sum.105
  255.5 0.7 reshape.95
  256.2 11.2 %all-to-all-start.5 = ((bf16[16,2,3072]{2,1,0:T(2,128)(2,1)}), bf16[16,2,3072]{2,1,0:T(2,128)(2,1)S(1)}, u32[]{:S(2)}, u32[]{:S(2)}) async-start(bf16[16,2,3072]{2,1,0:T(2,128)(2,1)} %reshape.95), calls=%async_computation.5 | async-start | bytes 393216 | tf_op jit(solution)/shard_map/all_to_all | solution.py:27
  267.4 0.0 copy-done.2
  267.4 0.0 copy-done
  267.5 0.2 fusion.20
  267.7 0.2 select_reduce_fusion.1
  267.8 0.1 exponential_reduce_fusion
  268.0 15.3 %all-to-all-done.5 = bf16[16,2,3072]{2,1,0:T(2,128)(2,1)S(1)} async-done(((bf16[16,2,3072]{2,1,0:T(2,128)(2,1)}), bf16[16,2,3072]{2,1,0:T(2,128)(2,1)S(1)}, u32[]{:S(2)}, u32[]{:S(2)}) %all-to-all-start.5) | async-done | bytes 196640 | tf_op jit(solution)/shard_map/all_to_all | solution.py:27
  283.2 0.1 copy.21
  283.3 0.7 copy.22
  284.0 4.8 %all-to-all-start.6 = ((bf16[4,8,3072]{2,1,0:T(8,128)(2,1)}), bf16[4,8,3072]{2,1,0:T(8,128)(2,1)S(1)}, u32[]{:S(2)}, u32[]{:S(2)}) async-start(bf16[4,8,3072]{2,1,0:T(8,128)(2,1)} %copy.22), calls=%async_computation.6 | async-start | bytes 393216 | tf_op jit(solution)/shard_map/all_to_all | solution.py:27
  288.8 0.1 exponential_divide_fusion
  288.9 0.1 select_reduce_fusion
  289.0 4.1 %all-to-all-done.6 = bf16[4,8,3072]{2,1,0:T(8,128)(2,1)S(1)} async-done(((bf16[4,8,3072]{2,1,0:T(8,128)(2,1)}), bf16[4,8,3072]{2,1,0:T(8,128)(2,1)S(1)}, u32[]{:S(2)}, u32[]{:S(2)}) %all-to-all-start.6) | async-done | bytes 196640 | tf_op jit(solution)/shard_map/all_to_all | solution.py:27
  293.1 0.8 convolution_convert_fusion.1
  (6 shorter events, 0.1 us)
Async XLA Ops:
  7.2 260.3 %copy-start = (bf16[3072,16]{0,1:T(8,128)(2,1)S(1)}, bf16[3072,16]{0,1:T(8,128)(2,1)}, u32[]{:S(2)}) copy-start(bf16[3072,16]{0,1:T(8,128)(2,1)} %param.13) | copy-start | bytes 294916
  7.2 59.5 %copy-start.3 = (s32[4,4]{1,0:T(4,128)S(1)}, s32[4,4]{1,0:T(4,128)}, u32[]{:S(2)}) copy-start(s32[4,4]{1,0:T(4,128)} %param.17) | copy-start | bytes 196
  7.2 59.9 %copy-start.5 = (bf16[3072]{0:T(1024)(128)(2,1)S(1)}, bf16[3072]{0:T(1024)(128)(2,1)}, u32[]{:S(2)}) copy-start(bf16[3072]{0:T(1024)(128)(2,1)} %param.12) | copy-start | bytes 18436
  7.2 66.0 %copy-start.4 = (bf16[4,3072]{1,0:T(4,128)(2,1)S(1)}, bf16[4,3072]{1,0:T(4,128)(2,1)}, u32[]{:S(2)}) copy-start(bf16[4,3072]{1,0:T(4,128)(2,1)} %param.11) | copy-start | bytes 73732
  59.3 13.8 %all-to-all-start = ((bf16[32,4,768]{2,1,0:T(4,128)(2,1)}), bf16[32,4,768]{2,1,0:T(4,128)(2,1)S(1)}, u32[]{:S(2)}, u32[]{:S(2)}) async-start(bf16[32,4,768]{2,1,0:T(4,128)(2,1)} %reshape.87), calls=%async_computation | async-start | bytes 393216 | tf_op jit(solution)/shard_map/all_to_all | solution.py:27
  66.7 97.1 %all-gather.2.cloned.1.call-start = ((), (), s32[]{:S(2)}) async-start(), calls=%async_computation.7 | async-start | bytes 3932160 | tf_op jit(solution)/shard_map/all_gather | solution.py:91
  73.3 194.1 %copy-start.2 = (bf16[4,3072]{1,0:T(4,128)(2,1)}, bf16[4,3072]{1,0:T(4,128)(2,1)S(1)}, u32[]{:S(2)}) copy-start(bf16[4,3072]{1,0:T(4,128)(2,1)S(1)} %get-tuple-element.3) | copy-start | bytes 73732
  124.5 43.6 %collective-permute-start = (bf16[3072,256]{1,0:T(8,128)(2,1)}, bf16[3072,256]{1,0:T(8,128)(2,1)}, u32[]{:S(2)}, u32[]{:S(2)}) collective-permute-start(bf16[3072,256]{1,0:T(8,128)(2,1)} %param.14), channel_id=1, source_target_pairs={{0,1},{1,0},{2,3},{3,2},{4,5},{5,4},{6,7},{7,6},{8,9},{9,8},{10,11... | collective-permute-start | bytes 4718600 | tf_op jit(solution)/shard_map/ppermute | solution.py:67
  126.4 53.0 %collective-permute-start.1 = (bf16[3072,256]{1,0:T(8,128)(2,1)}, bf16[3072,256]{1,0:T(8,128)(2,1)}, u32[]{:S(2)}, u32[]{:S(2)}) collective-permute-start(bf16[3072,256]{1,0:T(8,128)(2,1)} %param.15), channel_id=1, source_target_pairs={{0,1},{1,0},{2,3},{3,2},{4,5},{5,4},{6,7},{7,6},{8,9},{9,8},{10,11... | collective-permute-start | bytes 4718600 | tf_op jit(solution)/shard_map/ppermute | solution.py:67
  128.8 50.6 %collective-permute-start.2 = (bf16[256,3072]{1,0:T(8,128)(2,1)}, bf16[256,3072]{1,0:T(8,128)(2,1)}, u32[]{:S(2)}, u32[]{:S(2)}) collective-permute-start(bf16[256,3072]{1,0:T(8,128)(2,1)} %param.16), channel_id=1, source_target_pairs={{0,1},{1,0},{2,3},{3,2},{4,5},{5,4},{6,7},{7,6},{8,9},{9,8},{10,11... | collective-permute-start | bytes 4718600 | tf_op jit(solution)/shard_map/ppermute | solution.py:67
  163.8 4.3 %copy-start.1 = (bf16[512,3072]{1,0:T(8,128)(2,1)S(1)}, bf16[512,3072]{1,0:T(8,128)(2,1)}, u32[]{:S(2)}) copy-start(bf16[512,3072]{1,0:T(8,128)(2,1)} %all-gather.2.cloned.1.call-done) | copy-start | bytes 9437188
  256.2 27.0 %all-to-all-start.5 = ((bf16[16,2,3072]{2,1,0:T(2,128)(2,1)}), bf16[16,2,3072]{2,1,0:T(2,128)(2,1)S(1)}, u32[]{:S(2)}, u32[]{:S(2)}) async-start(bf16[16,2,3072]{2,1,0:T(2,128)(2,1)} %reshape.95), calls=%async_computation.5 | async-start | bytes 393216 | tf_op jit(solution)/shard_map/all_to_all | solution.py:27
  284.0 9.0 %all-to-all-start.6 = ((bf16[4,8,3072]{2,1,0:T(8,128)(2,1)}), bf16[4,8,3072]{2,1,0:T(8,128)(2,1)S(1)}, u32[]{:S(2)}, u32[]{:S(2)}) async-start(bf16[4,8,3072]{2,1,0:T(8,128)(2,1)} %copy.22), calls=%async_computation.6 | async-start | bytes 393216 | tf_op jit(solution)/shard_map/all_to_all | solution.py:27
Sparse Core Ops, SparseCore 0:
  124.6 39.1 all-gather.1

commit v2 on v1

--- a/solution.py
+++ b/solution.py
@@ -2,6 +2,8 @@
 import jax.numpy as jnp
 import numpy as np
 from jax import lax
+from jax.experimental import pallas as pl
+from jax.experimental.pallas import tpu as pltpu
 from jax.sharding import Mesh, PartitionSpec as P
 
 CAP = 2
@@ -39,15 +41,49 @@
     return jnp.transpose(jnp.sum(pieces, axis=1), (1, 0, 2)).reshape(-1, 4 * width)
 
 
+def expert_kernel(rows_ref, g0, u0, d0, g1, u1, d1, out_ref, sums):
+    depth = rows_ref.shape[1]
+    step = 768
+
+    def inner(k, carry):
+        at = pl.ds(pl.multiple_of(k * step, step), step)
+        piece = rows_ref[:, at]
+        for i, weight in enumerate((g0, u0, g1, u1)):
+            sums[i] += jnp.dot(piece, weight[at, :], preferred_element_type=jnp.float32)
+        return carry
+
+    sums[...] = jnp.zeros_like(sums)
+    lax.fori_loop(0, depth // step, inner, 0)
+    first = (jax.nn.silu(sums[0]) * sums[1]).astype(jnp.bfloat16)
+    second = (jax.nn.silu(sums[2]) * sums[3]).astype(jnp.bfloat16)
+
+    def outer(k, carry):
+        at = pl.ds(pl.multiple_of(k * step, step), step)
+        total = jnp.dot(first, d0[:, at], preferred_element_type=jnp.float32)
+        total += jnp.dot(second, d1[:, at], preferred_element_type=jnp.float32)
+        out_ref[:, at] = total.astype(jnp.bfloat16)
+        return carry
+
+    lax.fori_loop(0, depth // step, outer, 0)
+
+
 def both_cores(rows, weights, partner):
-    total = None
-    for gate, up, down in (weights, partner):
-        gate_value = jnp.dot(rows, gate, preferred_element_type=jnp.float32)
-        up_value = jnp.dot(rows, up, preferred_element_type=jnp.float32)
-        hidden = (jax.nn.silu(gate_value) * up_value).astype(jnp.bfloat16)
-        part = jnp.dot(hidden, down, preferred_element_type=jnp.float32)
-        total = part if total is None else total + part
-    return total.astype(jnp.bfloat16)
+    count, width = rows.shape
+    units = weights[0].shape[1]
+    vmem = pl.BlockSpec(memory_space=pltpu.VMEM)
+    return pl.pallas_call(
+        expert_kernel,
+        out_shape=jax.ShapeDtypeStruct((count, width), jnp.bfloat16),
+        in_specs=[vmem] * 7,
+        out_specs=vmem,
+        scratch_shapes=[pltpu.VMEM((4, count, units), jnp.float32)],
+        compiler_params=pltpu.CompilerParams(vmem_limit_bytes=32 * 1024 * 1024),
+        cost_estimate=pl.CostEstimate(
+            flops=12 * count * width * units,
+            bytes_accessed=4 * count * width + 12 * width * units,
+            transcendentals=2 * count * units,
+        ),
+    )(rows, *weights, *partner)
 
 
 def on_device(
@@ -88,15 +124,25 @@
     by_z = jnp.transpose(at_x.reshape(4, 4, CAP, width), (1, 0, 2, 3)).reshape(16, CAP, width)
     at_z = swap(by_z, ("B", "I")).reshape(16 * CAP, width)
     block_rows = lax.all_gather(at_z, "I", axis=0, tiled=True)
-    rows = lax.all_gather(block_rows, "Y", axis=0, tiled=True)
 
-    partial_value = both_cores(rows, weights, partner)
+    def turn(value, by):
+        return lax.ppermute(value, "Y", [(i, (i + by) % 4) for i in range(4)])
+
+    half = block_rows.shape[0] // 2
+    below, above = turn(block_rows, 1), turn(block_rows, -1)
+    far = jnp.concatenate([turn(below[:half], 1), turn(above[half:], -1)], axis=0)
+    near = both_cores(jnp.concatenate([below, above], axis=0), weights, partner)
+    to_below, to_above = turn(near[: 2 * half], -1), turn(near[2 * half :], 1)
+    to_far = turn(both_cores(far, weights, partner), 2)
+    own = both_cores(block_rows, weights, partner)
+    over_y = own.astype(jnp.float32) + to_far.astype(jnp.float32)
+    over_y += to_below.astype(jnp.float32) + to_above.astype(jnp.float32)
+    over_y = over_y.astype(jnp.bfloat16)
 
     def summed(value, axes, parts):
         got = swap(value.reshape(parts, -1, width), axes)
         return jnp.sum(got.astype(jnp.float32), axis=0).astype(jnp.bfloat16)
 
-    over_y = summed(partial_value, "Y", 4)
     over_block = summed(over_y, "I", 4)
     back_z = swap(over_block.reshape(16, CAP, width), ("B", "I"))
     back_x = jnp.transpose(back_z.reshape(4, 4, CAP, width), (1, 0, 2, 3)).reshape(4, 4 * CAP, width)

time: 303 us -> 240 us (0.79)
  blocking collectives: 167 us -> 93.8 us
  starting transfers between devices: 29.7 us -> 54.5 us
  matrix products: 26.2 us -> 1.59 us
  Pallas kernels: 0 us -> 16.5 us
  between operations: 14.2 us -> 1.02 us
  waiting for transfers between devices: 58.3 us -> 62.3 us
    all_to_all x4 -> x2, blocking collectives: 97 us -> 25.2 us  [swap(): return lax.all_to_all(value, axes, split_axis=0, concat_axis=0, tiled=True)]
    all_gather x1 -> x0, waiting for transfers between devices: 33 us -> none  [on_device(): rows = lax.all_gather(block_rows, 'Y', axis=0, tiled=True)]
    ppermute x0 -> x7, waiting for transfers between devices: none -> 29.4 us  [turn(): return lax.ppermute(value, 'Y', [(i, (i + by) % 4) for i in range(4)])]
    dot_general x4 -> x0, matrix products: 24.6 us -> none  [the longest x2 17.1 us: both_cores(): part = jnp.dot(hidden, down, preferred_element_type=jnp.float32)]
    ppermute x0 -> x7, starting transfers between devices: none -> 21.8 us  [turn(): return lax.ppermute(value, 'Y', [(i, (i + by) % 4) for i in range(4)])]
    pallas_call x0 -> x3, Pallas kernels: none -> 16.5 us  [both_cores(): pl.pallas_call(expert_kernel, out_shape=jax.ShapeDtypeStruct((count, widt...]
    all_to_all x3 -> x4, waiting for transfers between devices: 25.2 us -> 32.8 us  [swap(): return lax.all_to_all(value, axes, split_axis=0, concat_axis=0, tiled=True)]
    all_to_all x3 -> x4, starting transfers between devices: 23.4 us -> 26.5 us  [swap(): return lax.all_to_all(value, axes, split_axis=0, concat_axis=0, tiled=True)]
  transfers between devices with their start and end apart: 7 -> 14, of which waited for: 4 -> 7; matrix products, arithmetic and copies ran while one was open for 6% -> 1% of each run, Pallas kernels for 0% -> 7%
where the time goes in v2:
time: 240 us; the launch traced here: 238 us
  blocking collectives  93.8 us (39%)
  waiting for transfers between devices  62.3 us (26%)
  starting transfers between devices  54.5 us (23%)
  Pallas kernels  16.5 us (7%)
  local copies, waits for them, and re-layouts  5.7 us (2%)
    all_gather x1, blocking collectives, attention_rows(): columns = lax.all_gather(out_weight.T, ('B', 'I'), axis=0, tiled=True)  36.1 us
    all_to_all x4, waiting for transfers between devices, swap(): return lax.all_to_all(value, axes, split_axis=0, concat_axis=0, tiled=True)  32.8 us
    ppermute x7, waiting for transfers between devices, turn(): return lax.ppermute(value, 'Y', [(i, (i + by) % 4) for i in range(4)])  29.4 us
    all_to_all x4, starting transfers between devices, swap(): return lax.all_to_all(value, axes, split_axis=0, concat_axis=0, tiled=True)  26.5 us
    all_to_all x2, blocking collectives, swap(): return lax.all_to_all(value, axes, split_axis=0, concat_axis=0, tiled=True)  25.2 us
    ppermute x7, starting transfers between devices, turn(): return lax.ppermute(value, 'Y', [(i, (i + by) % 4) for i in range(4)])  21.8 us
    all_gather x1, blocking collectives, on_device(): block_rows = lax.all_gather(at_z, 'I', axis=0, tiled=True)  17.6 us
    pallas_call x3, Pallas kernels, both_cores(): pl.pallas_call(expert_kernel, out_shape=jax.ShapeDtypeStruct((count, widt...  16.5 us
  transfers between devices with their start and end apart: 14, of which 7 were waited for; matrix products, arithmetic and copies ran while one was open for 1% of the time, Pallas kernels for 7%

profile of v2, /device:TPU:6, one launch (start us, length us, event | category | flops | bytes accessed | tf_op | source)
XLA Modules:
  0.0 237.5 jit_solution(8962460745197463869)
XLA Ops:
  0.6 0.0 copy-start
  0.7 15.0 %all_gather.9 = bf16[128,384]{1,0:T(8,128)(2,1)S(1)} all-gather(bf16[32,384]{1,0:T(8,128)(2,1)} %param.9), channel_id=1, replica_groups=mesh['X'=4,'B'=4,'I'=4,'Y'=4,'C'=2] {'X'}, dimensions={0}, use_global_device_ids=true | all-gather | bytes 122880 | tf_op jit(solution)/shard_map/all_gather | solution.py:33
  15.6 36.1 %all_gather.10 = bf16[768,384]{1,0:T(8,128)(2,1)S(1)} all-gather(bf16[48,384]{1,0:T(8,128)(2,1)} %bitcast.30), channel_id=1, replica_groups=mesh['X'=4,'B'=4,'I'=4,'Y'=4,'C'=2] {'B','I'}, dimensions={0}, use_global_device_ids=true | all-gather | bytes 626688 | tf_op jit(solution)/shard_map/all_gather | solution.py:34
  51.7 0.3 convolution_convert_fusion.2
  52.1 0.0 copy-start.1
  52.1 0.7 reshape.84
  52.8 7.3 %all-to-all-start = ((bf16[32,4,768]{2,1,0:T(4,128)(2,1)}), bf16[32,4,768]{2,1,0:T(4,128)(2,1)S(1)}, u32[]{:S(2)}, u32[]{:S(2)}) async-start(bf16[32,4,768]{2,1,0:T(4,128)(2,1)} %reshape.84), calls=%async_computation | async-start | bytes 393216 | tf_op jit(solution)/shard_map/all_to_all | solution.py:29
  60.1 0.1 convert_reduce_fusion.2
  60.3 0.2 select_reduce_fusion.2
  60.5 0.1 fusion.7
  60.6 5.9 %all-to-all-done = bf16[32,4,768]{2,1,0:T(4,128)(2,1)S(1)} async-done(((bf16[32,4,768]{2,1,0:T(4,128)(2,1)}), bf16[32,4,768]{2,1,0:T(4,128)(2,1)S(1)}, u32[]{:S(2)}, u32[]{:S(2)}) %all-to-all-start) | async-done | bytes 196640 | tf_op jit(solution)/shard_map/all_to_all | solution.py:29
  66.5 0.1 convert_reduce_fusion
  66.6 0.1 convert_reduce_fusion.1
  66.8 0.2 fusion.4
  67.0 0.3 fusion
  67.3 9.1 %all_to_all.30 = bf16[4,8,3072]{2,1,0:T(8,128)(2,1)S(1)} all-to-all(bf16[4,8,3072]{2,1,0:T(8,128)(2,1)S(1)} %fusion), channel_id=1, replica_groups=mesh['X'=4,'B'=4,'I'=4,'Y'=4,'C'=2] {'X'}, dimensions={0} | all-to-all | bytes 393216 | tf_op jit(solution)/shard_map/all_to_all | solution.py:29
  76.4 0.7 reshape.87
  77.1 1.7 copy.19
  78.9 6.7 %all-to-all-start.2 = ((bf16[16,2,3072]{2,1,0:T(2,128)(2,1)}), bf16[16,2,3072]{2,1,0:T(2,128)(2,1)S(1)}, u32[]{:S(2)}, u32[]{:S(2)}) async-start(bf16[16,2,3072]{2,1,0:T(2,128)(2,1)} %bitcast.26), calls=%async_computation.2 | async-start | bytes 393216 | tf_op jit(solution)/shard_map/all_to_all | solution.py:29
  85.6 1.9 collective-permute-start
  87.5 2.4 %collective-permute-start.1 = (bf16[3072,256]{1,0:T(8,128)(2,1)S(1)}, bf16[3072,256]{1,0:T(8,128)(2,1)}, u32[]{:S(2)}, u32[]{:S(2)}) collective-permute-start(bf16[3072,256]{1,0:T(8,128)(2,1)S(1)} %copy-done.2), channel_id=1, source_target_pairs={{0,1},{1,0},{2,3},{3,2},{4,5},{5,4},{6,7},{7,6},{8,9},{9,8},{10,11... | collective-permute-start | bytes 4718600 | tf_op jit(solution)/shard_map/ppermute | solution.py:103
  90.0 1.9 collective-permute-start.2
  91.9 9.8 %all-to-all-done.2 = bf16[16,2,3072]{2,1,0:T(2,128)(2,1)S(1)} async-done(((bf16[16,2,3072]{2,1,0:T(2,128)(2,1)}), bf16[16,2,3072]{2,1,0:T(2,128)(2,1)S(1)}, u32[]{:S(2)}, u32[]{:S(2)}) %all-to-all-start.2) | async-done | bytes 196640 | tf_op jit(solution)/shard_map/all_to_all | solution.py:29
  101.7 0.7 reshape.89
  102.4 17.6 %all_gather.11.rows_ref = bf16[128,3072]{1,0:T(8,128)(2,1)S(1)} all-gather(bf16[32,3072]{1,0:T(8,128)(2,1)} %reshape.89), channel_id=1, replica_groups=mesh['X'=4,'B'=4,'I'=4,'Y'=4,'C'=2] {'I'}, dimensions={0}, use_global_device_ids=true | all-gather | bytes 983040 | tf_op jit(solution)/shard_map/all_gather | solution.py:126
  120.0 3.1 %collective-permute-start.5 = (bf16[128,3072]{1,0:T(8,128)(2,1)S(1)}, bf16[128,3072]{1,0:T(8,128)(2,1)S(1)}, u32[]{:S(2)}, u32[]{:S(2)}) collective-permute-start(bf16[128,3072]{1,0:T(8,128)(2,1)S(1)} %all_gather.11.rows_ref), channel_id=1, source_target_pairs={{0,6},{2,0},{4,2},{6,4},{1,7},{3,1},{5,3},{7,5},{8,14},{10,8},{12,... | collective-permute-start | bytes 2359304 | tf_op jit(solution)/shard_map/ppermute | solution.py:129
  123.1 2.7 %collective-permute-start.3 = (bf16[128,3072]{1,0:T(8,128)(2,1)S(1)}, bf16[128,3072]{1,0:T(8,128)(2,1)S(1)}, u32[]{:S(2)}, u32[]{:S(2)}) collective-permute-start(bf16[128,3072]{1,0:T(8,128)(2,1)S(1)} %all_gather.11.rows_ref), channel_id=1, source_target_pairs={{0,2},{2,4},{4,6},{6,0},{1,3},{3,5},{5,7},{7,1},{8,10},{10,12},{12... | collective-permute-start | bytes 2359304 | tf_op jit(solution)/shard_map/ppermute | solution.py:129
  125.9 11.8 %collective-permute-done.5 = bf16[128,3072]{1,0:T(8,128)(2,1)S(1)} collective-permute-done((bf16[128,3072]{1,0:T(8,128)(2,1)S(1)}, bf16[128,3072]{1,0:T(8,128)(2,1)S(1)}, u32[]{:S(2)}, u32[]{:S(2)}) %collective-permute-start.5) | collective-permute-done | bytes 786464 | tf_op jit(solution)/shard_map/ppermute | solution.py:129
  137.7 3.5 %collective-permute-start.6 = (bf16[64,3072]{1,0:T(8,128)(2,1)S(1)}, bf16[64,3072]{1,0:T(8,128)(2,1)S(1)}, u32[]{:S(2)}, u32[]{:S(2)}) collective-permute-start(bf16[64,3072]{1,0:T(8,128)(2,1)S(1)} %slice.17), channel_id=1, source_target_pairs={{0,6},{2,0},{4,2},{6,4},{1,7},{3,1},{5,3},{7,5},{8,14},{10,8},{12,... | collective-permute-start | bytes 1179656 | tf_op jit(solution)/shard_map/ppermute | solution.py:129
  141.2 0.0 collective-permute-done.3
  141.3 0.0 copy-start.3
  141.3 2.5 %collective-permute-start.4 = (bf16[64,3072]{1,0:T(8,128)(2,1)S(1)}, bf16[64,3072]{1,0:T(8,128)(2,1)S(1)}, u32[]{:S(2)}, u32[]{:S(2)}) collective-permute-start(bf16[64,3072]{1,0:T(8,128)(2,1)S(1)} %slice.16), channel_id=1, source_target_pairs={{0,2},{2,4},{4,6},{6,0},{1,3},{3,5},{5,7},{7,1},{8,10},{10,12},{12... | collective-permute-start | bytes 1179656 | tf_op jit(solution)/shard_map/ppermute | solution.py:129
  143.8 0.1 pad_maximum_fusion.rows_ref
  143.9 0.0 collective-permute-done.g1
  143.9 0.0 collective-permute-done.2.d1
  143.9 6.3 %shard_map.106 = bf16[256,3072]{1,0:T(8,128)(2,1)S(1)} custom-call(bf16[256,3072]{1,0:T(8,128)(2,1)S(1)} %pad_maximum_fusion.rows_ref, bf16[3072,256]{1,0:T(8,128)(2,1)S(1)} %copy-done.1, bf16[3072,256]{1,0:T(8,128)(2,1)S(1)} %copy-done.2, bf16[256,3072]{1,0:T(8,128)(2,1)S(1)} %copy-done.3, bf16[3072,256]{1,0:T(8,128)(2,1)} %collective-permute-done.g1, ...), custom_call_target="tpu_custom_call" | custom-call | flops 2415919104 | bytes 12582912 | tf_op jit(solution)/shard_map/pallas_call | solution.py:74
  150.3 0.1 fusion.11
  150.4 4.7 %collective-permute-start.8 = (bf16[128,3072]{1,0:T(8,128)(2,1)S(1)}, bf16[128,3072]{1,0:T(8,128)(2,1)S(1)}, u32[]{:S(2)}, u32[]{:S(2)}) collective-permute-start(bf16[128,3072]{1,0:T(8,128)(2,1)S(1)} %get-tuple-element.4), channel_id=1, source_target_pairs={{0,6},{2,0},{4,2},{6,4},{1,7},{3,1},{5,3},{7,5},{8,14},{10,8},{12,... | collective-permute-start | bytes 2359304 | tf_op jit(solution)/shard_map/ppermute | solution.py:129
  155.1 1.9 collective-permute-start.9
  157.0 0.0 collective-permute-done.6
  157.0 0.0 collective-permute-done.4
  157.0 0.1 pad_maximum_fusion.1.rows_ref
  157.1 5.1 %shard_map.105 = bf16[128,3072]{1,0:T(8,128)(2,1)S(1)} custom-call(bf16[128,3072]{1,0:T(8,128)(2,1)S(1)} %pad_maximum_fusion.1.rows_ref, bf16[3072,256]{1,0:T(8,128)(2,1)S(1)} %copy-done.1, bf16[3072,256]{1,0:T(8,128)(2,1)S(1)} %copy-done.2, bf16[256,3072]{1,0:T(8,128)(2,1)S(1)} %copy-done.3, bf16[3072,256]{1,0:T(8,128)(2,1)} %collective-permute-done.g1, ...), custom_call_target="tpu_custom_call" | custom-call | flops 1207959552 | bytes 11010048 | tf_op jit(solution)/shard_map/pallas_call | solution.py:74
  162.2 3.4 %collective-permute-start.7 = (bf16[128,3072]{1,0:T(8,128)(2,1)S(1)}, bf16[128,3072]{1,0:T(8,128)(2,1)S(1)}, u32[]{:S(2)}, u32[]{:S(2)}) collective-permute-start(bf16[128,3072]{1,0:T(8,128)(2,1)S(1)} %shard_map.105), channel_id=1, source_target_pairs={{0,4},{2,6},{4,0},{6,2},{1,5},{3,7},{5,1},{7,3},{8,12},{10,14},{12... | collective-permute-start | bytes 2359304 | tf_op jit(solution)/shard_map/ppermute | solution.py:129
  165.5 5.1 %shard_map.104 = bf16[128,3072]{1,0:T(8,128)(2,1)S(1)} custom-call(bf16[128,3072]{1,0:T(8,128)(2,1)S(1)} %all_gather.11.rows_ref, bf16[3072,256]{1,0:T(8,128)(2,1)S(1)} %copy-done.1, bf16[3072,256]{1,0:T(8,128)(2,1)S(1)} %copy-done.2, bf16[256,3072]{1,0:T(8,128)(2,1)S(1)} %copy-done.3, bf16[3072,256]{1,0:T(8,128)(2,1)} %collective-permute-done.g1, ...), custom_call_target="tpu_custom_call" | custom-call | flops 1207959552 | bytes 11010048 | tf_op jit(solution)/shard_map/pallas_call | solution.py:74
  170.6 12.3 %collective-permute-done.8 = bf16[128,3072]{1,0:T(8,128)(2,1)S(1)} collective-permute-done((bf16[128,3072]{1,0:T(8,128)(2,1)S(1)}, bf16[128,3072]{1,0:T(8,128)(2,1)S(1)}, u32[]{:S(2)}, u32[]{:S(2)}) %collective-permute-start.8) | collective-permute-done | bytes 786464 | tf_op jit(solution)/shard_map/ppermute | solution.py:129
  182.9 5.3 %collective-permute-done.9 = bf16[128,3072]{1,0:T(8,128)(2,1)S(1)} collective-permute-done((bf16[128,3072]{1,0:T(8,128)(2,1)S(1)}, bf16[128,3072]{1,0:T(8,128)(2,1)S(1)}, u32[]{:S(2)}, u32[]{:S(2)}) %collective-permute-start.9) | collective-permute-done | bytes 786464 | tf_op jit(solution)/shard_map/ppermute | solution.py:129
  188.2 0.0 collective-permute-done.7
  188.2 0.5 add_convert_fusion
  188.7 16.1 %all_to_all.31 = bf16[4,32,3072]{2,1,0:T(8,128)(2,1)S(1)} all-to-all(bf16[4,32,3072]{2,1,0:T(8,128)(2,1)S(1)} %bitcast.25), channel_id=1, replica_groups=mesh['X'=4,'B'=4,'I'=4,'Y'=4,'C'=2] {'I'}, dimensions={0} | all-to-all | bytes 1572864 | tf_op jit(solution)/shard_map/all_to_all | solution.py:29
  204.8 0.2 reduce_sum.92
  205.0 0.7 reshape.91
  205.7 7.0 %all-to-all-start.4 = ((bf16[16,2,3072]{2,1,0:T(2,128)(2,1)}), bf16[16,2,3072]{2,1,0:T(2,128)(2,1)S(1)}, u32[]{:S(2)}, u32[]{:S(2)}) async-start(bf16[16,2,3072]{2,1,0:T(2,128)(2,1)} %reshape.91), calls=%async_computation.4 | async-start | bytes 393216 | tf_op jit(solution)/shard_map/all_to_all | solution.py:29
  212.7 0.2 fusion.9
  212.9 0.2 select_reduce_fusion.1
  213.1 0.1 exponential_reduce_fusion
  213.2 13.0 %all-to-all-done.4 = bf16[16,2,3072]{2,1,0:T(2,128)(2,1)S(1)} async-done(((bf16[16,2,3072]{2,1,0:T(2,128)(2,1)}), bf16[16,2,3072]{2,1,0:T(2,128)(2,1)S(1)}, u32[]{:S(2)}, u32[]{:S(2)}) %all-to-all-start.4) | async-done | bytes 196640 | tf_op jit(solution)/shard_map/all_to_all | solution.py:29
  226.2 0.1 copy.20
  226.3 0.7 copy.21
  227.0 5.4 %all-to-all-start.5 = ((bf16[4,8,3072]{2,1,0:T(8,128)(2,1)}), bf16[4,8,3072]{2,1,0:T(8,128)(2,1)S(1)}, u32[]{:S(2)}, u32[]{:S(2)}) async-start(bf16[4,8,3072]{2,1,0:T(8,128)(2,1)} %copy.21), calls=%async_computation.5 | async-start | bytes 393216 | tf_op jit(solution)/shard_map/all_to_all | solution.py:29
  232.5 0.1 exponential_divide_fusion
  232.5 0.1 select_reduce_fusion
  232.6 4.1 %all-to-all-done.5 = bf16[4,8,3072]{2,1,0:T(8,128)(2,1)S(1)} async-done(((bf16[4,8,3072]{2,1,0:T(8,128)(2,1)}), bf16[4,8,3072]{2,1,0:T(8,128)(2,1)S(1)}, u32[]{:S(2)}, u32[]{:S(2)}) %all-to-all-start.5) | async-done | bytes 196640 | tf_op jit(solution)/shard_map/all_to_all | solution.py:29
  236.7 0.8 convolution_convert_fusion.1
  (22 shorter events, 0.2 us)
Async XLA Ops:
  0.6 212.1 %copy-start = (bf16[3072,16]{0,1:T(8,128)(2,1)S(1)}, bf16[3072,16]{0,1:T(8,128)(2,1)}, u32[]{:S(2)}) copy-start(bf16[3072,16]{0,1:T(8,128)(2,1)} %param.13) | copy-start | bytes 294916
  0.6 59.5 %copy-start.5 = (s32[4,4]{1,0:T(4,128)S(1)}, s32[4,4]{1,0:T(4,128)}, u32[]{:S(2)}) copy-start(s32[4,4]{1,0:T(4,128)} %param.17) | copy-start | bytes 196
  0.7 59.9 %copy-start.7 = (bf16[3072]{0:T(1024)(128)(2,1)S(1)}, bf16[3072]{0:T(1024)(128)(2,1)}, u32[]{:S(2)}) copy-start(bf16[3072]{0:T(1024)(128)(2,1)} %param.12) | copy-start | bytes 18436
  0.7 66.0 %copy-start.6 = (bf16[4,3072]{1,0:T(4,128)(2,1)S(1)}, bf16[4,3072]{1,0:T(4,128)(2,1)}, u32[]{:S(2)}) copy-start(bf16[4,3072]{1,0:T(4,128)(2,1)} %param.11) | copy-start | bytes 73732
  51.7 35.8 %copy-start.2 = (bf16[3072,256]{1,0:T(8,128)(2,1)S(1)}, bf16[3072,256]{1,0:T(8,128)(2,1)}, u32[]{:S(2)}) copy-start(bf16[3072,256]{1,0:T(8,128)(2,1)} %u0.5) | copy-start | bytes 4718596
  52.1 33.5 %copy-start.1 = (bf16[3072,256]{1,0:T(8,128)(2,1)S(1)}, bf16[3072,256]{1,0:T(8,128)(2,1)}, u32[]{:S(2)}) copy-start(bf16[3072,256]{1,0:T(8,128)(2,1)} %g0.5) | copy-start | bytes 4718596
  52.8 13.8 %all-to-all-start = ((bf16[32,4,768]{2,1,0:T(4,128)(2,1)}), bf16[32,4,768]{2,1,0:T(4,128)(2,1)S(1)}, u32[]{:S(2)}, u32[]{:S(2)}) async-start(bf16[32,4,768]{2,1,0:T(4,128)(2,1)} %reshape.84), calls=%async_computation | async-start | bytes 393216 | tf_op jit(solution)/shard_map/all_to_all | solution.py:29
  66.8 145.9 %copy-start.4 = (bf16[4,3072]{1,0:T(4,128)(2,1)}, bf16[4,3072]{1,0:T(4,128)(2,1)S(1)}, u32[]{:S(2)}) copy-start(bf16[4,3072]{1,0:T(4,128)(2,1)S(1)} %get-tuple-element.3) | copy-start | bytes 73732
  78.9 22.8 %all-to-all-start.2 = ((bf16[16,2,3072]{2,1,0:T(2,128)(2,1)}), bf16[16,2,3072]{2,1,0:T(2,128)(2,1)S(1)}, u32[]{:S(2)}, u32[]{:S(2)}) async-start(bf16[16,2,3072]{2,1,0:T(2,128)(2,1)} %bitcast.26), calls=%async_computation.2 | async-start | bytes 393216 | tf_op jit(solution)/shard_map/all_to_all | solution.py:29
  85.6 58.3 %collective-permute-start = (bf16[3072,256]{1,0:T(8,128)(2,1)S(1)}, bf16[3072,256]{1,0:T(8,128)(2,1)}, u32[]{:S(2)}, u32[]{:S(2)}) collective-permute-start(bf16[3072,256]{1,0:T(8,128)(2,1)S(1)} %copy-done.1), channel_id=1, source_target_pairs={{0,1},{1,0},{2,3},{3,2},{4,5},{5,4},{6,7},{7,6},{8,9},{9,8},{10,11... | collective-permute-start | bytes 4718600 | tf_op jit(solution)/shard_map/ppermute | solution.py:103
  87.5 56.4 %collective-permute-start.1 = (bf16[3072,256]{1,0:T(8,128)(2,1)S(1)}, bf16[3072,256]{1,0:T(8,128)(2,1)}, u32[]{:S(2)}, u32[]{:S(2)}) collective-permute-start(bf16[3072,256]{1,0:T(8,128)(2,1)S(1)} %copy-done.2), channel_id=1, source_target_pairs={{0,1},{1,0},{2,3},{3,2},{4,5},{5,4},{6,7},{7,6},{8,9},{9,8},{10,11... | collective-permute-start | bytes 4718600 | tf_op jit(solution)/shard_map/ppermute | solution.py:103
  90.0 53.9 %collective-permute-start.2 = (bf16[256,3072]{1,0:T(8,128)(2,1)}, bf16[256,3072]{1,0:T(8,128)(2,1)}, u32[]{:S(2)}, u32[]{:S(2)}) collective-permute-start(bf16[256,3072]{1,0:T(8,128)(2,1)} %d0.5), channel_id=1, source_target_pairs={{0,1},{1,0},{2,3},{3,2},{4,5},{5,4},{6,7},{7,6},{8,9},{9,8},{10,11... | collective-permute-start | bytes 4718600 | tf_op jit(solution)/shard_map/ppermute | solution.py:103
  120.0 17.7 %collective-permute-start.5 = (bf16[128,3072]{1,0:T(8,128)(2,1)S(1)}, bf16[128,3072]{1,0:T(8,128)(2,1)S(1)}, u32[]{:S(2)}, u32[]{:S(2)}) collective-permute-start(bf16[128,3072]{1,0:T(8,128)(2,1)S(1)} %all_gather.11.rows_ref), channel_id=1, source_target_pairs={{0,6},{2,0},{4,2},{6,4},{1,7},{3,1},{5,3},{7,5},{8,14},{10,8},{12,... | collective-permute-start | bytes 2359304 | tf_op jit(solution)/shard_map/ppermute | solution.py:129
  123.1 18.1 %collective-permute-start.3 = (bf16[128,3072]{1,0:T(8,128)(2,1)S(1)}, bf16[128,3072]{1,0:T(8,128)(2,1)S(1)}, u32[]{:S(2)}, u32[]{:S(2)}) collective-permute-start(bf16[128,3072]{1,0:T(8,128)(2,1)S(1)} %all_gather.11.rows_ref), channel_id=1, source_target_pairs={{0,2},{2,4},{4,6},{6,0},{1,3},{3,5},{5,7},{7,1},{8,10},{10,12},{12... | collective-permute-start | bytes 2359304 | tf_op jit(solution)/shard_map/ppermute | solution.py:129
  137.7 19.3 %collective-permute-start.6 = (bf16[64,3072]{1,0:T(8,128)(2,1)S(1)}, bf16[64,3072]{1,0:T(8,128)(2,1)S(1)}, u32[]{:S(2)}, u32[]{:S(2)}) collective-permute-start(bf16[64,3072]{1,0:T(8,128)(2,1)S(1)} %slice.17), channel_id=1, source_target_pairs={{0,6},{2,0},{4,2},{6,4},{1,7},{3,1},{5,3},{7,5},{8,14},{10,8},{12,... | collective-permute-start | bytes 1179656 | tf_op jit(solution)/shard_map/ppermute | solution.py:129
  141.3 2.7 %copy-start.3 = (bf16[256,3072]{1,0:T(8,128)(2,1)S(1)}, bf16[256,3072]{1,0:T(8,128)(2,1)}, u32[]{:S(2)}) copy-start(bf16[256,3072]{1,0:T(8,128)(2,1)} %d0.5) | copy-start | bytes 4718596
  141.3 15.8 %collective-permute-start.4 = (bf16[64,3072]{1,0:T(8,128)(2,1)S(1)}, bf16[64,3072]{1,0:T(8,128)(2,1)S(1)}, u32[]{:S(2)}, u32[]{:S(2)}) collective-permute-start(bf16[64,3072]{1,0:T(8,128)(2,1)S(1)} %slice.16), channel_id=1, source_target_pairs={{0,2},{2,4},{4,6},{6,0},{1,3},{3,5},{5,7},{7,1},{8,10},{10,12},{12... | collective-permute-start | bytes 1179656 | tf_op jit(solution)/shard_map/ppermute | solution.py:129
  150.4 32.5 %collective-permute-start.8 = (bf16[128,3072]{1,0:T(8,128)(2,1)S(1)}, bf16[128,3072]{1,0:T(8,128)(2,1)S(1)}, u32[]{:S(2)}, u32[]{:S(2)}) collective-permute-start(bf16[128,3072]{1,0:T(8,128)(2,1)S(1)} %get-tuple-element.4), channel_id=1, source_target_pairs={{0,6},{2,0},{4,2},{6,4},{1,7},{3,1},{5,3},{7,5},{8,14},{10,8},{12,... | collective-permute-start | bytes 2359304 | tf_op jit(solution)/shard_map/ppermute | solution.py:129
  155.1 33.1 %collective-permute-start.9 = (bf16[128,3072]{1,0:T(8,128)(2,1)S(1)}, bf16[128,3072]{1,0:T(8,128)(2,1)S(1)}, u32[]{:S(2)}, u32[]{:S(2)}) collective-permute-start(bf16[128,3072]{1,0:T(8,128)(2,1)S(1)} %get-tuple-element.5), channel_id=1, source_target_pairs={{0,2},{2,4},{4,6},{6,0},{1,3},{3,5},{5,7},{7,1},{8,10},{10,12},{12... | collective-permute-start | bytes 2359304 | tf_op jit(solution)/shard_map/ppermute | solution.py:129
  162.2 26.1 %collective-permute-start.7 = (bf16[128,3072]{1,0:T(8,128)(2,1)S(1)}, bf16[128,3072]{1,0:T(8,128)(2,1)S(1)}, u32[]{:S(2)}, u32[]{:S(2)}) collective-permute-start(bf16[128,3072]{1,0:T(8,128)(2,1)S(1)} %shard_map.105), channel_id=1, source_target_pairs={{0,4},{2,6},{4,0},{6,2},{1,5},{3,7},{5,1},{7,3},{8,12},{10,14},{12... | collective-permute-start | bytes 2359304 | tf_op jit(solution)/shard_map/ppermute | solution.py:129
  205.7 20.5 %all-to-all-start.4 = ((bf16[16,2,3072]{2,1,0:T(2,128)(2,1)}), bf16[16,2,3072]{2,1,0:T(2,128)(2,1)S(1)}, u32[]{:S(2)}, u32[]{:S(2)}) async-start(bf16[16,2,3072]{2,1,0:T(2,128)(2,1)} %reshape.91), calls=%async_computation.4 | async-start | bytes 393216 | tf_op jit(solution)/shard_map/all_to_all | solution.py:29
  227.0 9.7 %all-to-all-start.5 = ((bf16[4,8,3072]{2,1,0:T(8,128)(2,1)}), bf16[4,8,3072]{2,1,0:T(8,128)(2,1)S(1)}, u32[]{:S(2)}, u32[]{:S(2)}) async-start(bf16[4,8,3072]{2,1,0:T(8,128)(2,1)} %copy.21), calls=%async_computation.5 | async-start | bytes 393216 | tf_op jit(solution)/shard_map/all_to_all | solution.py:29

commit v3 on v2

--- a/solution.py
+++ b/solution.py
@@ -1,3 +1,5 @@
+import functools
+
 import jax
 import jax.numpy as jnp
 import numpy as np
@@ -29,53 +31,68 @@
     return lax.all_to_all(value, axes, split_axis=0, concat_axis=0, tiled=True)
 
 
+def spread(value, axes, parts):
+    return swap(jnp.broadcast_to(value[None], (parts,) + value.shape), axes)
+
+
 def attention_rows(context, out_weight):
-    tokens = lax.all_gather(context, "X", axis=0, tiled=True)
-    columns = lax.all_gather(out_weight.T, ("B", "I"), axis=0, tiled=True)
+    tokens = spread(context, ("X", "I"), 16).reshape(-1, context.shape[1])
+    columns = spread(out_weight.T, "B", 4).reshape(-1, out_weight.shape[0])
     partial_sum = lax.dot_general(
         tokens, columns, (((1,), (1,)), ((), ())), preferred_element_type=jnp.float32
     ).astype(jnp.bfloat16)
     width = columns.shape[0]
-    pieces = swap(partial_sum.reshape(32, -1, width), ("X", "Y", "C"))
-    pieces = pieces.reshape(4, 8, -1, width).astype(jnp.float32)
-    return jnp.transpose(jnp.sum(pieces, axis=1), (1, 0, 2)).reshape(-1, 4 * width)
+    pieces = swap(partial_sum.reshape(128, -1, width), ("X", "I", "Y", "C"))
+    count = pieces.shape[1]
+    pieces = pieces.reshape(16, 8, count, width).astype(jnp.float32)
+    summed = jnp.sum(pieces, axis=1).reshape(4, 4, count, 4, width // 4)
+    return jnp.transpose(summed, (2, 0, 3, 1, 4)).reshape(count, 16 * width)
 
 
-def expert_kernel(rows_ref, g0, u0, d0, g1, u1, d1, out_ref, sums):
-    depth = rows_ref.shape[1]
-    step = 768
-
-    def inner(k, carry):
-        at = pl.ds(pl.multiple_of(k * step, step), step)
-        piece = rows_ref[:, at]
+def expert_kernel(layout, *refs):
+    pieces = sum(len(group) for group in layout)
+    inputs, refs = refs[:pieces], refs[pieces:]
+    g0, u0, d0, g1, u1, d1 = refs[:6]
+    results, sums = refs[6 : 6 + len(layout)], refs[-1]
+    step = results[0].shape[2]
+    rows = results[0].shape[1]
+    sums[...] = jnp.zeros_like(sums)
+    for part in range(results[0].shape[0]):
+        at = slice(part * step, (part + 1) * step)
+        held = []
+        first = 0
+        for group in layout:
+            left = part
+            for number, parts in enumerate(group):
+                if 0 <= left < parts:
+                    held.append(inputs[first + number][left])
+                left -= parts
+            first += len(group)
+        piece = jnp.concatenate(held, axis=0) if len(held) > 1 else held[0]
         for i, weight in enumerate((g0, u0, g1, u1)):
             sums[i] += jnp.dot(piece, weight[at, :], preferred_element_type=jnp.float32)
-        return carry
-
-    sums[...] = jnp.zeros_like(sums)
-    lax.fori_loop(0, depth // step, inner, 0)
     first = (jax.nn.silu(sums[0]) * sums[1]).astype(jnp.bfloat16)
     second = (jax.nn.silu(sums[2]) * sums[3]).astype(jnp.bfloat16)
-
-    def outer(k, carry):
-        at = pl.ds(pl.multiple_of(k * step, step), step)
+    for part in range(results[0].shape[0]):
+        at = slice(part * step, (part + 1) * step)
         total = jnp.dot(first, d0[:, at], preferred_element_type=jnp.float32)
         total += jnp.dot(second, d1[:, at], preferred_element_type=jnp.float32)
-        out_ref[:, at] = total.astype(jnp.bfloat16)
-        return carry
-
-    lax.fori_loop(0, depth // step, outer, 0)
+        total = total.astype(jnp.bfloat16)
+        for number, result in enumerate(results):
+            result[part] = total[number * rows : (number + 1) * rows]
 
 
-def both_cores(rows, weights, partner):
-    count, width = rows.shape
-    units = weights[0].shape[1]
+def both_cores(groups, weights, partner):
+    layout = tuple(tuple(p.shape[0] for p in group) for group in groups)
+    parts, (rows, step) = sum(layout[0]), groups[0][0].shape[1:]
+    count, width, units = rows * len(groups), parts * step, weights[0].shape[1]
     vmem = pl.BlockSpec(memory_space=pltpu.VMEM)
+    flat = [p for group in groups for p in group]
     return pl.pallas_call(
-        expert_kernel,
-        out_shape=jax.ShapeDtypeStruct((count, width), jnp.bfloat16),
-        in_specs=[vmem] * 7,
-        out_specs=vmem,
+        functools.partial(expert_kernel, layout),
+        out_shape=[jax.ShapeDtypeStruct((parts, rows, step), jnp.bfloat16)] * len(groups),
+        in_specs=[vmem] * (len(flat) + 6),
+        out_specs=[vmem] * len(groups),
         scratch_shapes=[pltpu.VMEM((4, count, units), jnp.float32)],
         compiler_params=pltpu.CompilerParams(vmem_limit_bytes=32 * 1024 * 1024),
         cost_estimate=pl.CostEstimate(
@@ -83,7 +100,7 @@
             bytes_accessed=4 * count * width + 12 * width * units,
             transcendentals=2 * count * units,
         ),
-    )(rows, *weights, *partner)
+    )(*flat, *weights, *partner)
 
 
 def on_device(
@@ -120,33 +137,28 @@
         assign.astype(jnp.bfloat16).T, normed, preferred_element_type=jnp.float32
     ).astype(jnp.bfloat16)
 
-    at_x = swap(send_rows.reshape(4, 4 * CAP, width), "X")
-    by_z = jnp.transpose(at_x.reshape(4, 4, CAP, width), (1, 0, 2, 3)).reshape(16, CAP, width)
-    at_z = swap(by_z, ("B", "I")).reshape(16 * CAP, width)
-    block_rows = lax.all_gather(at_z, "I", axis=0, tiled=True)
+    quarter = width // 4
+    outgoing = jnp.transpose(send_rows.reshape(experts, CAP, 4, quarter), (0, 2, 1, 3))
+    landed = swap(outgoing.reshape(4 * experts, CAP, quarter), EXPERT)
+    block_rows = spread(landed.reshape(-1, quarter), "I", 4)
 
     def turn(value, by):
         return lax.ppermute(value, "Y", [(i, (i + by) % 4) for i in range(4)])
 
-    half = block_rows.shape[0] // 2
     below, above = turn(block_rows, 1), turn(block_rows, -1)
-    far = jnp.concatenate([turn(below[:half], 1), turn(above[half:], -1)], axis=0)
-    near = both_cores(jnp.concatenate([below, above], axis=0), weights, partner)
-    to_below, to_above = turn(near[: 2 * half], -1), turn(near[2 * half :], 1)
-    to_far = turn(both_cores(far, weights, partner), 2)
-    own = both_cores(block_rows, weights, partner)
+    far = [turn(below[:2], 1), turn(above[2:], -1)]
+    near_below, near_above = both_cores([[below], [above]], weights, partner)
+    to_below, to_above = turn(near_below, -1), turn(near_above, 1)
+    to_far = turn(both_cores([far], weights, partner)[0], 2)
+    own = both_cores([[block_rows]], weights, partner)[0]
     over_y = own.astype(jnp.float32) + to_far.astype(jnp.float32)
     over_y += to_below.astype(jnp.float32) + to_above.astype(jnp.float32)
     over_y = over_y.astype(jnp.bfloat16)
 
-    def summed(value, axes, parts):
-        got = swap(value.reshape(parts, -1, width), axes)
-        return jnp.sum(got.astype(jnp.float32), axis=0).astype(jnp.bfloat16)
-
-    over_block = summed(over_y, "I", 4)
-    back_z = swap(over_block.reshape(16, CAP, width), ("B", "I"))
-    back_x = jnp.transpose(back_z.reshape(4, 4, CAP, width), (1, 0, 2, 3)).reshape(4, 4 * CAP, width)
-    chosen = swap(back_x, "X").reshape(experts * CAP, width)
+    over_block = jnp.sum(swap(over_y, "I").astype(jnp.float32), axis=0).astype(jnp.bfloat16)
+    back = swap(over_block.reshape(4 * experts, CAP, quarter), EXPERT)
+    chosen = jnp.transpose(back.reshape(experts, 4, CAP, quarter), (0, 2, 1, 3))
+    chosen = chosen.reshape(experts * CAP, width)
     cell_weight = jnp.sum(jnp.where(cells, route_weight[:, :, None], 0.0), axis=1)
     expert_mix = jnp.dot(
         cell_weight, chosen.astype(jnp.float32), precision=lax.Precision.HIGHEST

time: 240 us -> 246 us (1.025)
  waiting for transfers between devices: 62.3 us -> 76.5 us
  Pallas kernels: 16.5 us -> 13 us
  blocking collectives: 93.8 us -> 90.9 us
  starting transfers between devices: 54.5 us -> 51.7 us
    all_gather x3 -> x0, blocking collectives: 68.6 us -> none  [the longest x1 36.1 us: attention_rows(): columns = lax.all_gather(out_weight.T, ('B', 'I'), axis=0, tiled=True)]
    all_to_all x2 -> x4, blocking collectives: 25.2 us -> 90.9 us  [swap(): return lax.all_to_all(value, axes, split_axis=0, concat_axis=0, tiled=True)]
    ppermute x7, waiting for transfers between devices: 29.4 us -> 38 us  [turn(): return lax.ppermute(value, 'Y', [(i, (i + by) % 4) for i in range(4)])]
    all_to_all x4 -> x3, waiting for transfers between devices: 32.8 us -> 38.5 us  [swap(): return lax.all_to_all(value, axes, split_axis=0, concat_axis=0, tiled=True)]
    all_to_all x4 -> x3, starting transfers between devices: 26.5 us -> 21.9 us  [swap(): return lax.all_to_all(value, axes, split_axis=0, concat_axis=0, tiled=True)]
    broadcast_in_dim x0 -> x4, local copies, waits for them, and re-layouts: none -> 4.2 us  [spread(): return swap(jnp.broadcast_to(value[None], (parts,) + value.shape), axes)]
    pallas_call x3, Pallas kernels: 16.5 us -> 13 us  [both_cores(): pl.pallas_call(functools.partial(expert_kernel, layout), out_shape=[jax.S...]
    reshape x6, local copies, waits for them, and re-layouts: 5.43 us -> 2.09 us  [the longest x1 0.78 us: attention_rows(): pieces = swap(partial_sum.reshape(128, -1, width), ('X', 'I', 'Y', 'C'))]
  transfers between devices with their start and end apart: 14 -> 13, of which waited for: 7 -> 6; matrix products, arithmetic and copies ran while one was open for 1% -> 0% of each run, Pallas kernels for 7% -> 5%
where the time goes in v3:
time: 246 us; the launch traced here: 245 us
  blocking collectives  90.9 us (37%)
  waiting for transfers between devices  76.5 us (31%)
  starting transfers between devices  51.7 us (21%)
  Pallas kernels  13 us (5%)
  local copies, waits for them, and re-layouts  8.07 us (3%)
    all_to_all x4, blocking collectives, swap(): return lax.all_to_all(value, axes, split_axis=0, concat_axis=0, tiled=True)  90.9 us
    all_to_all x3, waiting for transfers between devices, swap(): return lax.all_to_all(value, axes, split_axis=0, concat_axis=0, tiled=True)  38.5 us
    ppermute x7, waiting for transfers between devices, turn(): return lax.ppermute(value, 'Y', [(i, (i + by) % 4) for i in range(4)])  38 us
    ppermute x7, starting transfers between devices, turn(): return lax.ppermute(value, 'Y', [(i, (i + by) % 4) for i in range(4)])  23.5 us
    all_to_all x3, starting transfers between devices, swap(): return lax.all_to_all(value, axes, split_axis=0, concat_axis=0, tiled=True)  21.9 us
    pallas_call x3, Pallas kernels, both_cores(): pl.pallas_call(functools.partial(expert_kernel, layout), out_shape=[jax.S...  13 us
    ppermute x3, starting transfers between devices, on_device(): partner = tuple((lax.ppermute(w, 'C', [(0, 1), (1, 0)]) for w in weights))  6.25 us
  transfers between devices with their start and end apart: 13, of which 6 were waited for; matrix products, arithmetic and copies ran while one was open for 0% of the time, Pallas kernels for 5%

profile of v3, /device:TPU:6, one launch (start us, length us, event | category | flops | bytes accessed | tf_op | source)
XLA Modules:
  0.0 244.7 jit_solution(340746310664025728)
XLA Ops:
  0.6 0.0 copy-start
  0.6 0.8 broadcast_in_dim.29
  1.5 30.1 %all_to_all.35 = bf16[4,48,384]{2,1,0:T(8,128)(2,1)S(1)} all-to-all(bf16[4,48,384]{2,1,0:T(8,128)(2,1)S(1)} %broadcast_in_dim.29), channel_id=1, replica_groups=mesh['X'=4,'B'=4,'I'=4,'Y'=4,'C'=2] {'B'}, dimensions={0} | all-to-all | bytes 294912 | tf_op jit(solution)/shard_map/all_to_all | solution.py:31
  31.6 0.8 broadcast_in_dim.28
  32.3 0.0 copy-start.5
  32.4 0.0 copy-start.7
  32.4 15.9 %all_to_all.36 = bf16[16,32,384]{2,1,0:T(8,128)(2,1)S(1)} all-to-all(bf16[16,32,384]{2,1,0:T(8,128)(2,1)S(1)} %broadcast_in_dim.28), channel_id=1, replica_groups=mesh['X'=4,'B'=4,'I'=4,'Y'=4,'C'=2] {'X','I'}, dimensions={0} | all-to-all | bytes 786432 | tf_op jit(solution)/shard_map/all_to_all | solution.py:31
  48.3 0.3 convolution_convert_fusion.2
  48.6 0.1 copy.22
  48.8 0.8 reshape.86
  49.5 10.0 %all-to-all-start.2 = ((bf16[128,4,192]{2,1,0:T(4,128)(2,1)}), bf16[128,4,192]{2,1,0:T(4,128)(2,1)S(1)}, u32[]{:S(2)}, u32[]{:S(2)}) async-start(bf16[128,4,192]{2,1,0:T(4,128)(2,1)} %reshape.86), calls=%async_computation.2 | async-start | bytes 524288 | tf_op jit(solution)/shard_map/all_to_all | solution.py:31
  59.5 0.1 convert_reduce_fusion.2
  59.7 0.2 select_reduce_fusion.2
  59.9 0.1 fusion.5
  60.0 10.6 %all-to-all-done.2 = bf16[128,4,192]{2,1,0:T(4,128)(2,1)S(1)} async-done(((bf16[128,4,192]{2,1,0:T(4,128)(2,1)}), bf16[128,4,192]{2,1,0:T(4,128)(2,1)S(1)}, u32[]{:S(2)}, u32[]{:S(2)}) %all-to-all-start.2) | async-done | bytes 196640 | tf_op jit(solution)/shard_map/all_to_all | solution.py:31
  70.5 0.1 convert_reduce_fusion
  70.7 0.1 reshape.87
  70.9 0.2 reshape.88
  71.0 0.1 convert_reduce_fusion.1
  71.2 0.2 fusion.2
  71.4 0.3 convolution_convert_fusion
  71.7 0.1 reshape.89
  71.8 0.2 copy.25
  72.0 0.0 copy-start.1
  72.0 0.0 copy-start.2
  72.0 26.7 %all_to_all.37 = bf16[64,2,768]{2,1,0:T(2,128)(2,1)S(1)} all-to-all(bf16[64,2,768]{2,1,0:T(2,128)(2,1)S(1)} %bitcast.27), channel_id=1, replica_groups=mesh['X'=4,'B'=4,'I'=4,'Y'=4,'C'=2] {'X','B','I'}, dimensions={0} | all-to-all | bytes 393216 | tf_op jit(solution)/shard_map/all_to_all | solution.py:31
  98.7 0.7 broadcast_in_dim.60
  99.4 1.9 broadcast_in_dim.61
  101.3 4.2 %all-to-all-start.4 = ((bf16[4,128,768]{2,1,0:T(8,128)(2,1)}), bf16[4,128,768]{2,1,0:T(8,128)(2,1)}, u32[]{:S(2)}, u32[]{:S(2)}) async-start(bf16[4,128,768]{2,1,0:T(8,128)(2,1)} %broadcast_in_dim.61), calls=%async_computation.4 | async-start | bytes 1572864 | tf_op jit(solution)/shard_map/all_to_all | solution.py:31
  105.5 1.9 collective-permute-start
  107.4 2.4 collective-permute-start.1
  109.8 1.9 collective-permute-start.2
  111.8 12.4 %all-to-all-done.4.refs_0_ = bf16[4,128,768]{2,1,0:T(8,128)(2,1)} async-done(((bf16[4,128,768]{2,1,0:T(8,128)(2,1)}), bf16[4,128,768]{2,1,0:T(8,128)(2,1)}, u32[]{:S(2)}, u32[]{:S(2)}) %all-to-all-start.4) | async-done | bytes 786464 | tf_op jit(solution)/shard_map/all_to_all | solution.py:31
  124.1 4.0 %collective-permute-start.5 = (bf16[4,128,768]{2,1,0:T(8,128)(2,1)}, bf16[4,128,768]{2,1,0:T(8,128)(2,1)S(1)}, u32[]{:S(2)}, u32[]{:S(2)}) collective-permute-start(bf16[4,128,768]{2,1,0:T(8,128)(2,1)} %all-to-all-done.4.refs_0_), channel_id=1, source_target_pairs={{0,6},{2,0},{4,2},{6,4},{1,7},{3,1},{5,3},{7,5},{8,14},{10,8},{12,... | collective-permute-start | bytes 2359304 | tf_op jit(solution)/shard_map/ppermute | solution.py:146
  128.2 1.9 collective-permute-start.3
  130.1 14.6 %collective-permute-done.5.refs_1_ = bf16[4,128,768]{2,1,0:T(8,128)(2,1)S(1)} collective-permute-done((bf16[4,128,768]{2,1,0:T(8,128)(2,1)}, bf16[4,128,768]{2,1,0:T(8,128)(2,1)S(1)}, u32[]{:S(2)}, u32[]{:S(2)}) %collective-permute-start.5) | collective-permute-done | bytes 786464 | tf_op jit(solution)/shard_map/ppermute | solution.py:146
  144.8 5.2 %collective-permute-start.6 = (bf16[2,128,768]{2,1,0:T(8,128)(2,1)S(1)}, bf16[2,128,768]{2,1,0:T(8,128)(2,1)S(1)}, u32[]{:S(2)}, u32[]{:S(2)}) collective-permute-start(bf16[2,128,768]{2,1,0:T(8,128)(2,1)S(1)} %slice.9), channel_id=1, source_target_pairs={{0,6},{2,0},{4,2},{6,4},{1,7},{3,1},{5,3},{7,5},{8,14},{10,8},{12,... | collective-permute-start | bytes 1179656 | tf_op jit(solution)/shard_map/ppermute | solution.py:146
  150.0 0.0 collective-permute-done.3.refs_0_
  150.1 1.9 collective-permute-start.4
  152.0 0.0 collective-permute-done.1.refs_5_.refs_6_
  152.0 0.0 collective-permute-done.2.refs_6_.refs_7_
  152.0 0.0 copy-start.3
  152.0 1.4 copy-done.3
  153.4 5.0 %shard_map.106 = (bf16[4,128,768]{2,1,0:T(8,128)(2,1)S(1)}, bf16[4,128,768]{2,1,0:T(8,128)(2,1)S(1)}) custom-call(bf16[4,128,768]{2,1,0:T(8,128)(2,1)S(1)} %collective-permute-done.3.refs_0_, bf16[4,128,768]{2,1,0:T(8,128)(2,1)S(1)} %collective-permute-done.5.refs_1_, bf16[3072,256]{1,0:T(8,128)(2,1)S(1)} %copy-done.1, bf16[3072,256]{1,0:T(8,128)(2,1)S(1)} %copy-done.2, ...), custom_call_target="tpu_custom_call" | custom-call | flops 2415919104 | bytes 12582912 | tf_op jit(solution)/shard_map/pallas_call | solution.py:91
  158.5 5.1 %collective-permute-start.8 = (bf16[4,128,768]{2,1,0:T(8,128)(2,1)S(1)}, bf16[4,128,768]{2,1,0:T(8,128)(2,1)S(1)}, u32[]{:S(2)}, u32[]{:S(2)}) collective-permute-start(bf16[4,128,768]{2,1,0:T(8,128)(2,1)S(1)} %get-tuple-element.4), channel_id=1, source_target_pairs={{0,6},{2,0},{4,2},{6,4},{1,7},{3,1},{5,3},{7,5},{8,14},{10,8},{12,... | collective-permute-start | bytes 2359304 | tf_op jit(solution)/shard_map/ppermute | solution.py:146
  163.6 1.9 collective-permute-start.9
  165.6 3.9 %shard_map.105 = bf16[4,128,768]{2,1,0:T(8,128)(2,1)S(1)} custom-call(bf16[2,128,768]{2,1,0:T(8,128)(2,1)S(1)} %collective-permute-done.4.refs_0_, bf16[2,128,768]{2,1,0:T(8,128)(2,1)S(1)} %collective-permute-done.6.refs_1_, bf16[3072,256]{1,0:T(8,128)(2,1)S(1)} %copy-done.1, bf16[3072,256]{1,0:T(8,128)(2,1)S(1)} %copy-done.2, ...), custom_call_target="tpu_custom_call" | custom-call | flops 1207959552 | bytes 11010048 | tf_op jit(solution)/shard_map/pallas_call | solution.py:91
  169.4 3.4 %collective-permute-start.7 = (bf16[4,128,768]{2,1,0:T(8,128)(2,1)S(1)}, bf16[4,128,768]{2,1,0:T(8,128)(2,1)S(1)}, u32[]{:S(2)}, u32[]{:S(2)}) collective-permute-start(bf16[4,128,768]{2,1,0:T(8,128)(2,1)S(1)} %shard_map.105), channel_id=1, source_target_pairs={{0,4},{2,6},{4,0},{6,2},{1,5},{3,7},{5,1},{7,3},{8,12},{10,14},{12... | collective-permute-start | bytes 2359304 | tf_op jit(solution)/shard_map/ppermute | solution.py:146
  172.8 4.1 %shard_map.104 = bf16[4,128,768]{2,1,0:T(8,128)(2,1)S(1)} custom-call(bf16[4,128,768]{2,1,0:T(8,128)(2,1)} %all-to-all-done.4.refs_0_, bf16[3072,256]{1,0:T(8,128)(2,1)S(1)} %copy-done.1, bf16[3072,256]{1,0:T(8,128)(2,1)S(1)} %copy-done.2, bf16[256,3072]{1,0:T(8,128)(2,1)S(1)} %copy-done.3, bf16[3072,256]{1,0:T(8,128)(2,1)} %collective-permute-done.refs_4_.refs_5_, ...), custom_call_target="tpu_custom_call" | custom-call | flops 1207959552 | bytes 11010048 | tf_op jit(solution)/shard_map/pallas_call | solution.py:91
  176.9 18.0 %collective-permute-done.8 = bf16[4,128,768]{2,1,0:T(8,128)(2,1)S(1)} collective-permute-done((bf16[4,128,768]{2,1,0:T(8,128)(2,1)S(1)}, bf16[4,128,768]{2,1,0:T(8,128)(2,1)S(1)}, u32[]{:S(2)}, u32[]{:S(2)}) %collective-permute-start.8) | collective-permute-done | bytes 786464 | tf_op jit(solution)/shard_map/ppermute | solution.py:146
  195.0 5.3 %collective-permute-done.9 = bf16[4,128,768]{2,1,0:T(8,128)(2,1)S(1)} collective-permute-done((bf16[4,128,768]{2,1,0:T(8,128)(2,1)S(1)}, bf16[4,128,768]{2,1,0:T(8,128)(2,1)S(1)}, u32[]{:S(2)}, u32[]{:S(2)}) %collective-permute-start.9) | collective-permute-done | bytes 786464 | tf_op jit(solution)/shard_map/ppermute | solution.py:146
  200.3 0.4 add_convert_fusion
  200.7 18.2 %all_to_all.38 = bf16[4,128,768]{2,1,0:T(8,128)(2,1)S(1)} all-to-all(bf16[4,128,768]{2,1,0:T(8,128)(2,1)S(1)} %add_convert_fusion), channel_id=1, replica_groups=mesh['X'=4,'B'=4,'I'=4,'Y'=4,'C'=2] {'I'}, dimensions={0} | all-to-all | bytes 1572864 | tf_op jit(solution)/shard_map/all_to_all | solution.py:31
  218.9 0.1 reduce_sum.92
  219.0 0.7 reshape.91
  219.7 7.7 %all-to-all-start.6 = ((bf16[64,2,768]{2,1,0:T(2,128)(2,1)}), bf16[64,2,768]{2,1,0:T(2,128)(2,1)S(1)}, u32[]{:S(2)}, u32[]{:S(2)}) async-start(bf16[64,2,768]{2,1,0:T(2,128)(2,1)} %reshape.91), calls=%async_computation.6 | async-start | bytes 393216 | tf_op jit(solution)/shard_map/all_to_all | solution.py:31
  227.5 0.2 fusion.7
  227.7 0.2 select_reduce_fusion.1
  227.9 0.1 exponential_reduce_fusion
  228.0 0.1 exponential_divide_fusion
  228.0 0.1 select_reduce_fusion
  228.2 15.6 %all-to-all-done.6 = bf16[64,2,768]{2,1,0:T(2,128)(2,1)S(1)} async-done(((bf16[64,2,768]{2,1,0:T(2,128)(2,1)}), bf16[64,2,768]{2,1,0:T(2,128)(2,1)S(1)}, u32[]{:S(2)}, u32[]{:S(2)}) %all-to-all-start.6) | async-done | bytes 196640 | tf_op jit(solution)/shard_map/all_to_all | solution.py:31
  243.8 0.1 copy.26
  243.9 0.8 convolution_convert_fusion.1
  (24 shorter events, 0.2 us)
Async XLA Ops:
  0.6 226.9 %copy-start = (bf16[3072,16]{0,1:T(8,128)(2,1)S(1)}, bf16[3072,16]{0,1:T(8,128)(2,1)}, u32[]{:S(2)}) copy-start(bf16[3072,16]{0,1:T(8,128)(2,1)} %param.13) | copy-start | bytes 294916
  32.3 27.2 %copy-start.5 = (s32[4,4]{1,0:T(4,128)S(1)}, s32[4,4]{1,0:T(4,128)}, u32[]{:S(2)}) copy-start(s32[4,4]{1,0:T(4,128)} %param.17) | copy-start | bytes 196
  32.4 27.3 %copy-start.7 = (bf16[3072]{0:T(1024)(128)(2,1)S(1)}, bf16[3072]{0:T(1024)(128)(2,1)}, u32[]{:S(2)}) copy-start(bf16[3072]{0:T(1024)(128)(2,1)} %param.12) | copy-start | bytes 18436
  48.3 22.7 %copy-start.6 = (bf16[4,3072]{1,0:T(4,128)(2,1)S(1)}, bf16[4,3072]{1,0:T(4,128)(2,1)}, u32[]{:S(2)}) copy-start(bf16[4,3072]{1,0:T(4,128)(2,1)} %param.11) | copy-start | bytes 73732
  49.5 21.0 %all-to-all-start.2 = ((bf16[128,4,192]{2,1,0:T(4,128)(2,1)}), bf16[128,4,192]{2,1,0:T(4,128)(2,1)S(1)}, u32[]{:S(2)}, u32[]{:S(2)}) async-start(bf16[128,4,192]{2,1,0:T(4,128)(2,1)} %reshape.86), calls=%async_computation.2 | async-start | bytes 524288 | tf_op jit(solution)/shard_map/all_to_all | solution.py:31
  71.2 156.3 %copy-start.4 = (bf16[4,3072]{1,0:T(4,128)(2,1)}, bf16[4,3072]{1,0:T(4,128)(2,1)S(1)}, u32[]{:S(2)}) copy-start(bf16[4,3072]{1,0:T(4,128)(2,1)S(1)} %get-tuple-element.7) | copy-start | bytes 73732
  72.0 33.5 %copy-start.1 = (bf16[3072,256]{1,0:T(8,128)(2,1)S(1)}, bf16[3072,256]{1,0:T(8,128)(2,1)}, u32[]{:S(2)}) copy-start(bf16[3072,256]{1,0:T(8,128)(2,1)} %refs_2_.5) | copy-start | bytes 4718596
  72.0 35.4 %copy-start.2 = (bf16[3072,256]{1,0:T(8,128)(2,1)S(1)}, bf16[3072,256]{1,0:T(8,128)(2,1)}, u32[]{:S(2)}) copy-start(bf16[3072,256]{1,0:T(8,128)(2,1)} %refs_3_.5) | copy-start | bytes 4718596
  101.3 22.9 %all-to-all-start.4 = ((bf16[4,128,768]{2,1,0:T(8,128)(2,1)}), bf16[4,128,768]{2,1,0:T(8,128)(2,1)}, u32[]{:S(2)}, u32[]{:S(2)}) async-start(bf16[4,128,768]{2,1,0:T(8,128)(2,1)} %broadcast_in_dim.61), calls=%async_computation.4 | async-start | bytes 1572864 | tf_op jit(solution)/shard_map/all_to_all | solution.py:31
  105.5 46.5 %collective-permute-start = (bf16[3072,256]{1,0:T(8,128)(2,1)S(1)}, bf16[3072,256]{1,0:T(8,128)(2,1)}, u32[]{:S(2)}, u32[]{:S(2)}) collective-permute-start(bf16[3072,256]{1,0:T(8,128)(2,1)S(1)} %copy-done.1), channel_id=1, source_target_pairs={{0,1},{1,0},{2,3},{3,2},{4,5},{5,4},{6,7},{7,6},{8,9},{9,8},{10,11... | collective-permute-start | bytes 4718600 | tf_op jit(solution)/shard_map/ppermute | solution.py:120
  107.4 44.6 %collective-permute-start.1 = (bf16[3072,256]{1,0:T(8,128)(2,1)S(1)}, bf16[3072,256]{1,0:T(8,128)(2,1)}, u32[]{:S(2)}, u32[]{:S(2)}) collective-permute-start(bf16[3072,256]{1,0:T(8,128)(2,1)S(1)} %copy-done.2), channel_id=1, source_target_pairs={{0,1},{1,0},{2,3},{3,2},{4,5},{5,4},{6,7},{7,6},{8,9},{9,8},{10,11... | collective-permute-start | bytes 4718600 | tf_op jit(solution)/shard_map/ppermute | solution.py:120
  109.8 42.2 %collective-permute-start.2 = (bf16[256,3072]{1,0:T(8,128)(2,1)}, bf16[256,3072]{1,0:T(8,128)(2,1)}, u32[]{:S(2)}, u32[]{:S(2)}) collective-permute-start(bf16[256,3072]{1,0:T(8,128)(2,1)} %refs_4_.3), channel_id=1, source_target_pairs={{0,1},{1,0},{2,3},{3,2},{4,5},{5,4},{6,7},{7,6},{8,9},{9,8},{10,11... | collective-permute-start | bytes 4718600 | tf_op jit(solution)/shard_map/ppermute | solution.py:120
  124.1 20.6 %collective-permute-start.5 = (bf16[4,128,768]{2,1,0:T(8,128)(2,1)}, bf16[4,128,768]{2,1,0:T(8,128)(2,1)S(1)}, u32[]{:S(2)}, u32[]{:S(2)}) collective-permute-start(bf16[4,128,768]{2,1,0:T(8,128)(2,1)} %all-to-all-done.4.refs_0_), channel_id=1, source_target_pairs={{0,6},{2,0},{4,2},{6,4},{1,7},{3,1},{5,3},{7,5},{8,14},{10,8},{12,... | collective-permute-start | bytes 2359304 | tf_op jit(solution)/shard_map/ppermute | solution.py:146
  128.2 21.8 %collective-permute-start.3 = (bf16[4,128,768]{2,1,0:T(8,128)(2,1)}, bf16[4,128,768]{2,1,0:T(8,128)(2,1)S(1)}, u32[]{:S(2)}, u32[]{:S(2)}) collective-permute-start(bf16[4,128,768]{2,1,0:T(8,128)(2,1)} %all-to-all-done.4.refs_0_), channel_id=1, source_target_pairs={{0,2},{2,4},{4,6},{6,0},{1,3},{3,5},{5,7},{7,1},{8,10},{10,12},{12... | collective-permute-start | bytes 2359304 | tf_op jit(solution)/shard_map/ppermute | solution.py:146
  144.8 20.8 %collective-permute-start.6 = (bf16[2,128,768]{2,1,0:T(8,128)(2,1)S(1)}, bf16[2,128,768]{2,1,0:T(8,128)(2,1)S(1)}, u32[]{:S(2)}, u32[]{:S(2)}) collective-permute-start(bf16[2,128,768]{2,1,0:T(8,128)(2,1)S(1)} %slice.9), channel_id=1, source_target_pairs={{0,6},{2,0},{4,2},{6,4},{1,7},{3,1},{5,3},{7,5},{8,14},{10,8},{12,... | collective-permute-start | bytes 1179656 | tf_op jit(solution)/shard_map/ppermute | solution.py:146
  150.1 15.5 %collective-permute-start.4 = (bf16[2,128,768]{2,1,0:T(8,128)(2,1)S(1)}, bf16[2,128,768]{2,1,0:T(8,128)(2,1)S(1)}, u32[]{:S(2)}, u32[]{:S(2)}) collective-permute-start(bf16[2,128,768]{2,1,0:T(8,128)(2,1)S(1)} %slice.8), channel_id=1, source_target_pairs={{0,2},{2,4},{4,6},{6,0},{1,3},{3,5},{5,7},{7,1},{8,10},{10,12},{12... | collective-permute-start | bytes 1179656 | tf_op jit(solution)/shard_map/ppermute | solution.py:146
  152.0 1.4 copy-start.3
  158.5 36.5 %collective-permute-start.8 = (bf16[4,128,768]{2,1,0:T(8,128)(2,1)S(1)}, bf16[4,128,768]{2,1,0:T(8,128)(2,1)S(1)}, u32[]{:S(2)}, u32[]{:S(2)}) collective-permute-start(bf16[4,128,768]{2,1,0:T(8,128)(2,1)S(1)} %get-tuple-element.4), channel_id=1, source_target_pairs={{0,6},{2,0},{4,2},{6,4},{1,7},{3,1},{5,3},{7,5},{8,14},{10,8},{12,... | collective-permute-start | bytes 2359304 | tf_op jit(solution)/shard_map/ppermute | solution.py:146
  163.6 36.7 %collective-permute-start.9 = (bf16[4,128,768]{2,1,0:T(8,128)(2,1)S(1)}, bf16[4,128,768]{2,1,0:T(8,128)(2,1)S(1)}, u32[]{:S(2)}, u32[]{:S(2)}) collective-permute-start(bf16[4,128,768]{2,1,0:T(8,128)(2,1)S(1)} %get-tuple-element.5), channel_id=1, source_target_pairs={{0,2},{2,4},{4,6},{6,0},{1,3},{3,5},{5,7},{7,1},{8,10},{10,12},{12... | collective-permute-start | bytes 2359304 | tf_op jit(solution)/shard_map/ppermute | solution.py:146
  169.4 30.9 %collective-permute-start.7 = (bf16[4,128,768]{2,1,0:T(8,128)(2,1)S(1)}, bf16[4,128,768]{2,1,0:T(8,128)(2,1)S(1)}, u32[]{:S(2)}, u32[]{:S(2)}) collective-permute-start(bf16[4,128,768]{2,1,0:T(8,128)(2,1)S(1)} %shard_map.105), channel_id=1, source_target_pairs={{0,4},{2,6},{4,0},{6,2},{1,5},{3,7},{5,1},{7,3},{8,12},{10,14},{12... | collective-permute-start | bytes 2359304 | tf_op jit(solution)/shard_map/ppermute | solution.py:146
  219.7 24.0 %all-to-all-start.6 = ((bf16[64,2,768]{2,1,0:T(2,128)(2,1)}), bf16[64,2,768]{2,1,0:T(2,128)(2,1)S(1)}, u32[]{:S(2)}, u32[]{:S(2)}) async-start(bf16[64,2,768]{2,1,0:T(2,128)(2,1)} %reshape.91), calls=%async_computation.6 | async-start | bytes 393216 | tf_op jit(solution)/shard_map/all_to_all | solution.py:31

commit v4 on v3

--- a/solution.py
+++ b/solution.py
@@ -31,22 +31,16 @@
     return lax.all_to_all(value, axes, split_axis=0, concat_axis=0, tiled=True)
 
 
-def spread(value, axes, parts):
-    return swap(jnp.broadcast_to(value[None], (parts,) + value.shape), axes)
-
-
 def attention_rows(context, out_weight):
-    tokens = spread(context, ("X", "I"), 16).reshape(-1, context.shape[1])
-    columns = spread(out_weight.T, "B", 4).reshape(-1, out_weight.shape[0])
+    tokens = lax.all_gather(context, "X", axis=0, tiled=True)
+    columns = lax.all_gather(out_weight.T, ("B", "I"), axis=0, tiled=True)
     partial_sum = lax.dot_general(
         tokens, columns, (((1,), (1,)), ((), ())), preferred_element_type=jnp.float32
     ).astype(jnp.bfloat16)
     width = columns.shape[0]
-    pieces = swap(partial_sum.reshape(128, -1, width), ("X", "I", "Y", "C"))
-    count = pieces.shape[1]
-    pieces = pieces.reshape(16, 8, count, width).astype(jnp.float32)
-    summed = jnp.sum(pieces, axis=1).reshape(4, 4, count, 4, width // 4)
-    return jnp.transpose(summed, (2, 0, 3, 1, 4)).reshape(count, 16 * width)
+    pieces = swap(partial_sum.reshape(32, -1, width), ("X", "Y", "C"))
+    pieces = pieces.reshape(4, 8, -1, width).astype(jnp.float32)
+    return jnp.transpose(jnp.sum(pieces, axis=1), (1, 0, 2)).reshape(-1, 4 * width)
 
 
 def expert_kernel(layout, *refs):
@@ -137,10 +131,11 @@
         assign.astype(jnp.bfloat16).T, normed, preferred_element_type=jnp.float32
     ).astype(jnp.bfloat16)
 
+    send_rows, partner = lax.optimization_barrier((send_rows, partner))
     quarter = width // 4
     outgoing = jnp.transpose(send_rows.reshape(experts, CAP, 4, quarter), (0, 2, 1, 3))
     landed = swap(outgoing.reshape(4 * experts, CAP, quarter), EXPERT)
-    block_rows = spread(landed.reshape(-1, quarter), "I", 4)
+    block_rows = lax.all_gather(landed.reshape(-1, quarter), "I")
 
     def turn(value, by):
         return lax.ppermute(value, "Y", [(i, (i + by) % 4) for i in range(4)])

time: 246 us -> 231 us (0.939)
  waiting for transfers between devices: 76.5 us -> 48.8 us
  blocking collectives: 90.9 us -> 115 us
  starting transfers between devices: 51.7 us -> 45.7 us
  local copies, waits for them, and re-layouts: 8.07 us -> 5.24 us
    all_gather x0 -> x3, blocking collectives: none -> 69.3 us  [the longest x1 36.1 us: attention_rows(): columns = lax.all_gather(out_weight.T, ('B', 'I'), axis=0, tiled=True)]
    all_to_all x4 -> x2, blocking collectives: 90.9 us -> 45.5 us  [swap(): return lax.all_to_all(value, axes, split_axis=0, concat_axis=0, tiled=True)]
    all_to_all x3 -> x2, waiting for transfers between devices: 38.5 us -> 14.7 us  [swap(): return lax.all_to_all(value, axes, split_axis=0, concat_axis=0, tiled=True)]
    all_to_all x3 -> x2, starting transfers between devices: 21.9 us -> 14.9 us  [swap(): return lax.all_to_all(value, axes, split_axis=0, concat_axis=0, tiled=True)]
    ppermute x7, waiting for transfers between devices: 38 us -> 32.7 us  [turn(): return lax.ppermute(value, 'Y', [(i, (i + by) % 4) for i in range(4)])]
    broadcast_in_dim x4 -> x0, local copies, waits for them, and re-layouts: 4.2 us -> none  [spread(): return swap(jnp.broadcast_to(value[None], (parts,) + value.shape), axes)]
  transfers between devices with their start and end apart: 13 -> 12, of which waited for: 6 -> 5; matrix products, arithmetic and copies ran while one was open for 0% -> 1% of each run, Pallas kernels for 5% -> 5%
where the time goes in v4:
time: 231 us; the launch traced here: 230 us
  blocking collectives  115 us (50%)
  waiting for transfers between devices  48.8 us (21%)
  starting transfers between devices  45.7 us (20%)
  Pallas kernels  11.4 us (5%)
  local copies, waits for them, and re-layouts  5.24 us (2%)
    all_to_all x2, blocking collectives, swap(): return lax.all_to_all(value, axes, split_axis=0, concat_axis=0, tiled=True)  45.5 us
    all_gather x1, blocking collectives, attention_rows(): columns = lax.all_gather(out_weight.T, ('B', 'I'), axis=0, tiled=True)  36.1 us
    ppermute x7, waiting for transfers between devices, turn(): return lax.ppermute(value, 'Y', [(i, (i + by) % 4) for i in range(4)])  32.7 us
    ppermute x7, starting transfers between devices, turn(): return lax.ppermute(value, 'Y', [(i, (i + by) % 4) for i in range(4)])  24.5 us
    all_gather x1, blocking collectives, on_device(): block_rows = lax.all_gather(landed.reshape(-1, quarter), 'I')  18.2 us
    all_gather x1, blocking collectives, attention_rows(): tokens = lax.all_gather(context, 'X', axis=0, tiled=True)  15 us
    all_to_all x2, starting transfers between devices, swap(): return lax.all_to_all(value, axes, split_axis=0, concat_axis=0, tiled=True)  14.9 us
    all_to_all x2, waiting for transfers between devices, swap(): return lax.all_to_all(value, axes, split_axis=0, concat_axis=0, tiled=True)  14.7 us
  transfers between devices with their start and end apart: 12, of which 5 were waited for; matrix products, arithmetic and copies ran while one was open for 1% of the time, Pallas kernels for 5%

profile of v4, /device:TPU:6, one launch (start us, length us, event | category | flops | bytes accessed | tf_op | source)
XLA Modules:
  0.0 230.3 jit_solution(1056914703944742551)
XLA Ops:
  0.6 0.0 copy-start
  0.6 0.0 copy-start.1
  0.7 0.0 copy-start.7
  0.7 0.0 copy-start.9
  0.7 0.0 copy-start.8
  0.7 15.0 %all_gather.9 = bf16[128,384]{1,0:T(8,128)(2,1)S(1)} all-gather(bf16[32,384]{1,0:T(8,128)(2,1)} %param.9), channel_id=1, replica_groups=mesh['X'=4,'B'=4,'I'=4,'Y'=4,'C'=2] {'X'}, dimensions={0}, use_global_device_ids=true | all-gather | bytes 122880 | tf_op jit(solution)/shard_map/all_gather | solution.py:35
  15.7 36.1 %all_gather.10 = bf16[768,384]{1,0:T(8,128)(2,1)S(1)} all-gather(bf16[48,384]{1,0:T(8,128)(2,1)} %bitcast.27), channel_id=1, replica_groups=mesh['X'=4,'B'=4,'I'=4,'Y'=4,'C'=2] {'B','I'}, dimensions={0}, use_global_device_ids=true | all-gather | bytes 626688 | tf_op jit(solution)/shard_map/all_gather | solution.py:36
  51.7 0.3 convolution_convert_fusion.2
  52.1 0.7 reshape.72
  52.8 7.3 %all-to-all-start = ((bf16[32,4,768]{2,1,0:T(4,128)(2,1)}), bf16[32,4,768]{2,1,0:T(4,128)(2,1)S(1)}, u32[]{:S(2)}, u32[]{:S(2)}) async-start(bf16[32,4,768]{2,1,0:T(4,128)(2,1)} %reshape.72), calls=%async_computation | async-start | bytes 393216 | tf_op jit(solution)/shard_map/all_to_all | solution.py:31
  60.2 2.1 collective-permute-start
  62.2 2.3 collective-permute-start.1
  64.5 2.1 collective-permute-start.2
  66.6 0.1 convert_reduce_fusion.2
  66.7 0.2 select_reduce_fusion.2
  67.0 0.1 fusion.5
  67.1 0.0 all-to-all-done
  67.1 0.1 convert_reduce_fusion
  67.1 0.0 copy-done.8
  67.2 0.1 convert_reduce_fusion.1
  67.3 0.2 fusion.2
  67.5 0.3 convolution_convert_fusion
  67.8 0.0 collective-permute-done.refs_4_.refs_5_
  67.8 1.1 copy-done.4
  68.9 0.0 collective-permute-done.1.refs_5_.refs_6_
  68.9 1.4 collective-permute-done.2.refs_6_.refs_7_
  70.3 0.1 reshape.74
  70.4 0.2 copy.18
  70.6 0.0 copy-start.2
  70.6 28.7 %all_to_all.20 = bf16[64,2,768]{2,1,0:T(2,128)(2,1)S(1)} all-to-all(bf16[64,2,768]{2,1,0:T(2,128)(2,1)S(1)} %bitcast.24), channel_id=1, replica_groups=mesh['X'=4,'B'=4,'I'=4,'Y'=4,'C'=2] {'X','B','I'}, dimensions={0} | all-to-all | bytes 393216 | tf_op jit(solution)/shard_map/all_to_all | solution.py:31
  99.3 0.7 all_gather_reshape.3
  100.0 18.2 %all_gather.11.refs_0_ = bf16[4,128,768]{2,1,0:T(8,128)(2,1)S(1)} all-gather(bf16[1,128,768]{2,1,0:T(8,128)(2,1)} %all_gather_reshape.3), channel_id=1, replica_groups=mesh['X'=4,'B'=4,'I'=4,'Y'=4,'C'=2] {'I'}, dimensions={0}, use_global_device_ids=true | all-gather | bytes 983040 | tf_op jit(solution)/shard_map/all_gather | solution.py:138
  118.2 4.6 %collective-permute-start.5 = (bf16[4,128,768]{2,1,0:T(8,128)(2,1)S(1)}, bf16[4,128,768]{2,1,0:T(8,128)(2,1)S(1)}, u32[]{:S(2)}, u32[]{:S(2)}) collective-permute-start(bf16[4,128,768]{2,1,0:T(8,128)(2,1)S(1)} %all_gather.11.refs_0_), channel_id=1, source_target_pairs={{0,6},{2,0},{4,2},{6,4},{1,7},{3,1},{5,3},{7,5},{8,14},{10,8},{12,... | collective-permute-start | bytes 2359304 | tf_op jit(solution)/shard_map/ppermute | solution.py:141
  122.8 1.9 collective-permute-start.3
  124.8 11.1 %collective-permute-done.5.refs_1_ = bf16[4,128,768]{2,1,0:T(8,128)(2,1)S(1)} collective-permute-done((bf16[4,128,768]{2,1,0:T(8,128)(2,1)S(1)}, bf16[4,128,768]{2,1,0:T(8,128)(2,1)S(1)}, u32[]{:S(2)}, u32[]{:S(2)}) %collective-permute-start.5) | collective-permute-done | bytes 786464 | tf_op jit(solution)/shard_map/ppermute | solution.py:141
  135.9 5.6 %collective-permute-start.6 = (bf16[2,128,768]{2,1,0:T(8,128)(2,1)S(1)}, bf16[2,128,768]{2,1,0:T(8,128)(2,1)S(1)}, u32[]{:S(2)}, u32[]{:S(2)}) collective-permute-start(bf16[2,128,768]{2,1,0:T(8,128)(2,1)S(1)} %slice.9), channel_id=1, source_target_pairs={{0,6},{2,0},{4,2},{6,4},{1,7},{3,1},{5,3},{7,5},{8,14},{10,8},{12,... | collective-permute-start | bytes 1179656 | tf_op jit(solution)/shard_map/ppermute | solution.py:141
  141.5 0.0 collective-permute-done.3.refs_0_
  141.6 1.9 collective-permute-start.4
  143.5 0.0 copy-done.2
  143.5 1.4 copy-done.5
  144.9 4.6 %shard_map.106 = (bf16[4,128,768]{2,1,0:T(8,128)(2,1)S(1)}, bf16[4,128,768]{2,1,0:T(8,128)(2,1)S(1)}) custom-call(bf16[4,128,768]{2,1,0:T(8,128)(2,1)S(1)} %collective-permute-done.3.refs_0_, bf16[4,128,768]{2,1,0:T(8,128)(2,1)S(1)} %collective-permute-done.5.refs_1_, bf16[3072,256]{1,0:T(8,128)(2,1)S(1)} %copy-done.1, bf16[3072,256]{1,0:T(8,128)(2,1)S(1)} %copy-done.2, ...), custom_call_target="tpu_custom_call" | custom-call | flops 2415919104 | bytes 12582912 | tf_op jit(solution)/shard_map/pallas_call | solution.py:85
  149.5 5.1 %collective-permute-start.8 = (bf16[4,128,768]{2,1,0:T(8,128)(2,1)S(1)}, bf16[4,128,768]{2,1,0:T(8,128)(2,1)S(1)}, u32[]{:S(2)}, u32[]{:S(2)}) collective-permute-start(bf16[4,128,768]{2,1,0:T(8,128)(2,1)S(1)} %get-tuple-element.12), channel_id=1, source_target_pairs={{0,6},{2,0},{4,2},{6,4},{1,7},{3,1},{5,3},{7,5},{8,14},{10,8},{12,... | collective-permute-start | bytes 2359304 | tf_op jit(solution)/shard_map/ppermute | solution.py:141
  154.7 1.9 collective-permute-start.9
  156.6 0.0 collective-permute-done.6.refs_1_
  156.6 0.0 collective-permute-done.4.refs_0_
  156.6 3.4 %shard_map.105 = bf16[4,128,768]{2,1,0:T(8,128)(2,1)S(1)} custom-call(bf16[2,128,768]{2,1,0:T(8,128)(2,1)S(1)} %collective-permute-done.4.refs_0_, bf16[2,128,768]{2,1,0:T(8,128)(2,1)S(1)} %collective-permute-done.6.refs_1_, bf16[3072,256]{1,0:T(8,128)(2,1)S(1)} %copy-done.1, bf16[3072,256]{1,0:T(8,128)(2,1)S(1)} %copy-done.2, ...), custom_call_target="tpu_custom_call" | custom-call | flops 1207959552 | bytes 11010048 | tf_op jit(solution)/shard_map/pallas_call | solution.py:85
  160.0 3.4 %collective-permute-start.7 = (bf16[4,128,768]{2,1,0:T(8,128)(2,1)S(1)}, bf16[4,128,768]{2,1,0:T(8,128)(2,1)S(1)}, u32[]{:S(2)}, u32[]{:S(2)}) collective-permute-start(bf16[4,128,768]{2,1,0:T(8,128)(2,1)S(1)} %shard_map.105), channel_id=1, source_target_pairs={{0,4},{2,6},{4,0},{6,2},{1,5},{3,7},{5,1},{7,3},{8,12},{10,14},{12... | collective-permute-start | bytes 2359304 | tf_op jit(solution)/shard_map/ppermute | solution.py:141
  163.4 3.4 %shard_map.104 = bf16[4,128,768]{2,1,0:T(8,128)(2,1)S(1)} custom-call(bf16[4,128,768]{2,1,0:T(8,128)(2,1)S(1)} %all_gather.11.refs_0_, bf16[3072,256]{1,0:T(8,128)(2,1)S(1)} %copy-done.1, bf16[3072,256]{1,0:T(8,128)(2,1)S(1)} %copy-done.2, bf16[256,3072]{1,0:T(8,128)(2,1)S(1)} %copy-done.3, bf16[3072,256]{1,0:T(8,128)(2,1)S(1)} %copy-done.5, ...), custom_call_target="tpu_custom_call" | custom-call | flops 1207959552 | bytes 11010048 | tf_op jit(solution)/shard_map/pallas_call | solution.py:85
  166.8 16.3 %collective-permute-done.8 = bf16[4,128,768]{2,1,0:T(8,128)(2,1)S(1)} collective-permute-done((bf16[4,128,768]{2,1,0:T(8,128)(2,1)S(1)}, bf16[4,128,768]{2,1,0:T(8,128)(2,1)S(1)}, u32[]{:S(2)}, u32[]{:S(2)}) %collective-permute-start.8) | collective-permute-done | bytes 786464 | tf_op jit(solution)/shard_map/ppermute | solution.py:141
  183.1 5.3 %collective-permute-done.9 = bf16[4,128,768]{2,1,0:T(8,128)(2,1)S(1)} collective-permute-done((bf16[4,128,768]{2,1,0:T(8,128)(2,1)S(1)}, bf16[4,128,768]{2,1,0:T(8,128)(2,1)S(1)}, u32[]{:S(2)}, u32[]{:S(2)}) %collective-permute-start.9) | collective-permute-done | bytes 786464 | tf_op jit(solution)/shard_map/ppermute | solution.py:141
  188.4 0.0 collective-permute-done.7
  188.4 0.4 add_convert_fusion
  188.8 16.9 %all_to_all.21 = bf16[4,128,768]{2,1,0:T(8,128)(2,1)S(1)} all-to-all(bf16[4,128,768]{2,1,0:T(8,128)(2,1)S(1)} %add_convert_fusion), channel_id=1, replica_groups=mesh['X'=4,'B'=4,'I'=4,'Y'=4,'C'=2] {'I'}, dimensions={0} | all-to-all | bytes 1572864 | tf_op jit(solution)/shard_map/all_to_all | solution.py:31
  205.7 0.1 reduce_sum.92
  205.8 0.7 reshape.76
  206.5 7.5 %all-to-all-start.3 = ((bf16[64,2,768]{2,1,0:T(2,128)(2,1)}), bf16[64,2,768]{2,1,0:T(2,128)(2,1)S(1)}, u32[]{:S(2)}, u32[]{:S(2)}) async-start(bf16[64,2,768]{2,1,0:T(2,128)(2,1)} %reshape.76), calls=%async_computation.3 | async-start | bytes 393216 | tf_op jit(solution)/shard_map/all_to_all | solution.py:31
  214.1 0.2 fusion.7
  214.3 0.2 select_reduce_fusion.1
  214.5 0.1 exponential_reduce_fusion
  214.6 0.1 exponential_divide_fusion
  214.7 0.1 select_reduce_fusion
  214.8 14.7 %all-to-all-done.3 = bf16[64,2,768]{2,1,0:T(2,128)(2,1)S(1)} async-done(((bf16[64,2,768]{2,1,0:T(2,128)(2,1)}), bf16[64,2,768]{2,1,0:T(2,128)(2,1)S(1)}, u32[]{:S(2)}, u32[]{:S(2)}) %all-to-all-start.3) | async-done | bytes 196640 | tf_op jit(solution)/shard_map/all_to_all | solution.py:31
  229.4 0.1 copy.19
  229.5 0.8 convolution_convert_fusion.1
  (19 shorter events, 0.2 us)
Async XLA Ops:
  0.6 213.5 %copy-start = (bf16[3072,16]{0,1:T(8,128)(2,1)S(1)}, bf16[3072,16]{0,1:T(8,128)(2,1)}, u32[]{:S(2)}) copy-start(bf16[3072,16]{0,1:T(8,128)(2,1)} %param.13) | copy-start | bytes 294916
  0.6 59.5 %copy-start.1 = (bf16[3072,256]{1,0:T(8,128)(2,1)S(1)}, bf16[3072,256]{1,0:T(8,128)(2,1)}, u32[]{:S(2)}) copy-start(bf16[3072,256]{1,0:T(8,128)(2,1)} %refs_2_.5) | copy-start | bytes 4718596
  0.7 65.9 %copy-start.7 = (s32[4,4]{1,0:T(4,128)S(1)}, s32[4,4]{1,0:T(4,128)}, u32[]{:S(2)}) copy-start(s32[4,4]{1,0:T(4,128)} %param.17) | copy-start | bytes 196
  0.7 66.3 %copy-start.9 = (bf16[3072]{0:T(1024)(128)(2,1)S(1)}, bf16[3072]{0:T(1024)(128)(2,1)}, u32[]{:S(2)}) copy-start(bf16[3072]{0:T(1024)(128)(2,1)} %param.12) | copy-start | bytes 18436
  0.7 66.5 %copy-start.8 = (bf16[4,3072]{1,0:T(4,128)(2,1)S(1)}, bf16[4,3072]{1,0:T(4,128)(2,1)}, u32[]{:S(2)}) copy-start(bf16[4,3072]{1,0:T(4,128)(2,1)} %param.11) | copy-start | bytes 73732
  52.8 14.3 %all-to-all-start = ((bf16[32,4,768]{2,1,0:T(4,128)(2,1)}), bf16[32,4,768]{2,1,0:T(4,128)(2,1)S(1)}, u32[]{:S(2)}, u32[]{:S(2)}) async-start(bf16[32,4,768]{2,1,0:T(4,128)(2,1)} %reshape.72), calls=%async_computation | async-start | bytes 393216 | tf_op jit(solution)/shard_map/all_to_all | solution.py:31
  60.2 7.6 %collective-permute-start = (bf16[3072,256]{1,0:T(8,128)(2,1)S(1)}, bf16[3072,256]{1,0:T(8,128)(2,1)S(1)}, u32[]{:S(2)}, u32[]{:S(2)}) collective-permute-start(bf16[3072,256]{1,0:T(8,128)(2,1)S(1)} %copy-done.1), channel_id=1, source_target_pairs={{0,1},{1,0},{2,3},{3,2},{4,5},{5,4},{6,7},{7,6},{8,9},{9,8},{10,11... | collective-permute-start | bytes 4718600 | tf_op jit(solution)/shard_map/ppermute | solution.py:114
  62.2 6.7 %collective-permute-start.1 = (bf16[3072,256]{1,0:T(8,128)(2,1)}, bf16[3072,256]{1,0:T(8,128)(2,1)}, u32[]{:S(2)}, u32[]{:S(2)}) collective-permute-start(bf16[3072,256]{1,0:T(8,128)(2,1)} %refs_3_.5), channel_id=1, source_target_pairs={{0,1},{1,0},{2,3},{3,2},{4,5},{5,4},{6,7},{7,6},{8,9},{9,8},{10,11... | collective-permute-start | bytes 4718600 | tf_op jit(solution)/shard_map/ppermute | solution.py:114
  64.5 5.8 %collective-permute-start.2 = (bf16[256,3072]{1,0:T(8,128)(2,1)}, bf16[256,3072]{1,0:T(8,128)(2,1)}, u32[]{:S(2)}, u32[]{:S(2)}) collective-permute-start(bf16[256,3072]{1,0:T(8,128)(2,1)} %refs_4_.3), channel_id=1, source_target_pairs={{0,1},{1,0},{2,3},{3,2},{4,5},{5,4},{6,7},{7,6},{8,9},{9,8},{10,11... | collective-permute-start | bytes 4718600 | tf_op jit(solution)/shard_map/ppermute | solution.py:114
  67.3 146.8 %copy-start.6 = (bf16[4,3072]{1,0:T(4,128)(2,1)}, bf16[4,3072]{1,0:T(4,128)(2,1)S(1)}, u32[]{:S(2)}) copy-start(bf16[4,3072]{1,0:T(4,128)(2,1)S(1)} %get-tuple-element.15) | copy-start | bytes 73732
  67.8 1.1 copy-start.4
  70.6 72.9 %copy-start.2 = (bf16[3072,256]{1,0:T(8,128)(2,1)S(1)}, bf16[3072,256]{1,0:T(8,128)(2,1)}, u32[]{:S(2)}) copy-start(bf16[3072,256]{1,0:T(8,128)(2,1)} %refs_3_.5) | copy-start | bytes 4718596
  100.0 43.5 %copy-start.3 = (bf16[256,3072]{1,0:T(8,128)(2,1)S(1)}, bf16[256,3072]{1,0:T(8,128)(2,1)}, u32[]{:S(2)}) copy-start(bf16[256,3072]{1,0:T(8,128)(2,1)} %refs_4_.3) | copy-start | bytes 4718596
  118.2 17.7 %collective-permute-start.5 = (bf16[4,128,768]{2,1,0:T(8,128)(2,1)S(1)}, bf16[4,128,768]{2,1,0:T(8,128)(2,1)S(1)}, u32[]{:S(2)}, u32[]{:S(2)}) collective-permute-start(bf16[4,128,768]{2,1,0:T(8,128)(2,1)S(1)} %all_gather.11.refs_0_), channel_id=1, source_target_pairs={{0,6},{2,0},{4,2},{6,4},{1,7},{3,1},{5,3},{7,5},{8,14},{10,8},{12,... | collective-permute-start | bytes 2359304 | tf_op jit(solution)/shard_map/ppermute | solution.py:141
  122.8 18.7 %collective-permute-start.3 = (bf16[4,128,768]{2,1,0:T(8,128)(2,1)S(1)}, bf16[4,128,768]{2,1,0:T(8,128)(2,1)S(1)}, u32[]{:S(2)}, u32[]{:S(2)}) collective-permute-start(bf16[4,128,768]{2,1,0:T(8,128)(2,1)S(1)} %all_gather.11.refs_0_), channel_id=1, source_target_pairs={{0,2},{2,4},{4,6},{6,0},{1,3},{3,5},{5,7},{7,1},{8,10},{10,12},{12... | collective-permute-start | bytes 2359304 | tf_op jit(solution)/shard_map/ppermute | solution.py:141
  135.9 20.7 %collective-permute-start.6 = (bf16[2,128,768]{2,1,0:T(8,128)(2,1)S(1)}, bf16[2,128,768]{2,1,0:T(8,128)(2,1)S(1)}, u32[]{:S(2)}, u32[]{:S(2)}) collective-permute-start(bf16[2,128,768]{2,1,0:T(8,128)(2,1)S(1)} %slice.9), channel_id=1, source_target_pairs={{0,6},{2,0},{4,2},{6,4},{1,7},{3,1},{5,3},{7,5},{8,14},{10,8},{12,... | collective-permute-start | bytes 1179656 | tf_op jit(solution)/shard_map/ppermute | solution.py:141
  141.6 15.0 %collective-permute-start.4 = (bf16[2,128,768]{2,1,0:T(8,128)(2,1)S(1)}, bf16[2,128,768]{2,1,0:T(8,128)(2,1)S(1)}, u32[]{:S(2)}, u32[]{:S(2)}) collective-permute-start(bf16[2,128,768]{2,1,0:T(8,128)(2,1)S(1)} %slice.8), channel_id=1, source_target_pairs={{0,2},{2,4},{4,6},{6,0},{1,3},{3,5},{5,7},{7,1},{8,10},{10,12},{12... | collective-permute-start | bytes 1179656 | tf_op jit(solution)/shard_map/ppermute | solution.py:141
  143.5 1.4 copy-start.5
  149.5 33.6 %collective-permute-start.8 = (bf16[4,128,768]{2,1,0:T(8,128)(2,1)S(1)}, bf16[4,128,768]{2,1,0:T(8,128)(2,1)S(1)}, u32[]{:S(2)}, u32[]{:S(2)}) collective-permute-start(bf16[4,128,768]{2,1,0:T(8,128)(2,1)S(1)} %get-tuple-element.12), channel_id=1, source_target_pairs={{0,6},{2,0},{4,2},{6,4},{1,7},{3,1},{5,3},{7,5},{8,14},{10,8},{12,... | collective-permute-start | bytes 2359304 | tf_op jit(solution)/shard_map/ppermute | solution.py:141
  154.7 33.8 %collective-permute-start.9 = (bf16[4,128,768]{2,1,0:T(8,128)(2,1)S(1)}, bf16[4,128,768]{2,1,0:T(8,128)(2,1)S(1)}, u32[]{:S(2)}, u32[]{:S(2)}) collective-permute-start(bf16[4,128,768]{2,1,0:T(8,128)(2,1)S(1)} %get-tuple-element.13), channel_id=1, source_target_pairs={{0,2},{2,4},{4,6},{6,0},{1,3},{3,5},{5,7},{7,1},{8,10},{10,12},{12... | collective-permute-start | bytes 2359304 | tf_op jit(solution)/shard_map/ppermute | solution.py:141
  160.0 28.4 %collective-permute-start.7 = (bf16[4,128,768]{2,1,0:T(8,128)(2,1)S(1)}, bf16[4,128,768]{2,1,0:T(8,128)(2,1)S(1)}, u32[]{:S(2)}, u32[]{:S(2)}) collective-permute-start(bf16[4,128,768]{2,1,0:T(8,128)(2,1)S(1)} %shard_map.105), channel_id=1, source_target_pairs={{0,4},{2,6},{4,0},{6,2},{1,5},{3,7},{5,1},{7,3},{8,12},{10,14},{12... | collective-permute-start | bytes 2359304 | tf_op jit(solution)/shard_map/ppermute | solution.py:141
  206.5 22.9 %all-to-all-start.3 = ((bf16[64,2,768]{2,1,0:T(2,128)(2,1)}), bf16[64,2,768]{2,1,0:T(2,128)(2,1)S(1)}, u32[]{:S(2)}, u32[]{:S(2)}) async-start(bf16[64,2,768]{2,1,0:T(2,128)(2,1)} %reshape.76), calls=%async_computation.3 | async-start | bytes 393216 | tf_op jit(solution)/shard_map/all_to_all | solution.py:31

commit v5 on v4

--- a/solution.py
+++ b/solution.py
@@ -31,16 +31,23 @@
     return lax.all_to_all(value, axes, split_axis=0, concat_axis=0, tiled=True)
 
 
-def attention_rows(context, out_weight):
-    tokens = lax.all_gather(context, "X", axis=0, tiled=True)
+def spread(value, axes, parts):
+    return swap(jnp.broadcast_to(value[None], (parts,) + value.shape), axes)
+
+
+def attention_rows(context, out_weight, weights):
+    tokens = spread(context, "X", 4).reshape(-1, context.shape[1])
     columns = lax.all_gather(out_weight.T, ("B", "I"), axis=0, tiled=True)
     partial_sum = lax.dot_general(
         tokens, columns, (((1,), (1,)), ((), ())), preferred_element_type=jnp.float32
     ).astype(jnp.bfloat16)
+    partial_sum, *weights = lax.optimization_barrier((partial_sum, *weights))
+    partner = tuple(lax.ppermute(w, "C", [(0, 1), (1, 0)]) for w in weights)
     width = columns.shape[0]
     pieces = swap(partial_sum.reshape(32, -1, width), ("X", "Y", "C"))
     pieces = pieces.reshape(4, 8, -1, width).astype(jnp.float32)
-    return jnp.transpose(jnp.sum(pieces, axis=1), (1, 0, 2)).reshape(-1, 4 * width)
+    summed = jnp.transpose(jnp.sum(pieces, axis=1), (1, 0, 2)).reshape(-1, 4 * width)
+    return summed, partner
 
 
 def expert_kernel(layout, *refs):
@@ -97,6 +104,10 @@
     )(*flat, *weights, *partner)
 
 
+def over_block(value):
+    return jnp.sum(swap(value, "I").astype(jnp.float32), axis=0)
+
+
 def on_device(
     context,
     out_weight,
@@ -111,8 +122,7 @@
     width = residual.shape[1]
     experts = router_weight.shape[1]
     weights = (gate_weight, up_weight, down_weight)
-    partner = tuple(lax.ppermute(w, "C", [(0, 1), (1, 0)]) for w in weights)
-    attention_sum = attention_rows(context, out_weight)
+    attention_sum, partner = attention_rows(context, out_weight, weights)
     hidden_state = (residual.astype(jnp.float32) + attention_sum).astype(jnp.bfloat16)
     normed = layer_norm(hidden_state, norm_gain)
     logits = jnp.dot(normed, router_weight, preferred_element_type=jnp.float32)
@@ -131,27 +141,30 @@
         assign.astype(jnp.bfloat16).T, normed, preferred_element_type=jnp.float32
     ).astype(jnp.bfloat16)
 
-    send_rows, partner = lax.optimization_barrier((send_rows, partner))
     quarter = width // 4
     outgoing = jnp.transpose(send_rows.reshape(experts, CAP, 4, quarter), (0, 2, 1, 3))
     landed = swap(outgoing.reshape(4 * experts, CAP, quarter), EXPERT)
+    landed, partner = lax.optimization_barrier((landed, partner))
     block_rows = lax.all_gather(landed.reshape(-1, quarter), "I")
 
     def turn(value, by):
         return lax.ppermute(value, "Y", [(i, (i + by) % 4) for i in range(4)])
 
-    below, above = turn(block_rows, 1), turn(block_rows, -1)
-    far = [turn(below[:2], 1), turn(above[2:], -1)]
-    near_below, near_above = both_cores([[below], [above]], weights, partner)
+    low, high = block_rows[:2], block_rows[2:]
+    below_low, above_high = turn(low, 1), turn(high, -1)
+    below_high, above_low = turn(high, 1), turn(low, -1)
+    far = [turn(below_low, 1), turn(above_high, -1)]
+    near_below, near_above = both_cores(
+        [[below_low, below_high], [above_low, above_high]], weights, partner
+    )
+    *far, near_below, near_above = lax.optimization_barrier((*far, near_below, near_above))
     to_below, to_above = turn(near_below, -1), turn(near_above, 1)
-    to_far = turn(both_cores([far], weights, partner)[0], 2)
+    far_block = over_block(both_cores([far], weights, partner)[0])
+    to_far = turn(far_block.astype(jnp.bfloat16), 2)
     own = both_cores([[block_rows]], weights, partner)[0]
-    over_y = own.astype(jnp.float32) + to_far.astype(jnp.float32)
-    over_y += to_below.astype(jnp.float32) + to_above.astype(jnp.float32)
-    over_y = over_y.astype(jnp.bfloat16)
-
-    over_block = jnp.sum(swap(over_y, "I").astype(jnp.float32), axis=0).astype(jnp.bfloat16)
-    back = swap(over_block.reshape(4 * experts, CAP, quarter), EXPERT)
+    near = own.astype(jnp.float32) + to_below.astype(jnp.float32) + to_above.astype(jnp.float32)
+    summed = over_block(near.astype(jnp.bfloat16)) + to_far.astype(jnp.float32)
+    back = swap(summed.astype(jnp.bfloat16).reshape(4 * experts, CAP, quarter), EXPERT)
     chosen = jnp.transpose(back.reshape(experts, 4, CAP, quarter), (0, 2, 1, 3))
     chosen = chosen.reshape(experts * CAP, width)
     cell_weight = jnp.sum(jnp.where(cells, route_weight[:, :, None], 0.0), axis=1)

time: 231 us -> 218 us (0.944)
  blocking collectives: 115 us -> 81.8 us
  starting transfers between devices: 45.7 us -> 73.1 us
  waiting for transfers between devices: 48.8 us -> 29.9 us
  local copies, waits for them, and re-layouts: 5.24 us -> 10.8 us
  other arithmetic: 1.86 us -> 5.28 us
    ppermute x7 -> x9, waiting for transfers between devices: 32.7 us -> 8.51 us  [turn(): return lax.ppermute(value, 'Y', [(i, (i + by) % 4) for i in range(4)])]
    all_to_all x2 -> x5, starting transfers between devices: 14.9 us -> 33.6 us  [swap(): return lax.all_to_all(value, axes, split_axis=0, concat_axis=0, tiled=True)]
    all_to_all x2 -> x1, blocking collectives: 45.5 us -> 29 us  [swap(): return lax.all_to_all(value, axes, split_axis=0, concat_axis=0, tiled=True)]
    all_gather x1 -> x0, blocking collectives: 15 us -> none  [attention_rows(): tokens = lax.all_gather(context, 'X', axis=0, tiled=True)]
    ppermute x7 -> x9, starting transfers between devices: 24.5 us -> 33.1 us  [turn(): return lax.ppermute(value, 'Y', [(i, (i + by) % 4) for i in range(4)])]
    all_to_all x2 -> x5, waiting for transfers between devices: 14.7 us -> 21.4 us  [swap(): return lax.all_to_all(value, axes, split_axis=0, concat_axis=0, tiled=True)]
    unnamed x21 -> x29, local copies, waits for them, and re-layouts: 2.59 us -> 6.63 us
  transfers between devices with their start and end apart: 12 -> 17, of which waited for: 5 -> 7; matrix products, arithmetic and copies ran while one was open for 1% -> 3% of each run, Pallas kernels for 5% -> 4%
where the time goes in v5:
time: 218 us; the launch traced here: 216 us
  blocking collectives  81.8 us (38%)
  starting transfers between devices  73.1 us (34%)
  waiting for transfers between devices  29.9 us (14%)
  Pallas kernels  12.8 us (6%)
  local copies, waits for them, and re-layouts  10.8 us (5%)
  other arithmetic  5.28 us (2%)
    all_gather x1, blocking collectives, attention_rows(): columns = lax.all_gather(out_weight.T, ('B', 'I'), axis=0, tiled=True)  34.7 us
    all_to_all x5, starting transfers between devices, swap(): return lax.all_to_all(value, axes, split_axis=0, concat_axis=0, tiled=True)  33.6 us
    ppermute x9, starting transfers between devices, turn(): return lax.ppermute(value, 'Y', [(i, (i + by) % 4) for i in range(4)])  33.1 us
    all_to_all x1, blocking collectives, swap(): return lax.all_to_all(value, axes, split_axis=0, concat_axis=0, tiled=True)  29 us
    all_to_all x5, waiting for transfers between devices, swap(): return lax.all_to_all(value, axes, split_axis=0, concat_axis=0, tiled=True)  21.4 us
    all_gather x1, blocking collectives, on_device(): block_rows = lax.all_gather(landed.reshape(-1, quarter), 'I')  18.1 us
    pallas_call x3, Pallas kernels, both_cores(): pl.pallas_call(functools.partial(expert_kernel, layout), out_shape=[jax.S...  12.8 us
    ppermute x9, waiting for transfers between devices, turn(): return lax.ppermute(value, 'Y', [(i, (i + by) % 4) for i in range(4)])  8.51 us
  transfers between devices with their start and end apart: 17, of which 7 were waited for; matrix products, arithmetic and copies ran while one was open for 3% of the time, Pallas kernels for 4%

profile of v5, /device:TPU:6, one launch (start us, length us, event | category | flops | bytes accessed | tf_op | source)
XLA Modules:
  0.0 216.3 jit_solution(13214093107572997744)
XLA Ops:
  0.6 0.0 copy-start
  0.6 0.0 copy-start.11
  0.7 1.5 broadcast_in_dim.22
  2.2 9.1 %all-to-all-start = ((bf16[4,32,384]{2,1,0:T(8,128)(2,1)}), bf16[4,32,384]{2,1,0:T(8,128)(2,1)S(1)}, u32[]{:S(2)}, u32[]{:S(2)}) async-start(bf16[4,32,384]{2,1,0:T(8,128)(2,1)} %broadcast_in_dim.22), calls=%async_computation | async-start | bytes 196608 | tf_op jit(solution)/shard_map/all_to_all | solution.py:31
  11.3 34.7 %all_gather.6 = bf16[768,384]{1,0:T(8,128)(2,1)S(1)} all-gather(bf16[48,384]{1,0:T(8,128)(2,1)} %bitcast.29), channel_id=1, replica_groups=mesh['X'=4,'B'=4,'I'=4,'Y'=4,'C'=2] {'B','I'}, dimensions={0}, use_global_device_ids=true | all-gather | bytes 626688 | tf_op jit(solution)/shard_map/all_gather | solution.py:40
  46.0 0.8 convert_reduce_fusion.3
  46.8 0.9 select_reduce_fusion.2
  47.7 0.3 convolution_convert_fusion.2
  48.1 0.7 reshape.77
  48.8 7.6 %all-to-all-start.1 = ((bf16[32,4,768]{2,1,0:T(4,128)(2,1)}), bf16[32,4,768]{2,1,0:T(4,128)(2,1)S(1)}, u32[]{:S(2)}, u32[]{:S(2)}) async-start(bf16[32,4,768]{2,1,0:T(4,128)(2,1)} %reshape.77), calls=%async_computation.1 | async-start | bytes 393216 | tf_op jit(solution)/shard_map/all_to_all | solution.py:31
  56.5 0.1 fusion.5
  56.6 2.1 collective-permute-start
  58.6 2.3 %collective-permute-start.1 = (bf16[3072,256]{1,0:T(8,128)(2,1)}, bf16[3072,256]{1,0:T(8,128)(2,1)}, u32[]{:S(2)}, u32[]{:S(2)}) collective-permute-start(bf16[3072,256]{1,0:T(8,128)(2,1)} %refs_3_.3), channel_id=1, source_target_pairs={{0,1},{1,0},{2,3},{3,2},{4,5},{5,4},{6,7},{7,6},{8,9},{9,8},{10,11... | collective-permute-start | bytes 4718600 | tf_op jit(solution)/shard_map/ppermute | solution.py:45
  60.9 2.1 collective-permute-start.2
  63.0 0.1 convert_reduce_fusion.1
  63.1 0.1 convert_reduce_fusion.2
  63.3 0.2 fusion.2
  63.5 0.3 convolution_convert_fusion
  63.7 0.1 reshape.79
  63.9 0.2 copy.18
  64.0 29.0 %all_to_all.30 = bf16[64,2,768]{2,1,0:T(2,128)(2,1)S(1)} all-to-all(bf16[64,2,768]{2,1,0:T(2,128)(2,1)S(1)} %bitcast.25), channel_id=1, replica_groups=mesh['X'=4,'B'=4,'I'=4,'Y'=4,'C'=2] {'X','B','I'}, dimensions={0} | all-to-all | bytes 393216 | tf_op jit(solution)/shard_map/all_to_all | solution.py:31
  93.1 0.7 all_gather_reshape.3
  93.8 18.1 %all_gather.7.refs_0_ = bf16[4,128,768]{2,1,0:T(8,128)(2,1)S(1)} all-gather(bf16[1,128,768]{2,1,0:T(8,128)(2,1)} %all_gather_reshape.3), channel_id=1, replica_groups=mesh['X'=4,'B'=4,'I'=4,'Y'=4,'C'=2] {'I'}, dimensions={0}, use_global_device_ids=true | all-gather | bytes 983040 | tf_op jit(solution)/shard_map/all_gather | solution.py:148
  111.9 0.1 fusion.9
  112.0 3.4 %collective-permute-start.3 = (bf16[2,128,768]{2,1,0:T(8,128)(2,1)S(1)}, bf16[2,128,768]{2,1,0:T(8,128)(2,1)S(1)}, u32[]{:S(2)}, u32[]{:S(2)}) collective-permute-start(bf16[2,128,768]{2,1,0:T(8,128)(2,1)S(1)} %get-tuple-element.33), channel_id=1, source_target_pairs={{0,2},{2,4},{4,6},{6,0},{1,3},{3,5},{5,7},{7,1},{8,10},{10,12},{12... | collective-permute-start | bytes 1179656 | tf_op jit(solution)/shard_map/ppermute | solution.py:151
  115.3 3.7 %collective-permute-start.5 = (bf16[2,128,768]{2,1,0:T(8,128)(2,1)S(1)}, bf16[2,128,768]{2,1,0:T(8,128)(2,1)S(1)}, u32[]{:S(2)}, u32[]{:S(2)}) collective-permute-start(bf16[2,128,768]{2,1,0:T(8,128)(2,1)S(1)} %get-tuple-element.32), channel_id=1, source_target_pairs={{0,6},{2,0},{4,2},{6,4},{1,7},{3,1},{5,3},{7,5},{8,14},{10,8},{12,... | collective-permute-start | bytes 1179656 | tf_op jit(solution)/shard_map/ppermute | solution.py:151
  119.0 2.2 collective-permute-start.7
  121.2 4.9 %collective-permute-start.8 = (bf16[2,128,768]{2,1,0:T(8,128)(2,1)S(1)}, bf16[2,128,768]{2,1,0:T(8,128)(2,1)S(1)}, u32[]{:S(2)}, u32[]{:S(2)}) collective-permute-start(bf16[2,128,768]{2,1,0:T(8,128)(2,1)S(1)} %get-tuple-element.33), channel_id=1, source_target_pairs={{0,6},{2,0},{4,2},{6,4},{1,7},{3,1},{5,3},{7,5},{8,14},{10,8},{12,... | collective-permute-start | bytes 1179656 | tf_op jit(solution)/shard_map/ppermute | solution.py:151
  126.1 2.7 %collective-permute-start.4 = (bf16[2,128,768]{2,1,0:T(8,128)(2,1)S(1)}, bf16[2,128,768]{2,1,0:T(8,128)(2,1)S(1)}, u32[]{:S(2)}, u32[]{:S(2)}) collective-permute-start(bf16[2,128,768]{2,1,0:T(8,128)(2,1)S(1)} %collective-permute-done.3.refs_0_), channel_id=1, source_target_pairs={{0,2},{2,4},{4,6},{6,0},{1,3},{3,5},{5,7},{7,1},{8,10},{10,12},{12... | collective-permute-start | bytes 1179656 | tf_op jit(solution)/shard_map/ppermute | solution.py:151
  128.8 0.2 collective-permute-done.5.refs_3_
  129.0 4.2 %collective-permute-start.6 = (bf16[2,128,768]{2,1,0:T(8,128)(2,1)S(1)}, bf16[2,128,768]{2,1,0:T(8,128)(2,1)S(1)}, u32[]{:S(2)}, u32[]{:S(2)}) collective-permute-start(bf16[2,128,768]{2,1,0:T(8,128)(2,1)S(1)} %collective-permute-done.5.refs_3_), channel_id=1, source_target_pairs={{0,6},{2,0},{4,2},{6,4},{1,7},{3,1},{5,3},{7,5},{8,14},{10,8},{12,... | collective-permute-start | bytes 1179656 | tf_op jit(solution)/shard_map/ppermute | solution.py:151
  133.2 1.0 collective-permute-done.7.refs_1_
  134.2 3.3 %collective-permute-done.8.refs_2_ = bf16[2,128,768]{2,1,0:T(8,128)(2,1)S(1)} collective-permute-done((bf16[2,128,768]{2,1,0:T(8,128)(2,1)S(1)}, bf16[2,128,768]{2,1,0:T(8,128)(2,1)S(1)}, u32[]{:S(2)}, u32[]{:S(2)}) %collective-permute-start.8) | collective-permute-done | bytes 393248 | tf_op jit(solution)/shard_map/ppermute | solution.py:151
  137.4 1.4 copy-done.3
  138.9 5.0 %shard_map.105 = (bf16[4,128,768]{2,1,0:T(8,128)(2,1)S(1)}, bf16[4,128,768]{2,1,0:T(8,128)(2,1)S(1)}) custom-call(bf16[2,128,768]{2,1,0:T(8,128)(2,1)S(1)} %collective-permute-done.3.refs_0_, bf16[2,128,768]{2,1,0:T(8,128)(2,1)S(1)} %collective-permute-done.7.refs_1_, bf16[2,128,768]{2,1,0:T(8,128)(2,1)S(1)} %collective-permute-done.8.refs_2_, ...), custom_call_target="tpu_custom_call" | custom-call | flops 2415919104 | bytes 12582912 | tf_op jit(solution)/shard_map/pallas_call | solution.py:92
  143.9 0.9 copy-done.8
  144.8 0.9 copy-done.9
  145.7 3.9 %shard_map.106 = bf16[4,128,768]{2,1,0:T(8,128)(2,1)S(1)} custom-call(bf16[2,128,768]{2,1,0:T(8,128)(2,1)S(1)} %collective-permute-done.4.refs_0_, bf16[2,128,768]{2,1,0:T(8,128)(2,1)S(1)} %collective-permute-done.6.refs_1_, bf16[3072,256]{1,0:T(8,128)(2,1)S(1)} %copy-done.1, bf16[3072,256]{1,0:T(8,128)(2,1)S(1)} %copy-done.2, ...), custom_call_target="tpu_custom_call" | custom-call | flops 1207959552 | bytes 11010048 | tf_op jit(solution)/shard_map/pallas_call | solution.py:92
  149.6 0.9 copy-done.7
  150.4 4.2 %all-to-all-start.4 = ((bf16[4,128,768]{2,1,0:T(8,128)(2,1)}), bf16[4,128,768]{2,1,0:T(8,128)(2,1)}, u32[]{:S(2)}, u32[]{:S(2)}) async-start(bf16[4,128,768]{2,1,0:T(8,128)(2,1)} %copy-done.7), calls=%async_computation.4 | async-start | bytes 1572864 | tf_op jit(solution)/shard_map/all_to_all | solution.py:31
  154.6 3.4 %collective-permute-start.10 = (bf16[4,128,768]{2,1,0:T(8,128)(2,1)}, bf16[4,128,768]{2,1,0:T(8,128)(2,1)S(1)}, u32[]{:S(2)}, u32[]{:S(2)}) collective-permute-start(bf16[4,128,768]{2,1,0:T(8,128)(2,1)} %copy-done.9), channel_id=1, source_target_pairs={{0,2},{2,4},{4,6},{6,0},{1,3},{3,5},{5,7},{7,1},{8,10},{10,12},{12... | collective-permute-start | bytes 2359304 | tf_op jit(solution)/shard_map/ppermute | solution.py:151
  158.1 3.6 %collective-permute-start.9 = (bf16[4,128,768]{2,1,0:T(8,128)(2,1)}, bf16[4,128,768]{2,1,0:T(8,128)(2,1)S(1)}, u32[]{:S(2)}, u32[]{:S(2)}) collective-permute-start(bf16[4,128,768]{2,1,0:T(8,128)(2,1)} %copy-done.8), channel_id=1, source_target_pairs={{0,6},{2,0},{4,2},{6,4},{1,7},{3,1},{5,3},{7,5},{8,14},{10,8},{12,... | collective-permute-start | bytes 2359304 | tf_op jit(solution)/shard_map/ppermute | solution.py:151
  161.7 0.0 copy-start.4
  161.7 1.4 copy-done.4
  163.1 1.1 copy-done.6
  164.2 3.9 %shard_map.104 = bf16[4,128,768]{2,1,0:T(8,128)(2,1)S(1)} custom-call(bf16[4,128,768]{2,1,0:T(8,128)(2,1)S(1)} %copy-done.6, bf16[3072,256]{1,0:T(8,128)(2,1)S(1)} %copy-done.1, bf16[3072,256]{1,0:T(8,128)(2,1)S(1)} %copy-done.2, bf16[256,3072]{1,0:T(8,128)(2,1)S(1)} %copy-done.4, bf16[3072,256]{1,0:T(8,128)(2,1)} %collective-permute-done.refs_4_.refs_7_.refs_5_, ...), custom_call_target="tpu_custom_call" | custom-call | flops 1207959552 | bytes 11010048 | tf_op jit(solution)/shard_map/pallas_call | solution.py:92
  168.1 2.7 %collective-permute-done.10 = bf16[4,128,768]{2,1,0:T(8,128)(2,1)S(1)} collective-permute-done((bf16[4,128,768]{2,1,0:T(8,128)(2,1)}, bf16[4,128,768]{2,1,0:T(8,128)(2,1)S(1)}, u32[]{:S(2)}, u32[]{:S(2)}) %collective-permute-start.10) | collective-permute-done | bytes 786464 | tf_op jit(solution)/shard_map/ppermute | solution.py:151
  170.8 1.4 collective-permute-done.9
  172.2 1.2 add_convert_fusion
  173.3 5.0 %all-to-all-start.3 = ((bf16[4,128,768]{2,1,0:T(8,128)(2,1)}), bf16[4,128,768]{2,1,0:T(8,128)(2,1)S(1)}, u32[]{:S(2)}, u32[]{:S(2)}) async-start(bf16[4,128,768]{2,1,0:T(8,128)(2,1)} %add_convert_fusion), calls=%async_computation.3 | async-start | bytes 1572864 | tf_op jit(solution)/shard_map/all_to_all | solution.py:31
  178.4 1.3 reduce_sum.102
  179.6 5.1 %collective-permute-start.11 = (bf16[128,768]{1,0:T(8,128)(2,1)S(1)}, bf16[128,768]{1,0:T(8,128)(2,1)S(1)}, u32[]{:S(2)}, u32[]{:S(2)}) collective-permute-start(bf16[128,768]{1,0:T(8,128)(2,1)S(1)} %reduce_sum.102), channel_id=1, source_target_pairs={{0,4},{2,6},{4,0},{6,2},{1,5},{3,7},{5,1},{7,3},{8,12},{10,14},{12... | collective-permute-start | bytes 589832 | tf_op jit(solution)/shard_map/ppermute | solution.py:151
  184.7 6.7 %all-to-all-done.3 = bf16[4,128,768]{2,1,0:T(8,128)(2,1)S(1)} async-done(((bf16[4,128,768]{2,1,0:T(8,128)(2,1)}), bf16[4,128,768]{2,1,0:T(8,128)(2,1)S(1)}, u32[]{:S(2)}, u32[]{:S(2)}) %all-to-all-start.3) | async-done | bytes 786464 | tf_op jit(solution)/shard_map/all_to_all | solution.py:31
  191.5 0.1 convert_reduce_fusion
  191.6 0.7 reshape.81
  192.4 7.6 %all-to-all-start.5 = ((bf16[64,2,768]{2,1,0:T(2,128)(2,1)}), bf16[64,2,768]{2,1,0:T(2,128)(2,1)S(1)}, u32[]{:S(2)}, u32[]{:S(2)}) async-start(bf16[64,2,768]{2,1,0:T(2,128)(2,1)} %reshape.81), calls=%async_computation.5 | async-start | bytes 393216 | tf_op jit(solution)/shard_map/all_to_all | solution.py:31
  200.0 0.2 fusion.7
  200.2 0.2 select_reduce_fusion.1
  200.4 0.1 exponential_reduce_fusion
  200.5 0.1 exponential_divide_fusion
  200.6 0.1 select_reduce_fusion
  200.7 14.7 %all-to-all-done.5 = bf16[64,2,768]{2,1,0:T(2,128)(2,1)S(1)} async-done(((bf16[64,2,768]{2,1,0:T(2,128)(2,1)}), bf16[64,2,768]{2,1,0:T(2,128)(2,1)S(1)}, u32[]{:S(2)}, u32[]{:S(2)}) %all-to-all-start.5) | async-done | bytes 196640 | tf_op jit(solution)/shard_map/all_to_all | solution.py:31
  215.3 0.1 copy.19
  215.5 0.8 convolution_convert_fusion.1
  (37 shorter events, 0.2 us)
Async XLA Ops:
  0.6 199.4 %copy-start = (bf16[3072,16]{0,1:T(8,128)(2,1)S(1)}, bf16[3072,16]{0,1:T(8,128)(2,1)}, u32[]{:S(2)}) copy-start(bf16[3072,16]{0,1:T(8,128)(2,1)} %param.13) | copy-start | bytes 294916
  0.6 55.8 %copy-start.11 = (s32[4,4]{1,0:T(4,128)S(1)}, s32[4,4]{1,0:T(4,128)}, u32[]{:S(2)}) copy-start(s32[4,4]{1,0:T(4,128)} %param.17) | copy-start | bytes 196
  0.7 55.9 %copy-start.1 = (bf16[3072,256]{1,0:T(8,128)(2,1)S(1)}, bf16[3072,256]{1,0:T(8,128)(2,1)}, u32[]{:S(2)}) copy-start(bf16[3072,256]{1,0:T(8,128)(2,1)} %refs_2_.3) | copy-start | bytes 4718596
  0.7 55.8 %copy-start.13 = (bf16[3072]{0:T(1024)(128)(2,1)S(1)}, bf16[3072]{0:T(1024)(128)(2,1)}, u32[]{:S(2)}) copy-start(bf16[3072]{0:T(1024)(128)(2,1)} %param.12) | copy-start | bytes 18436
  0.7 62.4 %copy-start.12 = (bf16[4,3072]{1,0:T(4,128)(2,1)S(1)}, bf16[4,3072]{1,0:T(4,128)(2,1)}, u32[]{:S(2)}) copy-start(bf16[4,3072]{1,0:T(4,128)(2,1)} %param.11) | copy-start | bytes 73732
  2.2 45.6 %all-to-all-start = ((bf16[4,32,384]{2,1,0:T(8,128)(2,1)}), bf16[4,32,384]{2,1,0:T(8,128)(2,1)S(1)}, u32[]{:S(2)}, u32[]{:S(2)}) async-start(bf16[4,32,384]{2,1,0:T(8,128)(2,1)} %broadcast_in_dim.22), calls=%async_computation | async-start | bytes 196608 | tf_op jit(solution)/shard_map/all_to_all | solution.py:31
  48.8 14.2 %all-to-all-start.1 = ((bf16[32,4,768]{2,1,0:T(4,128)(2,1)}), bf16[32,4,768]{2,1,0:T(4,128)(2,1)S(1)}, u32[]{:S(2)}, u32[]{:S(2)}) async-start(bf16[32,4,768]{2,1,0:T(4,128)(2,1)} %reshape.77), calls=%async_computation.1 | async-start | bytes 393216 | tf_op jit(solution)/shard_map/all_to_all | solution.py:31
  56.6 36.5 %collective-permute-start = (bf16[3072,256]{1,0:T(8,128)(2,1)S(1)}, bf16[3072,256]{1,0:T(8,128)(2,1)}, u32[]{:S(2)}, u32[]{:S(2)}) collective-permute-start(bf16[3072,256]{1,0:T(8,128)(2,1)S(1)} %copy-done.1), channel_id=1, source_target_pairs={{0,1},{1,0},{2,3},{3,2},{4,5},{5,4},{6,7},{7,6},{8,9},{9,8},{10,11... | collective-permute-start | bytes 4718600 | tf_op jit(solution)/shard_map/ppermute | solution.py:45
  58.6 34.4 %collective-permute-start.1 = (bf16[3072,256]{1,0:T(8,128)(2,1)}, bf16[3072,256]{1,0:T(8,128)(2,1)}, u32[]{:S(2)}, u32[]{:S(2)}) collective-permute-start(bf16[3072,256]{1,0:T(8,128)(2,1)} %refs_3_.3), channel_id=1, source_target_pairs={{0,1},{1,0},{2,3},{3,2},{4,5},{5,4},{6,7},{7,6},{8,9},{9,8},{10,11... | collective-permute-start | bytes 4718600 | tf_op jit(solution)/shard_map/ppermute | solution.py:45
  60.9 32.1 %collective-permute-start.2 = (bf16[256,3072]{1,0:T(8,128)(2,1)}, bf16[256,3072]{1,0:T(8,128)(2,1)}, u32[]{:S(2)}, u32[]{:S(2)}) collective-permute-start(bf16[256,3072]{1,0:T(8,128)(2,1)} %refs_4_.3), channel_id=1, source_target_pairs={{0,1},{1,0},{2,3},{3,2},{4,5},{5,4},{6,7},{7,6},{8,9},{9,8},{10,11... | collective-permute-start | bytes 4718600 | tf_op jit(solution)/shard_map/ppermute | solution.py:45
  63.2 136.8 %copy-start.10 = (bf16[4,3072]{1,0:T(4,128)(2,1)}, bf16[4,3072]{1,0:T(4,128)(2,1)S(1)}, u32[]{:S(2)}) copy-start(bf16[4,3072]{1,0:T(4,128)(2,1)S(1)} %get-tuple-element.31) | copy-start | bytes 73732
  93.0 44.4 %copy-start.2 = (bf16[3072,256]{1,0:T(8,128)(2,1)S(1)}, bf16[3072,256]{1,0:T(8,128)(2,1)}, u32[]{:S(2)}) copy-start(bf16[3072,256]{1,0:T(8,128)(2,1)} %refs_3_.3) | copy-start | bytes 4718596
  111.9 22.3 %copy-start.5 = (bf16[4,128,768]{2,1,0:T(8,128)(2,1)}, bf16[4,128,768]{2,1,0:T(8,128)(2,1)S(1)}, u32[]{:S(2)}) copy-start(bf16[4,128,768]{2,1,0:T(8,128)(2,1)S(1)} %all_gather.7.refs_0_) | copy-start | bytes 2359300
  112.0 14.1 %collective-permute-start.3 = (bf16[2,128,768]{2,1,0:T(8,128)(2,1)S(1)}, bf16[2,128,768]{2,1,0:T(8,128)(2,1)S(1)}, u32[]{:S(2)}, u32[]{:S(2)}) collective-permute-start(bf16[2,128,768]{2,1,0:T(8,128)(2,1)S(1)} %get-tuple-element.33), channel_id=1, source_target_pairs={{0,2},{2,4},{4,6},{6,0},{1,3},{3,5},{5,7},{7,1},{8,10},{10,12},{12... | collective-permute-start | bytes 1179656 | tf_op jit(solution)/shard_map/ppermute | solution.py:151
  115.3 13.7 %collective-permute-start.5 = (bf16[2,128,768]{2,1,0:T(8,128)(2,1)S(1)}, bf16[2,128,768]{2,1,0:T(8,128)(2,1)S(1)}, u32[]{:S(2)}, u32[]{:S(2)}) collective-permute-start(bf16[2,128,768]{2,1,0:T(8,128)(2,1)S(1)} %get-tuple-element.32), channel_id=1, source_target_pairs={{0,6},{2,0},{4,2},{6,4},{1,7},{3,1},{5,3},{7,5},{8,14},{10,8},{12,... | collective-permute-start | bytes 1179656 | tf_op jit(solution)/shard_map/ppermute | solution.py:151
  119.0 15.2 %collective-permute-start.7 = (bf16[2,128,768]{2,1,0:T(8,128)(2,1)S(1)}, bf16[2,128,768]{2,1,0:T(8,128)(2,1)S(1)}, u32[]{:S(2)}, u32[]{:S(2)}) collective-permute-start(bf16[2,128,768]{2,1,0:T(8,128)(2,1)S(1)} %get-tuple-element.32), channel_id=1, source_target_pairs={{0,2},{2,4},{4,6},{6,0},{1,3},{3,5},{5,7},{7,1},{8,10},{10,12},{12... | collective-permute-start | bytes 1179656 | tf_op jit(solution)/shard_map/ppermute | solution.py:151
  121.2 16.2 %collective-permute-start.8 = (bf16[2,128,768]{2,1,0:T(8,128)(2,1)S(1)}, bf16[2,128,768]{2,1,0:T(8,128)(2,1)S(1)}, u32[]{:S(2)}, u32[]{:S(2)}) collective-permute-start(bf16[2,128,768]{2,1,0:T(8,128)(2,1)S(1)} %get-tuple-element.33), channel_id=1, source_target_pairs={{0,6},{2,0},{4,2},{6,4},{1,7},{3,1},{5,3},{7,5},{8,14},{10,8},{12,... | collective-permute-start | bytes 1179656 | tf_op jit(solution)/shard_map/ppermute | solution.py:151
  126.1 19.6 %collective-permute-start.4 = (bf16[2,128,768]{2,1,0:T(8,128)(2,1)S(1)}, bf16[2,128,768]{2,1,0:T(8,128)(2,1)S(1)}, u32[]{:S(2)}, u32[]{:S(2)}) collective-permute-start(bf16[2,128,768]{2,1,0:T(8,128)(2,1)S(1)} %collective-permute-done.3.refs_0_), channel_id=1, source_target_pairs={{0,2},{2,4},{4,6},{6,0},{1,3},{3,5},{5,7},{7,1},{8,10},{10,12},{12... | collective-permute-start | bytes 1179656 | tf_op jit(solution)/shard_map/ppermute | solution.py:151
  129.0 16.7 %collective-permute-start.6 = (bf16[2,128,768]{2,1,0:T(8,128)(2,1)S(1)}, bf16[2,128,768]{2,1,0:T(8,128)(2,1)S(1)}, u32[]{:S(2)}, u32[]{:S(2)}) collective-permute-start(bf16[2,128,768]{2,1,0:T(8,128)(2,1)S(1)} %collective-permute-done.5.refs_3_), channel_id=1, source_target_pairs={{0,6},{2,0},{4,2},{6,4},{1,7},{3,1},{5,3},{7,5},{8,14},{10,8},{12,... | collective-permute-start | bytes 1179656 | tf_op jit(solution)/shard_map/ppermute | solution.py:151
  137.4 1.4 copy-start.3
  143.9 0.9 copy-start.8
  144.8 0.9 copy-start.9
  149.6 0.9 copy-start.7
  150.4 22.9 %all-to-all-start.4 = ((bf16[4,128,768]{2,1,0:T(8,128)(2,1)}), bf16[4,128,768]{2,1,0:T(8,128)(2,1)}, u32[]{:S(2)}, u32[]{:S(2)}) async-start(bf16[4,128,768]{2,1,0:T(8,128)(2,1)} %copy-done.7), calls=%async_computation.4 | async-start | bytes 1572864 | tf_op jit(solution)/shard_map/all_to_all | solution.py:31
  154.6 16.2 %collective-permute-start.10 = (bf16[4,128,768]{2,1,0:T(8,128)(2,1)}, bf16[4,128,768]{2,1,0:T(8,128)(2,1)S(1)}, u32[]{:S(2)}, u32[]{:S(2)}) collective-permute-start(bf16[4,128,768]{2,1,0:T(8,128)(2,1)} %copy-done.9), channel_id=1, source_target_pairs={{0,2},{2,4},{4,6},{6,0},{1,3},{3,5},{5,7},{7,1},{8,10},{10,12},{12... | collective-permute-start | bytes 2359304 | tf_op jit(solution)/shard_map/ppermute | solution.py:151
  158.1 14.1 %collective-permute-start.9 = (bf16[4,128,768]{2,1,0:T(8,128)(2,1)}, bf16[4,128,768]{2,1,0:T(8,128)(2,1)S(1)}, u32[]{:S(2)}, u32[]{:S(2)}) collective-permute-start(bf16[4,128,768]{2,1,0:T(8,128)(2,1)} %copy-done.8), channel_id=1, source_target_pairs={{0,6},{2,0},{4,2},{6,4},{1,7},{3,1},{5,3},{7,5},{8,14},{10,8},{12,... | collective-permute-start | bytes 2359304 | tf_op jit(solution)/shard_map/ppermute | solution.py:151
  161.7 1.4 copy-start.4
  163.1 1.1 copy-start.6
  173.3 18.1 %all-to-all-start.3 = ((bf16[4,128,768]{2,1,0:T(8,128)(2,1)}), bf16[4,128,768]{2,1,0:T(8,128)(2,1)S(1)}, u32[]{:S(2)}, u32[]{:S(2)}) async-start(bf16[4,128,768]{2,1,0:T(8,128)(2,1)} %add_convert_fusion), calls=%async_computation.3 | async-start | bytes 1572864 | tf_op jit(solution)/shard_map/all_to_all | solution.py:31
  179.6 11.9 %collective-permute-start.11 = (bf16[128,768]{1,0:T(8,128)(2,1)S(1)}, bf16[128,768]{1,0:T(8,128)(2,1)S(1)}, u32[]{:S(2)}, u32[]{:S(2)}) collective-permute-start(bf16[128,768]{1,0:T(8,128)(2,1)S(1)} %reduce_sum.102), channel_id=1, source_target_pairs={{0,4},{2,6},{4,0},{6,2},{1,5},{3,7},{5,1},{7,3},{8,12},{10,14},{12... | collective-permute-start | bytes 589832 | tf_op jit(solution)/shard_map/ppermute | solution.py:151
  192.4 23.0 %all-to-all-start.5 = ((bf16[64,2,768]{2,1,0:T(2,128)(2,1)}), bf16[64,2,768]{2,1,0:T(2,128)(2,1)S(1)}, u32[]{:S(2)}, u32[]{:S(2)}) async-start(bf16[64,2,768]{2,1,0:T(2,128)(2,1)} %reshape.81), calls=%async_computation.5 | async-start | bytes 393216 | tf_op jit(solution)/shard_map/all_to_all | solution.py:31

commit v6 on v5

--- a/solution.py
+++ b/solution.py
@@ -35,19 +35,19 @@
     return swap(jnp.broadcast_to(value[None], (parts,) + value.shape), axes)
 
 
-def attention_rows(context, out_weight, weights):
+def attention_rows(context, out_weight, weights, later):
     tokens = spread(context, "X", 4).reshape(-1, context.shape[1])
     columns = lax.all_gather(out_weight.T, ("B", "I"), axis=0, tiled=True)
     partial_sum = lax.dot_general(
         tokens, columns, (((1,), (1,)), ((), ())), preferred_element_type=jnp.float32
     ).astype(jnp.bfloat16)
-    partial_sum, *weights = lax.optimization_barrier((partial_sum, *weights))
+    partial_sum, weights, later = lax.optimization_barrier((partial_sum, weights, later))
     partner = tuple(lax.ppermute(w, "C", [(0, 1), (1, 0)]) for w in weights)
     width = columns.shape[0]
     pieces = swap(partial_sum.reshape(32, -1, width), ("X", "Y", "C"))
     pieces = pieces.reshape(4, 8, -1, width).astype(jnp.float32)
     summed = jnp.transpose(jnp.sum(pieces, axis=1), (1, 0, 2)).reshape(-1, 4 * width)
-    return summed, partner
+    return summed, partner, later
 
 
 def expert_kernel(layout, *refs):
@@ -122,7 +122,9 @@
     width = residual.shape[1]
     experts = router_weight.shape[1]
     weights = (gate_weight, up_weight, down_weight)
-    attention_sum, partner = attention_rows(context, out_weight, weights)
+    attention_sum, partner, (expert_ids, norm_gain) = attention_rows(
+        context, out_weight, weights, (expert_ids, norm_gain)
+    )
     hidden_state = (residual.astype(jnp.float32) + attention_sum).astype(jnp.bfloat16)
     normed = layer_norm(hidden_state, norm_gain)
     logits = jnp.dot(normed, router_weight, preferred_element_type=jnp.float32)

time: 218 us -> 217 us (level)
  transfers between devices with their start and end apart: 17 -> 17, of which waited for: 7 -> 7; matrix products, arithmetic and copies ran while one was open for 3% -> 2% of each run, Pallas kernels for 4% -> 4%
where the time goes in v6:
time: 217 us; the launch traced here: 215 us
  blocking collectives  81.8 us (38%)
  starting transfers between devices  73.1 us (34%)
  waiting for transfers between devices  29.9 us (14%)
  Pallas kernels  12.8 us (6%)
  local copies, waits for them, and re-layouts  10.8 us (5%)
  other arithmetic  3.92 us (2%)
    all_gather x1, blocking collectives, attention_rows(): columns = lax.all_gather(out_weight.T, ('B', 'I'), axis=0, tiled=True)  34.7 us
    all_to_all x5, starting transfers between devices, swap(): return lax.all_to_all(value, axes, split_axis=0, concat_axis=0, tiled=True)  33.6 us
    ppermute x9, starting transfers between devices, turn(): return lax.ppermute(value, 'Y', [(i, (i + by) % 4) for i in range(4)])  33.1 us
    all_to_all x1, blocking collectives, swap(): return lax.all_to_all(value, axes, split_axis=0, concat_axis=0, tiled=True)  29 us
    all_to_all x5, waiting for transfers between devices, swap(): return lax.all_to_all(value, axes, split_axis=0, concat_axis=0, tiled=True)  21.4 us
    all_gather x1, blocking collectives, on_device(): block_rows = lax.all_gather(landed.reshape(-1, quarter), 'I')  18.1 us
    pallas_call x3, Pallas kernels, both_cores(): pl.pallas_call(functools.partial(expert_kernel, layout), out_shape=[jax.S...  12.8 us
    ppermute x9, waiting for transfers between devices, turn(): return lax.ppermute(value, 'Y', [(i, (i + by) % 4) for i in range(4)])  8.51 us
  transfers between devices with their start and end apart: 17, of which 7 were waited for; matrix products, arithmetic and copies ran while one was open for 2% of the time, Pallas kernels for 4%

profile of v6, /device:TPU:6, one launch (start us, length us, event | category | flops | bytes accessed | tf_op | source)
XLA Modules:
  0.0 214.9 jit_solution(15048496227966656135)
XLA Ops:
  0.6 0.0 copy-start
  0.7 1.5 broadcast_in_dim.22
  2.2 9.1 %all-to-all-start = ((bf16[4,32,384]{2,1,0:T(8,128)(2,1)}), bf16[4,32,384]{2,1,0:T(8,128)(2,1)S(1)}, u32[]{:S(2)}, u32[]{:S(2)}) async-start(bf16[4,32,384]{2,1,0:T(8,128)(2,1)} %broadcast_in_dim.22), calls=%async_computation | async-start | bytes 196608 | tf_op jit(solution)/shard_map/all_to_all | solution.py:31
  11.3 34.7 %all_gather.6 = bf16[768,384]{1,0:T(8,128)(2,1)S(1)} all-gather(bf16[48,384]{1,0:T(8,128)(2,1)} %bitcast.29), channel_id=1, replica_groups=mesh['X'=4,'B'=4,'I'=4,'Y'=4,'C'=2] {'B','I'}, dimensions={0}, use_global_device_ids=true | all-gather | bytes 626688 | tf_op jit(solution)/shard_map/all_gather | solution.py:40
  46.0 0.0 all-to-all-done
  46.0 0.3 convolution_convert_fusion.2
  46.4 0.1 convert_reduce_fusion.3
  46.5 0.2 select_reduce_fusion.2
  46.7 0.7 reshape.77
  47.4 7.6 %all-to-all-start.1 = ((bf16[32,4,768]{2,1,0:T(4,128)(2,1)}), bf16[32,4,768]{2,1,0:T(4,128)(2,1)S(1)}, u32[]{:S(2)}, u32[]{:S(2)}) async-start(bf16[32,4,768]{2,1,0:T(4,128)(2,1)} %reshape.77), calls=%async_computation.1 | async-start | bytes 393216 | tf_op jit(solution)/shard_map/all_to_all | solution.py:31
  55.1 2.1 collective-permute-start
  57.2 2.3 %collective-permute-start.1 = (bf16[3072,256]{1,0:T(8,128)(2,1)}, bf16[3072,256]{1,0:T(8,128)(2,1)}, u32[]{:S(2)}, u32[]{:S(2)}) collective-permute-start(bf16[3072,256]{1,0:T(8,128)(2,1)} %refs_3_.3), channel_id=1, source_target_pairs={{0,1},{1,0},{2,3},{3,2},{4,5},{5,4},{6,7},{7,6},{8,9},{9,8},{10,11... | collective-permute-start | bytes 4718600 | tf_op jit(solution)/shard_map/ppermute | solution.py:45
  59.5 2.1 collective-permute-start.2
  61.5 0.1 fusion.5
  61.6 0.1 convert_reduce_fusion.1
  61.7 0.1 convert_reduce_fusion.2
  61.9 0.2 fusion.2
  62.1 0.3 convolution_convert_fusion
  62.4 0.1 reshape.79
  62.5 0.2 copy.18
  62.7 29.0 %all_to_all.30 = bf16[64,2,768]{2,1,0:T(2,128)(2,1)S(1)} all-to-all(bf16[64,2,768]{2,1,0:T(2,128)(2,1)S(1)} %bitcast.25), channel_id=1, replica_groups=mesh['X'=4,'B'=4,'I'=4,'Y'=4,'C'=2] {'X','B','I'}, dimensions={0} | all-to-all | bytes 393216 | tf_op jit(solution)/shard_map/all_to_all | solution.py:31
  91.7 0.7 all_gather_reshape.3
  92.5 18.1 %all_gather.7.refs_0_ = bf16[4,128,768]{2,1,0:T(8,128)(2,1)S(1)} all-gather(bf16[1,128,768]{2,1,0:T(8,128)(2,1)} %all_gather_reshape.3), channel_id=1, replica_groups=mesh['X'=4,'B'=4,'I'=4,'Y'=4,'C'=2] {'I'}, dimensions={0}, use_global_device_ids=true | all-gather | bytes 983040 | tf_op jit(solution)/shard_map/all_gather | solution.py:150
  110.5 0.1 fusion.9
  110.6 3.4 %collective-permute-start.3 = (bf16[2,128,768]{2,1,0:T(8,128)(2,1)S(1)}, bf16[2,128,768]{2,1,0:T(8,128)(2,1)S(1)}, u32[]{:S(2)}, u32[]{:S(2)}) collective-permute-start(bf16[2,128,768]{2,1,0:T(8,128)(2,1)S(1)} %get-tuple-element.37), channel_id=1, source_target_pairs={{0,2},{2,4},{4,6},{6,0},{1,3},{3,5},{5,7},{7,1},{8,10},{10,12},{12... | collective-permute-start | bytes 1179656 | tf_op jit(solution)/shard_map/ppermute | solution.py:153
  114.0 3.7 %collective-permute-start.5 = (bf16[2,128,768]{2,1,0:T(8,128)(2,1)S(1)}, bf16[2,128,768]{2,1,0:T(8,128)(2,1)S(1)}, u32[]{:S(2)}, u32[]{:S(2)}) collective-permute-start(bf16[2,128,768]{2,1,0:T(8,128)(2,1)S(1)} %get-tuple-element.36), channel_id=1, source_target_pairs={{0,6},{2,0},{4,2},{6,4},{1,7},{3,1},{5,3},{7,5},{8,14},{10,8},{12,... | collective-permute-start | bytes 1179656 | tf_op jit(solution)/shard_map/ppermute | solution.py:153
  117.7 2.2 %collective-permute-start.7 = (bf16[2,128,768]{2,1,0:T(8,128)(2,1)S(1)}, bf16[2,128,768]{2,1,0:T(8,128)(2,1)S(1)}, u32[]{:S(2)}, u32[]{:S(2)}) collective-permute-start(bf16[2,128,768]{2,1,0:T(8,128)(2,1)S(1)} %get-tuple-element.36), channel_id=1, source_target_pairs={{0,2},{2,4},{4,6},{6,0},{1,3},{3,5},{5,7},{7,1},{8,10},{10,12},{12... | collective-permute-start | bytes 1179656 | tf_op jit(solution)/shard_map/ppermute | solution.py:153
  119.8 4.9 %collective-permute-start.8 = (bf16[2,128,768]{2,1,0:T(8,128)(2,1)S(1)}, bf16[2,128,768]{2,1,0:T(8,128)(2,1)S(1)}, u32[]{:S(2)}, u32[]{:S(2)}) collective-permute-start(bf16[2,128,768]{2,1,0:T(8,128)(2,1)S(1)} %get-tuple-element.37), channel_id=1, source_target_pairs={{0,6},{2,0},{4,2},{6,4},{1,7},{3,1},{5,3},{7,5},{8,14},{10,8},{12,... | collective-permute-start | bytes 1179656 | tf_op jit(solution)/shard_map/ppermute | solution.py:153
  124.7 2.7 %collective-permute-start.4 = (bf16[2,128,768]{2,1,0:T(8,128)(2,1)S(1)}, bf16[2,128,768]{2,1,0:T(8,128)(2,1)S(1)}, u32[]{:S(2)}, u32[]{:S(2)}) collective-permute-start(bf16[2,128,768]{2,1,0:T(8,128)(2,1)S(1)} %collective-permute-done.3.refs_0_), channel_id=1, source_target_pairs={{0,2},{2,4},{4,6},{6,0},{1,3},{3,5},{5,7},{7,1},{8,10},{10,12},{12... | collective-permute-start | bytes 1179656 | tf_op jit(solution)/shard_map/ppermute | solution.py:153
  127.4 0.2 collective-permute-done.5.refs_3_
  127.7 4.2 %collective-permute-start.6 = (bf16[2,128,768]{2,1,0:T(8,128)(2,1)S(1)}, bf16[2,128,768]{2,1,0:T(8,128)(2,1)S(1)}, u32[]{:S(2)}, u32[]{:S(2)}) collective-permute-start(bf16[2,128,768]{2,1,0:T(8,128)(2,1)S(1)} %collective-permute-done.5.refs_3_), channel_id=1, source_target_pairs={{0,6},{2,0},{4,2},{6,4},{1,7},{3,1},{5,3},{7,5},{8,14},{10,8},{12,... | collective-permute-start | bytes 1179656 | tf_op jit(solution)/shard_map/ppermute | solution.py:153
  131.8 1.0 collective-permute-done.7.refs_1_
  132.8 3.3 %collective-permute-done.8.refs_2_ = bf16[2,128,768]{2,1,0:T(8,128)(2,1)S(1)} collective-permute-done((bf16[2,128,768]{2,1,0:T(8,128)(2,1)S(1)}, bf16[2,128,768]{2,1,0:T(8,128)(2,1)S(1)}, u32[]{:S(2)}, u32[]{:S(2)}) %collective-permute-start.8) | collective-permute-done | bytes 393248 | tf_op jit(solution)/shard_map/ppermute | solution.py:153
  136.1 1.4 copy-done.3
  137.5 5.0 %shard_map.105 = (bf16[4,128,768]{2,1,0:T(8,128)(2,1)S(1)}, bf16[4,128,768]{2,1,0:T(8,128)(2,1)S(1)}) custom-call(bf16[2,128,768]{2,1,0:T(8,128)(2,1)S(1)} %collective-permute-done.3.refs_0_, bf16[2,128,768]{2,1,0:T(8,128)(2,1)S(1)} %collective-permute-done.7.refs_1_, bf16[2,128,768]{2,1,0:T(8,128)(2,1)S(1)} %collective-permute-done.8.refs_2_, ...), custom_call_target="tpu_custom_call" | custom-call | flops 2415919104 | bytes 12582912 | tf_op jit(solution)/shard_map/pallas_call | solution.py:92
  142.6 0.9 copy-done.8
  143.4 0.9 copy-done.9
  144.3 3.9 %shard_map.106 = bf16[4,128,768]{2,1,0:T(8,128)(2,1)S(1)} custom-call(bf16[2,128,768]{2,1,0:T(8,128)(2,1)S(1)} %collective-permute-done.4.refs_0_, bf16[2,128,768]{2,1,0:T(8,128)(2,1)S(1)} %collective-permute-done.6.refs_1_, bf16[3072,256]{1,0:T(8,128)(2,1)S(1)} %copy-done.1, bf16[3072,256]{1,0:T(8,128)(2,1)S(1)} %copy-done.2, ...), custom_call_target="tpu_custom_call" | custom-call | flops 1207959552 | bytes 11010048 | tf_op jit(solution)/shard_map/pallas_call | solution.py:92
  148.2 0.9 copy-done.7
  149.1 4.2 %all-to-all-start.4 = ((bf16[4,128,768]{2,1,0:T(8,128)(2,1)}), bf16[4,128,768]{2,1,0:T(8,128)(2,1)}, u32[]{:S(2)}, u32[]{:S(2)}) async-start(bf16[4,128,768]{2,1,0:T(8,128)(2,1)} %copy-done.7), calls=%async_computation.4 | async-start | bytes 1572864 | tf_op jit(solution)/shard_map/all_to_all | solution.py:31
  153.3 3.4 %collective-permute-start.10 = (bf16[4,128,768]{2,1,0:T(8,128)(2,1)}, bf16[4,128,768]{2,1,0:T(8,128)(2,1)S(1)}, u32[]{:S(2)}, u32[]{:S(2)}) collective-permute-start(bf16[4,128,768]{2,1,0:T(8,128)(2,1)} %copy-done.9), channel_id=1, source_target_pairs={{0,2},{2,4},{4,6},{6,0},{1,3},{3,5},{5,7},{7,1},{8,10},{10,12},{12... | collective-permute-start | bytes 2359304 | tf_op jit(solution)/shard_map/ppermute | solution.py:153
  156.7 3.6 %collective-permute-start.9 = (bf16[4,128,768]{2,1,0:T(8,128)(2,1)}, bf16[4,128,768]{2,1,0:T(8,128)(2,1)S(1)}, u32[]{:S(2)}, u32[]{:S(2)}) collective-permute-start(bf16[4,128,768]{2,1,0:T(8,128)(2,1)} %copy-done.8), channel_id=1, source_target_pairs={{0,6},{2,0},{4,2},{6,4},{1,7},{3,1},{5,3},{7,5},{8,14},{10,8},{12,... | collective-permute-start | bytes 2359304 | tf_op jit(solution)/shard_map/ppermute | solution.py:153
  160.3 0.0 copy-start.4
  160.4 1.4 copy-done.4
  161.8 1.1 copy-done.6
  162.9 3.9 %shard_map.104 = bf16[4,128,768]{2,1,0:T(8,128)(2,1)S(1)} custom-call(bf16[4,128,768]{2,1,0:T(8,128)(2,1)S(1)} %copy-done.6, bf16[3072,256]{1,0:T(8,128)(2,1)S(1)} %copy-done.1, bf16[3072,256]{1,0:T(8,128)(2,1)S(1)} %copy-done.2, bf16[256,3072]{1,0:T(8,128)(2,1)S(1)} %copy-done.4, bf16[3072,256]{1,0:T(8,128)(2,1)} %collective-permute-done.refs_4_.refs_7_.refs_5_, ...), custom_call_target="tpu_custom_call" | custom-call | flops 1207959552 | bytes 11010048 | tf_op jit(solution)/shard_map/pallas_call | solution.py:92
  166.8 2.7 %collective-permute-done.10 = bf16[4,128,768]{2,1,0:T(8,128)(2,1)S(1)} collective-permute-done((bf16[4,128,768]{2,1,0:T(8,128)(2,1)}, bf16[4,128,768]{2,1,0:T(8,128)(2,1)S(1)}, u32[]{:S(2)}, u32[]{:S(2)}) %collective-permute-start.10) | collective-permute-done | bytes 786464 | tf_op jit(solution)/shard_map/ppermute | solution.py:153
  169.4 1.4 collective-permute-done.9
  170.8 1.2 add_convert_fusion
  172.0 5.0 %all-to-all-start.3 = ((bf16[4,128,768]{2,1,0:T(8,128)(2,1)}), bf16[4,128,768]{2,1,0:T(8,128)(2,1)S(1)}, u32[]{:S(2)}, u32[]{:S(2)}) async-start(bf16[4,128,768]{2,1,0:T(8,128)(2,1)} %add_convert_fusion), calls=%async_computation.3 | async-start | bytes 1572864 | tf_op jit(solution)/shard_map/all_to_all | solution.py:31
  177.0 1.3 reduce_sum.102
  178.3 5.1 %collective-permute-start.11 = (bf16[128,768]{1,0:T(8,128)(2,1)S(1)}, bf16[128,768]{1,0:T(8,128)(2,1)S(1)}, u32[]{:S(2)}, u32[]{:S(2)}) collective-permute-start(bf16[128,768]{1,0:T(8,128)(2,1)S(1)} %reduce_sum.102), channel_id=1, source_target_pairs={{0,4},{2,6},{4,0},{6,2},{1,5},{3,7},{5,1},{7,3},{8,12},{10,14},{12... | collective-permute-start | bytes 589832 | tf_op jit(solution)/shard_map/ppermute | solution.py:153
  183.4 6.7 %all-to-all-done.3 = bf16[4,128,768]{2,1,0:T(8,128)(2,1)S(1)} async-done(((bf16[4,128,768]{2,1,0:T(8,128)(2,1)}), bf16[4,128,768]{2,1,0:T(8,128)(2,1)S(1)}, u32[]{:S(2)}, u32[]{:S(2)}) %all-to-all-start.3) | async-done | bytes 786464 | tf_op jit(solution)/shard_map/all_to_all | solution.py:31
  190.1 0.1 convert_reduce_fusion
  190.3 0.7 reshape.81
  191.0 7.6 %all-to-all-start.5 = ((bf16[64,2,768]{2,1,0:T(2,128)(2,1)}), bf16[64,2,768]{2,1,0:T(2,128)(2,1)S(1)}, u32[]{:S(2)}, u32[]{:S(2)}) async-start(bf16[64,2,768]{2,1,0:T(2,128)(2,1)} %reshape.81), calls=%async_computation.5 | async-start | bytes 393216 | tf_op jit(solution)/shard_map/all_to_all | solution.py:31
  198.6 0.2 fusion.7
  198.9 0.2 select_reduce_fusion.1
  199.0 0.1 exponential_reduce_fusion
  199.1 0.1 exponential_divide_fusion
  199.2 0.1 select_reduce_fusion
  199.3 14.7 %all-to-all-done.5 = bf16[64,2,768]{2,1,0:T(2,128)(2,1)S(1)} async-done(((bf16[64,2,768]{2,1,0:T(2,128)(2,1)}), bf16[64,2,768]{2,1,0:T(2,128)(2,1)S(1)}, u32[]{:S(2)}, u32[]{:S(2)}) %all-to-all-start.5) | async-done | bytes 196640 | tf_op jit(solution)/shard_map/all_to_all | solution.py:31
  214.0 0.1 copy.19
  214.1 0.8 convolution_convert_fusion.1
  (37 shorter events, 0.2 us)
Async XLA Ops:
  0.6 198.0 %copy-start = (bf16[3072,16]{0,1:T(8,128)(2,1)S(1)}, bf16[3072,16]{0,1:T(8,128)(2,1)}, u32[]{:S(2)}) copy-start(bf16[3072,16]{0,1:T(8,128)(2,1)} %param.13) | copy-start | bytes 294916
  0.6 54.4 %copy-start.13 = (bf16[3072]{0:T(1024)(128)(2,1)S(1)}, bf16[3072]{0:T(1024)(128)(2,1)}, u32[]{:S(2)}) copy-start(bf16[3072]{0:T(1024)(128)(2,1)} %param.12) | copy-start | bytes 18436
  0.7 54.5 %copy-start.1 = (bf16[3072,256]{1,0:T(8,128)(2,1)S(1)}, bf16[3072,256]{1,0:T(8,128)(2,1)}, u32[]{:S(2)}) copy-start(bf16[3072,256]{1,0:T(8,128)(2,1)} %refs_2_.3) | copy-start | bytes 4718596
  0.7 45.7 %copy-start.11 = (s32[4,4]{1,0:T(4,128)S(1)}, s32[4,4]{1,0:T(4,128)}, u32[]{:S(2)}) copy-start(s32[4,4]{1,0:T(4,128)} %param.17) | copy-start | bytes 196
  0.7 61.1 %copy-start.12 = (bf16[4,3072]{1,0:T(4,128)(2,1)S(1)}, bf16[4,3072]{1,0:T(4,128)(2,1)}, u32[]{:S(2)}) copy-start(bf16[4,3072]{1,0:T(4,128)(2,1)} %param.11) | copy-start | bytes 73732
  2.2 43.8 %all-to-all-start = ((bf16[4,32,384]{2,1,0:T(8,128)(2,1)}), bf16[4,32,384]{2,1,0:T(8,128)(2,1)S(1)}, u32[]{:S(2)}, u32[]{:S(2)}) async-start(bf16[4,32,384]{2,1,0:T(8,128)(2,1)} %broadcast_in_dim.22), calls=%async_computation | async-start | bytes 196608 | tf_op jit(solution)/shard_map/all_to_all | solution.py:31
  47.4 14.2 %all-to-all-start.1 = ((bf16[32,4,768]{2,1,0:T(4,128)(2,1)}), bf16[32,4,768]{2,1,0:T(4,128)(2,1)S(1)}, u32[]{:S(2)}, u32[]{:S(2)}) async-start(bf16[32,4,768]{2,1,0:T(4,128)(2,1)} %reshape.77), calls=%async_computation.1 | async-start | bytes 393216 | tf_op jit(solution)/shard_map/all_to_all | solution.py:31
  55.1 36.6 %collective-permute-start = (bf16[3072,256]{1,0:T(8,128)(2,1)S(1)}, bf16[3072,256]{1,0:T(8,128)(2,1)}, u32[]{:S(2)}, u32[]{:S(2)}) collective-permute-start(bf16[3072,256]{1,0:T(8,128)(2,1)S(1)} %copy-done.1), channel_id=1, source_target_pairs={{0,1},{1,0},{2,3},{3,2},{4,5},{5,4},{6,7},{7,6},{8,9},{9,8},{10,11... | collective-permute-start | bytes 4718600 | tf_op jit(solution)/shard_map/ppermute | solution.py:45
  57.2 34.5 %collective-permute-start.1 = (bf16[3072,256]{1,0:T(8,128)(2,1)}, bf16[3072,256]{1,0:T(8,128)(2,1)}, u32[]{:S(2)}, u32[]{:S(2)}) collective-permute-start(bf16[3072,256]{1,0:T(8,128)(2,1)} %refs_3_.3), channel_id=1, source_target_pairs={{0,1},{1,0},{2,3},{3,2},{4,5},{5,4},{6,7},{7,6},{8,9},{9,8},{10,11... | collective-permute-start | bytes 4718600 | tf_op jit(solution)/shard_map/ppermute | solution.py:45
  59.5 32.2 %collective-permute-start.2 = (bf16[256,3072]{1,0:T(8,128)(2,1)}, bf16[256,3072]{1,0:T(8,128)(2,1)}, u32[]{:S(2)}, u32[]{:S(2)}) collective-permute-start(bf16[256,3072]{1,0:T(8,128)(2,1)} %refs_4_.3), channel_id=1, source_target_pairs={{0,1},{1,0},{2,3},{3,2},{4,5},{5,4},{6,7},{7,6},{8,9},{9,8},{10,11... | collective-permute-start | bytes 4718600 | tf_op jit(solution)/shard_map/ppermute | solution.py:45
  61.9 136.8 %copy-start.10 = (bf16[4,3072]{1,0:T(4,128)(2,1)}, bf16[4,3072]{1,0:T(4,128)(2,1)S(1)}, u32[]{:S(2)}) copy-start(bf16[4,3072]{1,0:T(4,128)(2,1)S(1)} %get-tuple-element.35) | copy-start | bytes 73732
  91.7 44.4 %copy-start.2 = (bf16[3072,256]{1,0:T(8,128)(2,1)S(1)}, bf16[3072,256]{1,0:T(8,128)(2,1)}, u32[]{:S(2)}) copy-start(bf16[3072,256]{1,0:T(8,128)(2,1)} %refs_3_.3) | copy-start | bytes 4718596
  110.5 22.3 %copy-start.5 = (bf16[4,128,768]{2,1,0:T(8,128)(2,1)}, bf16[4,128,768]{2,1,0:T(8,128)(2,1)S(1)}, u32[]{:S(2)}) copy-start(bf16[4,128,768]{2,1,0:T(8,128)(2,1)S(1)} %all_gather.7.refs_0_) | copy-start | bytes 2359300
  110.6 14.1 %collective-permute-start.3 = (bf16[2,128,768]{2,1,0:T(8,128)(2,1)S(1)}, bf16[2,128,768]{2,1,0:T(8,128)(2,1)S(1)}, u32[]{:S(2)}, u32[]{:S(2)}) collective-permute-start(bf16[2,128,768]{2,1,0:T(8,128)(2,1)S(1)} %get-tuple-element.37), channel_id=1, source_target_pairs={{0,2},{2,4},{4,6},{6,0},{1,3},{3,5},{5,7},{7,1},{8,10},{10,12},{12... | collective-permute-start | bytes 1179656 | tf_op jit(solution)/shard_map/ppermute | solution.py:153
  114.0 13.7 %collective-permute-start.5 = (bf16[2,128,768]{2,1,0:T(8,128)(2,1)S(1)}, bf16[2,128,768]{2,1,0:T(8,128)(2,1)S(1)}, u32[]{:S(2)}, u32[]{:S(2)}) collective-permute-start(bf16[2,128,768]{2,1,0:T(8,128)(2,1)S(1)} %get-tuple-element.36), channel_id=1, source_target_pairs={{0,6},{2,0},{4,2},{6,4},{1,7},{3,1},{5,3},{7,5},{8,14},{10,8},{12,... | collective-permute-start | bytes 1179656 | tf_op jit(solution)/shard_map/ppermute | solution.py:153
  117.7 15.2 %collective-permute-start.7 = (bf16[2,128,768]{2,1,0:T(8,128)(2,1)S(1)}, bf16[2,128,768]{2,1,0:T(8,128)(2,1)S(1)}, u32[]{:S(2)}, u32[]{:S(2)}) collective-permute-start(bf16[2,128,768]{2,1,0:T(8,128)(2,1)S(1)} %get-tuple-element.36), channel_id=1, source_target_pairs={{0,2},{2,4},{4,6},{6,0},{1,3},{3,5},{5,7},{7,1},{8,10},{10,12},{12... | collective-permute-start | bytes 1179656 | tf_op jit(solution)/shard_map/ppermute | solution.py:153
  119.8 16.2 %collective-permute-start.8 = (bf16[2,128,768]{2,1,0:T(8,128)(2,1)S(1)}, bf16[2,128,768]{2,1,0:T(8,128)(2,1)S(1)}, u32[]{:S(2)}, u32[]{:S(2)}) collective-permute-start(bf16[2,128,768]{2,1,0:T(8,128)(2,1)S(1)} %get-tuple-element.37), channel_id=1, source_target_pairs={{0,6},{2,0},{4,2},{6,4},{1,7},{3,1},{5,3},{7,5},{8,14},{10,8},{12,... | collective-permute-start | bytes 1179656 | tf_op jit(solution)/shard_map/ppermute | solution.py:153
  124.7 19.6 %collective-permute-start.4 = (bf16[2,128,768]{2,1,0:T(8,128)(2,1)S(1)}, bf16[2,128,768]{2,1,0:T(8,128)(2,1)S(1)}, u32[]{:S(2)}, u32[]{:S(2)}) collective-permute-start(bf16[2,128,768]{2,1,0:T(8,128)(2,1)S(1)} %collective-permute-done.3.refs_0_), channel_id=1, source_target_pairs={{0,2},{2,4},{4,6},{6,0},{1,3},{3,5},{5,7},{7,1},{8,10},{10,12},{12... | collective-permute-start | bytes 1179656 | tf_op jit(solution)/shard_map/ppermute | solution.py:153
  127.7 16.7 %collective-permute-start.6 = (bf16[2,128,768]{2,1,0:T(8,128)(2,1)S(1)}, bf16[2,128,768]{2,1,0:T(8,128)(2,1)S(1)}, u32[]{:S(2)}, u32[]{:S(2)}) collective-permute-start(bf16[2,128,768]{2,1,0:T(8,128)(2,1)S(1)} %collective-permute-done.5.refs_3_), channel_id=1, source_target_pairs={{0,6},{2,0},{4,2},{6,4},{1,7},{3,1},{5,3},{7,5},{8,14},{10,8},{12,... | collective-permute-start | bytes 1179656 | tf_op jit(solution)/shard_map/ppermute | solution.py:153
  136.1 1.4 copy-start.3
  142.5 0.9 copy-start.8
  143.4 0.9 copy-start.9
  148.2 0.9 copy-start.7
  149.1 22.9 %all-to-all-start.4 = ((bf16[4,128,768]{2,1,0:T(8,128)(2,1)}), bf16[4,128,768]{2,1,0:T(8,128)(2,1)}, u32[]{:S(2)}, u32[]{:S(2)}) async-start(bf16[4,128,768]{2,1,0:T(8,128)(2,1)} %copy-done.7), calls=%async_computation.4 | async-start | bytes 1572864 | tf_op jit(solution)/shard_map/all_to_all | solution.py:31
  153.3 16.2 %collective-permute-start.10 = (bf16[4,128,768]{2,1,0:T(8,128)(2,1)}, bf16[4,128,768]{2,1,0:T(8,128)(2,1)S(1)}, u32[]{:S(2)}, u32[]{:S(2)}) collective-permute-start(bf16[4,128,768]{2,1,0:T(8,128)(2,1)} %copy-done.9), channel_id=1, source_target_pairs={{0,2},{2,4},{4,6},{6,0},{1,3},{3,5},{5,7},{7,1},{8,10},{10,12},{12... | collective-permute-start | bytes 2359304 | tf_op jit(solution)/shard_map/ppermute | solution.py:153
  156.7 14.1 %collective-permute-start.9 = (bf16[4,128,768]{2,1,0:T(8,128)(2,1)}, bf16[4,128,768]{2,1,0:T(8,128)(2,1)S(1)}, u32[]{:S(2)}, u32[]{:S(2)}) collective-permute-start(bf16[4,128,768]{2,1,0:T(8,128)(2,1)} %copy-done.8), channel_id=1, source_target_pairs={{0,6},{2,0},{4,2},{6,4},{1,7},{3,1},{5,3},{7,5},{8,14},{10,8},{12,... | collective-permute-start | bytes 2359304 | tf_op jit(solution)/shard_map/ppermute | solution.py:153
  160.3 1.4 copy-start.4
  161.8 1.1 copy-start.6
  172.0 18.1 %all-to-all-start.3 = ((bf16[4,128,768]{2,1,0:T(8,128)(2,1)}), bf16[4,128,768]{2,1,0:T(8,128)(2,1)S(1)}, u32[]{:S(2)}, u32[]{:S(2)}) async-start(bf16[4,128,768]{2,1,0:T(8,128)(2,1)} %add_convert_fusion), calls=%async_computation.3 | async-start | bytes 1572864 | tf_op jit(solution)/shard_map/all_to_all | solution.py:31
  178.3 11.9 %collective-permute-start.11 = (bf16[128,768]{1,0:T(8,128)(2,1)S(1)}, bf16[128,768]{1,0:T(8,128)(2,1)S(1)}, u32[]{:S(2)}, u32[]{:S(2)}) collective-permute-start(bf16[128,768]{1,0:T(8,128)(2,1)S(1)} %reduce_sum.102), channel_id=1, source_target_pairs={{0,4},{2,6},{4,0},{6,2},{1,5},{3,7},{5,1},{7,3},{8,12},{10,14},{12... | collective-permute-start | bytes 589832 | tf_op jit(solution)/shard_map/ppermute | solution.py:153
  191.0 22.9 %all-to-all-start.5 = ((bf16[64,2,768]{2,1,0:T(2,128)(2,1)}), bf16[64,2,768]{2,1,0:T(2,128)(2,1)S(1)}, u32[]{:S(2)}, u32[]{:S(2)}) async-start(bf16[64,2,768]{2,1,0:T(2,128)(2,1)} %reshape.81), calls=%async_computation.5 | async-start | bytes 393216 | tf_op jit(solution)/shard_map/all_to_all | solution.py:31

commit v7 on v6

--- a/solution.py
+++ b/solution.py
@@ -159,7 +159,7 @@
     near_below, near_above = both_cores(
         [[below_low, below_high], [above_low, above_high]], weights, partner
     )
-    *far, near_below, near_above = lax.optimization_barrier((*far, near_below, near_above))
+    *far, near_below = lax.optimization_barrier((*far, near_below))
     to_below, to_above = turn(near_below, -1), turn(near_above, 1)
     far_block = over_block(both_cores([far], weights, partner)[0])
     to_far = turn(far_block.astype(jnp.bfloat16), 2)

time: 217 us -> 217 us (level)
  no operation moved by 1% of the time
where the time goes in v7:
time: 217 us; the launch traced here: 215 us
  blocking collectives  81.8 us (38%)
  starting transfers between devices  73.1 us (34%)
  waiting for transfers between devices  29.9 us (14%)
  Pallas kernels  12.8 us (6%)
  local copies, waits for them, and re-layouts  10.8 us (5%)
  other arithmetic  3.92 us (2%)
    all_gather x1, blocking collectives, attention_rows(): columns = lax.all_gather(out_weight.T, ('B', 'I'), axis=0, tiled=True)  34.7 us
    all_to_all x5, starting transfers between devices, swap(): return lax.all_to_all(value, axes, split_axis=0, concat_axis=0, tiled=True)  33.6 us
    ppermute x9, starting transfers between devices, turn(): return lax.ppermute(value, 'Y', [(i, (i + by) % 4) for i in range(4)])  33.1 us
    all_to_all x1, blocking collectives, swap(): return lax.all_to_all(value, axes, split_axis=0, concat_axis=0, tiled=True)  29 us
    all_to_all x5, waiting for transfers between devices, swap(): return lax.all_to_all(value, axes, split_axis=0, concat_axis=0, tiled=True)  21.4 us
    all_gather x1, blocking collectives, on_device(): block_rows = lax.all_gather(landed.reshape(-1, quarter), 'I')  18.1 us
    pallas_call x3, Pallas kernels, both_cores(): pl.pallas_call(functools.partial(expert_kernel, layout), out_shape=[jax.S...  12.8 us
    ppermute x9, waiting for transfers between devices, turn(): return lax.ppermute(value, 'Y', [(i, (i + by) % 4) for i in range(4)])  8.51 us
  transfers between devices with their start and end apart: 17, of which 7 were waited for; matrix products, arithmetic and copies ran while one was open for 2% of the time, Pallas kernels for 4%

profile of v7, /device:TPU:6, one launch (start us, length us, event | category | flops | bytes accessed | tf_op | source)
XLA Modules:
  0.0 214.9 jit_solution(10055717381724024826)
XLA Ops:
  0.6 0.0 copy-start
  0.7 1.5 broadcast_in_dim.22
  2.2 9.1 %all-to-all-start = ((bf16[4,32,384]{2,1,0:T(8,128)(2,1)}), bf16[4,32,384]{2,1,0:T(8,128)(2,1)S(1)}, u32[]{:S(2)}, u32[]{:S(2)}) async-start(bf16[4,32,384]{2,1,0:T(8,128)(2,1)} %broadcast_in_dim.22), calls=%async_computation | async-start | bytes 196608 | tf_op jit(solution)/shard_map/all_to_all | solution.py:31
  11.3 34.7 %all_gather.6 = bf16[768,384]{1,0:T(8,128)(2,1)S(1)} all-gather(bf16[48,384]{1,0:T(8,128)(2,1)} %bitcast.29), channel_id=1, replica_groups=mesh['X'=4,'B'=4,'I'=4,'Y'=4,'C'=2] {'B','I'}, dimensions={0}, use_global_device_ids=true | all-gather | bytes 626688 | tf_op jit(solution)/shard_map/all_gather | solution.py:40
  46.0 0.3 convolution_convert_fusion.2
  46.3 0.7 reshape.77
  47.1 7.6 %all-to-all-start.1 = ((bf16[32,4,768]{2,1,0:T(4,128)(2,1)}), bf16[32,4,768]{2,1,0:T(4,128)(2,1)S(1)}, u32[]{:S(2)}, u32[]{:S(2)}) async-start(bf16[32,4,768]{2,1,0:T(4,128)(2,1)} %reshape.77), calls=%async_computation.1 | async-start | bytes 393216 | tf_op jit(solution)/shard_map/all_to_all | solution.py:31
  54.7 0.1 convert_reduce_fusion.3
  54.9 0.2 select_reduce_fusion.2
  55.1 2.1 collective-permute-start
  57.2 2.3 %collective-permute-start.1 = (bf16[3072,256]{1,0:T(8,128)(2,1)}, bf16[3072,256]{1,0:T(8,128)(2,1)}, u32[]{:S(2)}, u32[]{:S(2)}) collective-permute-start(bf16[3072,256]{1,0:T(8,128)(2,1)} %refs_3_.3), channel_id=1, source_target_pairs={{0,1},{1,0},{2,3},{3,2},{4,5},{5,4},{6,7},{7,6},{8,9},{9,8},{10,11... | collective-permute-start | bytes 4718600 | tf_op jit(solution)/shard_map/ppermute | solution.py:45
  59.5 2.1 collective-permute-start.2
  61.5 0.1 fusion.5
  61.6 0.1 convert_reduce_fusion.1
  61.7 0.1 convert_reduce_fusion.2
  61.9 0.2 fusion.2
  62.1 0.3 convolution_convert_fusion
  62.4 0.1 reshape.79
  62.5 0.2 copy.18
  62.7 29.0 %all_to_all.30 = bf16[64,2,768]{2,1,0:T(2,128)(2,1)S(1)} all-to-all(bf16[64,2,768]{2,1,0:T(2,128)(2,1)S(1)} %bitcast.25), channel_id=1, replica_groups=mesh['X'=4,'B'=4,'I'=4,'Y'=4,'C'=2] {'X','B','I'}, dimensions={0} | all-to-all | bytes 393216 | tf_op jit(solution)/shard_map/all_to_all | solution.py:31
  91.7 0.0 collective-permute-done.refs_4_.refs_7_.refs_5_
  91.7 0.7 all_gather_reshape.3
  92.4 18.1 %all_gather.7.refs_0_ = bf16[4,128,768]{2,1,0:T(8,128)(2,1)S(1)} all-gather(bf16[1,128,768]{2,1,0:T(8,128)(2,1)} %all_gather_reshape.3), channel_id=1, replica_groups=mesh['X'=4,'B'=4,'I'=4,'Y'=4,'C'=2] {'I'}, dimensions={0}, use_global_device_ids=true | all-gather | bytes 983040 | tf_op jit(solution)/shard_map/all_gather | solution.py:150
  110.5 0.1 fusion.9
  110.6 3.4 %collective-permute-start.3 = (bf16[2,128,768]{2,1,0:T(8,128)(2,1)S(1)}, bf16[2,128,768]{2,1,0:T(8,128)(2,1)S(1)}, u32[]{:S(2)}, u32[]{:S(2)}) collective-permute-start(bf16[2,128,768]{2,1,0:T(8,128)(2,1)S(1)} %get-tuple-element.35), channel_id=1, source_target_pairs={{0,2},{2,4},{4,6},{6,0},{1,3},{3,5},{5,7},{7,1},{8,10},{10,12},{12... | collective-permute-start | bytes 1179656 | tf_op jit(solution)/shard_map/ppermute | solution.py:153
  114.0 3.7 %collective-permute-start.5 = (bf16[2,128,768]{2,1,0:T(8,128)(2,1)S(1)}, bf16[2,128,768]{2,1,0:T(8,128)(2,1)S(1)}, u32[]{:S(2)}, u32[]{:S(2)}) collective-permute-start(bf16[2,128,768]{2,1,0:T(8,128)(2,1)S(1)} %get-tuple-element.34), channel_id=1, source_target_pairs={{0,6},{2,0},{4,2},{6,4},{1,7},{3,1},{5,3},{7,5},{8,14},{10,8},{12,... | collective-permute-start | bytes 1179656 | tf_op jit(solution)/shard_map/ppermute | solution.py:153
  117.7 2.2 %collective-permute-start.7 = (bf16[2,128,768]{2,1,0:T(8,128)(2,1)S(1)}, bf16[2,128,768]{2,1,0:T(8,128)(2,1)S(1)}, u32[]{:S(2)}, u32[]{:S(2)}) collective-permute-start(bf16[2,128,768]{2,1,0:T(8,128)(2,1)S(1)} %get-tuple-element.34), channel_id=1, source_target_pairs={{0,2},{2,4},{4,6},{6,0},{1,3},{3,5},{5,7},{7,1},{8,10},{10,12},{12... | collective-permute-start | bytes 1179656 | tf_op jit(solution)/shard_map/ppermute | solution.py:153
  119.8 4.9 %collective-permute-start.8 = (bf16[2,128,768]{2,1,0:T(8,128)(2,1)S(1)}, bf16[2,128,768]{2,1,0:T(8,128)(2,1)S(1)}, u32[]{:S(2)}, u32[]{:S(2)}) collective-permute-start(bf16[2,128,768]{2,1,0:T(8,128)(2,1)S(1)} %get-tuple-element.35), channel_id=1, source_target_pairs={{0,6},{2,0},{4,2},{6,4},{1,7},{3,1},{5,3},{7,5},{8,14},{10,8},{12,... | collective-permute-start | bytes 1179656 | tf_op jit(solution)/shard_map/ppermute | solution.py:153
  124.7 2.7 %collective-permute-start.4 = (bf16[2,128,768]{2,1,0:T(8,128)(2,1)S(1)}, bf16[2,128,768]{2,1,0:T(8,128)(2,1)S(1)}, u32[]{:S(2)}, u32[]{:S(2)}) collective-permute-start(bf16[2,128,768]{2,1,0:T(8,128)(2,1)S(1)} %collective-permute-done.3.refs_0_), channel_id=1, source_target_pairs={{0,2},{2,4},{4,6},{6,0},{1,3},{3,5},{5,7},{7,1},{8,10},{10,12},{12... | collective-permute-start | bytes 1179656 | tf_op jit(solution)/shard_map/ppermute | solution.py:153
  127.4 0.2 collective-permute-done.5.refs_3_
  127.6 4.2 %collective-permute-start.6 = (bf16[2,128,768]{2,1,0:T(8,128)(2,1)S(1)}, bf16[2,128,768]{2,1,0:T(8,128)(2,1)S(1)}, u32[]{:S(2)}, u32[]{:S(2)}) collective-permute-start(bf16[2,128,768]{2,1,0:T(8,128)(2,1)S(1)} %collective-permute-done.5.refs_3_), channel_id=1, source_target_pairs={{0,6},{2,0},{4,2},{6,4},{1,7},{3,1},{5,3},{7,5},{8,14},{10,8},{12,... | collective-permute-start | bytes 1179656 | tf_op jit(solution)/shard_map/ppermute | solution.py:153
  131.8 1.0 collective-permute-done.7.refs_1_
  132.8 3.3 %collective-permute-done.8.refs_2_ = bf16[2,128,768]{2,1,0:T(8,128)(2,1)S(1)} collective-permute-done((bf16[2,128,768]{2,1,0:T(8,128)(2,1)S(1)}, bf16[2,128,768]{2,1,0:T(8,128)(2,1)S(1)}, u32[]{:S(2)}, u32[]{:S(2)}) %collective-permute-start.8) | collective-permute-done | bytes 393248 | tf_op jit(solution)/shard_map/ppermute | solution.py:153
  136.1 1.4 copy-done.3
  137.5 5.0 %shard_map.105 = (bf16[4,128,768]{2,1,0:T(8,128)(2,1)S(1)}, bf16[4,128,768]{2,1,0:T(8,128)(2,1)S(1)}) custom-call(bf16[2,128,768]{2,1,0:T(8,128)(2,1)S(1)} %collective-permute-done.3.refs_0_, bf16[2,128,768]{2,1,0:T(8,128)(2,1)S(1)} %collective-permute-done.7.refs_1_, bf16[2,128,768]{2,1,0:T(8,128)(2,1)S(1)} %collective-permute-done.8.refs_2_, ...), custom_call_target="tpu_custom_call" | custom-call | flops 2415919104 | bytes 12582912 | tf_op jit(solution)/shard_map/pallas_call | solution.py:92
  142.5 0.9 copy-done.8
  143.4 0.9 copy-done.9
  144.3 3.9 %shard_map.106 = bf16[4,128,768]{2,1,0:T(8,128)(2,1)S(1)} custom-call(bf16[2,128,768]{2,1,0:T(8,128)(2,1)S(1)} %collective-permute-done.4.refs_0_, bf16[2,128,768]{2,1,0:T(8,128)(2,1)S(1)} %collective-permute-done.6.refs_1_, bf16[3072,256]{1,0:T(8,128)(2,1)S(1)} %copy-done.1, bf16[3072,256]{1,0:T(8,128)(2,1)S(1)} %copy-done.2, ...), custom_call_target="tpu_custom_call" | custom-call | flops 1207959552 | bytes 11010048 | tf_op jit(solution)/shard_map/pallas_call | solution.py:92
  148.2 0.9 copy-done.7
  149.1 4.2 %all-to-all-start.4 = ((bf16[4,128,768]{2,1,0:T(8,128)(2,1)}), bf16[4,128,768]{2,1,0:T(8,128)(2,1)}, u32[]{:S(2)}, u32[]{:S(2)}) async-start(bf16[4,128,768]{2,1,0:T(8,128)(2,1)} %copy-done.7), calls=%async_computation.4 | async-start | bytes 1572864 | tf_op jit(solution)/shard_map/all_to_all | solution.py:31
  153.3 3.4 %collective-permute-start.10 = (bf16[4,128,768]{2,1,0:T(8,128)(2,1)}, bf16[4,128,768]{2,1,0:T(8,128)(2,1)S(1)}, u32[]{:S(2)}, u32[]{:S(2)}) collective-permute-start(bf16[4,128,768]{2,1,0:T(8,128)(2,1)} %copy-done.9), channel_id=1, source_target_pairs={{0,2},{2,4},{4,6},{6,0},{1,3},{3,5},{5,7},{7,1},{8,10},{10,12},{12... | collective-permute-start | bytes 2359304 | tf_op jit(solution)/shard_map/ppermute | solution.py:153
  156.7 3.6 %collective-permute-start.9 = (bf16[4,128,768]{2,1,0:T(8,128)(2,1)}, bf16[4,128,768]{2,1,0:T(8,128)(2,1)S(1)}, u32[]{:S(2)}, u32[]{:S(2)}) collective-permute-start(bf16[4,128,768]{2,1,0:T(8,128)(2,1)} %copy-done.8), channel_id=1, source_target_pairs={{0,6},{2,0},{4,2},{6,4},{1,7},{3,1},{5,3},{7,5},{8,14},{10,8},{12,... | collective-permute-start | bytes 2359304 | tf_op jit(solution)/shard_map/ppermute | solution.py:153
  160.3 0.0 copy-start.4
  160.3 1.4 copy-done.4
  161.7 1.1 copy-done.6
  162.9 3.9 %shard_map.104 = bf16[4,128,768]{2,1,0:T(8,128)(2,1)S(1)} custom-call(bf16[4,128,768]{2,1,0:T(8,128)(2,1)S(1)} %copy-done.6, bf16[3072,256]{1,0:T(8,128)(2,1)S(1)} %copy-done.1, bf16[3072,256]{1,0:T(8,128)(2,1)S(1)} %copy-done.2, bf16[256,3072]{1,0:T(8,128)(2,1)S(1)} %copy-done.4, bf16[3072,256]{1,0:T(8,128)(2,1)} %collective-permute-done.refs_4_.refs_7_.refs_5_, ...), custom_call_target="tpu_custom_call" | custom-call | flops 1207959552 | bytes 11010048 | tf_op jit(solution)/shard_map/pallas_call | solution.py:92
  166.8 2.7 %collective-permute-done.10 = bf16[4,128,768]{2,1,0:T(8,128)(2,1)S(1)} collective-permute-done((bf16[4,128,768]{2,1,0:T(8,128)(2,1)}, bf16[4,128,768]{2,1,0:T(8,128)(2,1)S(1)}, u32[]{:S(2)}, u32[]{:S(2)}) %collective-permute-start.10) | collective-permute-done | bytes 786464 | tf_op jit(solution)/shard_map/ppermute | solution.py:153
  169.4 1.4 collective-permute-done.9
  170.8 1.2 add_convert_fusion
  172.0 5.0 %all-to-all-start.3 = ((bf16[4,128,768]{2,1,0:T(8,128)(2,1)}), bf16[4,128,768]{2,1,0:T(8,128)(2,1)S(1)}, u32[]{:S(2)}, u32[]{:S(2)}) async-start(bf16[4,128,768]{2,1,0:T(8,128)(2,1)} %add_convert_fusion), calls=%async_computation.3 | async-start | bytes 1572864 | tf_op jit(solution)/shard_map/all_to_all | solution.py:31
  177.0 1.3 reduce_sum.102
  178.3 5.1 %collective-permute-start.11 = (bf16[128,768]{1,0:T(8,128)(2,1)S(1)}, bf16[128,768]{1,0:T(8,128)(2,1)S(1)}, u32[]{:S(2)}, u32[]{:S(2)}) collective-permute-start(bf16[128,768]{1,0:T(8,128)(2,1)S(1)} %reduce_sum.102), channel_id=1, source_target_pairs={{0,4},{2,6},{4,0},{6,2},{1,5},{3,7},{5,1},{7,3},{8,12},{10,14},{12... | collective-permute-start | bytes 589832 | tf_op jit(solution)/shard_map/ppermute | solution.py:153
  183.4 6.7 %all-to-all-done.3 = bf16[4,128,768]{2,1,0:T(8,128)(2,1)S(1)} async-done(((bf16[4,128,768]{2,1,0:T(8,128)(2,1)}), bf16[4,128,768]{2,1,0:T(8,128)(2,1)S(1)}, u32[]{:S(2)}, u32[]{:S(2)}) %all-to-all-start.3) | async-done | bytes 786464 | tf_op jit(solution)/shard_map/all_to_all | solution.py:31
  190.1 0.1 convert_reduce_fusion
  190.3 0.7 reshape.81
  191.0 7.6 %all-to-all-start.5 = ((bf16[64,2,768]{2,1,0:T(2,128)(2,1)}), bf16[64,2,768]{2,1,0:T(2,128)(2,1)S(1)}, u32[]{:S(2)}, u32[]{:S(2)}) async-start(bf16[64,2,768]{2,1,0:T(2,128)(2,1)} %reshape.81), calls=%async_computation.5 | async-start | bytes 393216 | tf_op jit(solution)/shard_map/all_to_all | solution.py:31
  198.6 0.2 fusion.7
  198.9 0.2 select_reduce_fusion.1
  199.0 0.1 exponential_reduce_fusion
  199.1 0.1 exponential_divide_fusion
  199.2 0.1 select_reduce_fusion
  199.3 14.7 %all-to-all-done.5 = bf16[64,2,768]{2,1,0:T(2,128)(2,1)S(1)} async-done(((bf16[64,2,768]{2,1,0:T(2,128)(2,1)}), bf16[64,2,768]{2,1,0:T(2,128)(2,1)S(1)}, u32[]{:S(2)}, u32[]{:S(2)}) %all-to-all-start.5) | async-done | bytes 196640 | tf_op jit(solution)/shard_map/all_to_all | solution.py:31
  214.0 0.1 copy.19
  214.1 0.8 convolution_convert_fusion.1
  (37 shorter events, 0.2 us)
Async XLA Ops:
  0.6 198.0 %copy-start = (bf16[3072,16]{0,1:T(8,128)(2,1)S(1)}, bf16[3072,16]{0,1:T(8,128)(2,1)}, u32[]{:S(2)}) copy-start(bf16[3072,16]{0,1:T(8,128)(2,1)} %param.13) | copy-start | bytes 294916
  0.6 54.5 %copy-start.1 = (bf16[3072,256]{1,0:T(8,128)(2,1)S(1)}, bf16[3072,256]{1,0:T(8,128)(2,1)}, u32[]{:S(2)}) copy-start(bf16[3072,256]{1,0:T(8,128)(2,1)} %refs_2_.3) | copy-start | bytes 4718596
  0.7 54.1 %copy-start.11 = (s32[4,4]{1,0:T(4,128)S(1)}, s32[4,4]{1,0:T(4,128)}, u32[]{:S(2)}) copy-start(s32[4,4]{1,0:T(4,128)} %param.17) | copy-start | bytes 196
  0.7 54.4 %copy-start.13 = (bf16[3072]{0:T(1024)(128)(2,1)S(1)}, bf16[3072]{0:T(1024)(128)(2,1)}, u32[]{:S(2)}) copy-start(bf16[3072]{0:T(1024)(128)(2,1)} %param.12) | copy-start | bytes 18436
  0.7 61.0 %copy-start.12 = (bf16[4,3072]{1,0:T(4,128)(2,1)S(1)}, bf16[4,3072]{1,0:T(4,128)(2,1)}, u32[]{:S(2)}) copy-start(bf16[4,3072]{1,0:T(4,128)(2,1)} %param.11) | copy-start | bytes 73732
  2.2 43.8 %all-to-all-start = ((bf16[4,32,384]{2,1,0:T(8,128)(2,1)}), bf16[4,32,384]{2,1,0:T(8,128)(2,1)S(1)}, u32[]{:S(2)}, u32[]{:S(2)}) async-start(bf16[4,32,384]{2,1,0:T(8,128)(2,1)} %broadcast_in_dim.22), calls=%async_computation | async-start | bytes 196608 | tf_op jit(solution)/shard_map/all_to_all | solution.py:31
  47.1 14.6 %all-to-all-start.1 = ((bf16[32,4,768]{2,1,0:T(4,128)(2,1)}), bf16[32,4,768]{2,1,0:T(4,128)(2,1)S(1)}, u32[]{:S(2)}, u32[]{:S(2)}) async-start(bf16[32,4,768]{2,1,0:T(4,128)(2,1)} %reshape.77), calls=%async_computation.1 | async-start | bytes 393216 | tf_op jit(solution)/shard_map/all_to_all | solution.py:31
  55.1 36.6 %collective-permute-start = (bf16[3072,256]{1,0:T(8,128)(2,1)S(1)}, bf16[3072,256]{1,0:T(8,128)(2,1)}, u32[]{:S(2)}, u32[]{:S(2)}) collective-permute-start(bf16[3072,256]{1,0:T(8,128)(2,1)S(1)} %copy-done.1), channel_id=1, source_target_pairs={{0,1},{1,0},{2,3},{3,2},{4,5},{5,4},{6,7},{7,6},{8,9},{9,8},{10,11... | collective-permute-start | bytes 4718600 | tf_op jit(solution)/shard_map/ppermute | solution.py:45
  57.2 34.5 %collective-permute-start.1 = (bf16[3072,256]{1,0:T(8,128)(2,1)}, bf16[3072,256]{1,0:T(8,128)(2,1)}, u32[]{:S(2)}, u32[]{:S(2)}) collective-permute-start(bf16[3072,256]{1,0:T(8,128)(2,1)} %refs_3_.3), channel_id=1, source_target_pairs={{0,1},{1,0},{2,3},{3,2},{4,5},{5,4},{6,7},{7,6},{8,9},{9,8},{10,11... | collective-permute-start | bytes 4718600 | tf_op jit(solution)/shard_map/ppermute | solution.py:45
  59.5 32.2 %collective-permute-start.2 = (bf16[256,3072]{1,0:T(8,128)(2,1)}, bf16[256,3072]{1,0:T(8,128)(2,1)}, u32[]{:S(2)}, u32[]{:S(2)}) collective-permute-start(bf16[256,3072]{1,0:T(8,128)(2,1)} %refs_4_.3), channel_id=1, source_target_pairs={{0,1},{1,0},{2,3},{3,2},{4,5},{5,4},{6,7},{7,6},{8,9},{9,8},{10,11... | collective-permute-start | bytes 4718600 | tf_op jit(solution)/shard_map/ppermute | solution.py:45
  61.9 136.8 %copy-start.10 = (bf16[4,3072]{1,0:T(4,128)(2,1)}, bf16[4,3072]{1,0:T(4,128)(2,1)S(1)}, u32[]{:S(2)}) copy-start(bf16[4,3072]{1,0:T(4,128)(2,1)S(1)} %get-tuple-element.33) | copy-start | bytes 73732
  91.7 44.4 %copy-start.2 = (bf16[3072,256]{1,0:T(8,128)(2,1)S(1)}, bf16[3072,256]{1,0:T(8,128)(2,1)}, u32[]{:S(2)}) copy-start(bf16[3072,256]{1,0:T(8,128)(2,1)} %refs_3_.3) | copy-start | bytes 4718596
  110.5 22.3 %copy-start.5 = (bf16[4,128,768]{2,1,0:T(8,128)(2,1)}, bf16[4,128,768]{2,1,0:T(8,128)(2,1)S(1)}, u32[]{:S(2)}) copy-start(bf16[4,128,768]{2,1,0:T(8,128)(2,1)S(1)} %all_gather.7.refs_0_) | copy-start | bytes 2359300
  110.6 14.1 %collective-permute-start.3 = (bf16[2,128,768]{2,1,0:T(8,128)(2,1)S(1)}, bf16[2,128,768]{2,1,0:T(8,128)(2,1)S(1)}, u32[]{:S(2)}, u32[]{:S(2)}) collective-permute-start(bf16[2,128,768]{2,1,0:T(8,128)(2,1)S(1)} %get-tuple-element.35), channel_id=1, source_target_pairs={{0,2},{2,4},{4,6},{6,0},{1,3},{3,5},{5,7},{7,1},{8,10},{10,12},{12... | collective-permute-start | bytes 1179656 | tf_op jit(solution)/shard_map/ppermute | solution.py:153
  114.0 13.7 %collective-permute-start.5 = (bf16[2,128,768]{2,1,0:T(8,128)(2,1)S(1)}, bf16[2,128,768]{2,1,0:T(8,128)(2,1)S(1)}, u32[]{:S(2)}, u32[]{:S(2)}) collective-permute-start(bf16[2,128,768]{2,1,0:T(8,128)(2,1)S(1)} %get-tuple-element.34), channel_id=1, source_target_pairs={{0,6},{2,0},{4,2},{6,4},{1,7},{3,1},{5,3},{7,5},{8,14},{10,8},{12,... | collective-permute-start | bytes 1179656 | tf_op jit(solution)/shard_map/ppermute | solution.py:153
  117.7 15.2 %collective-permute-start.7 = (bf16[2,128,768]{2,1,0:T(8,128)(2,1)S(1)}, bf16[2,128,768]{2,1,0:T(8,128)(2,1)S(1)}, u32[]{:S(2)}, u32[]{:S(2)}) collective-permute-start(bf16[2,128,768]{2,1,0:T(8,128)(2,1)S(1)} %get-tuple-element.34), channel_id=1, source_target_pairs={{0,2},{2,4},{4,6},{6,0},{1,3},{3,5},{5,7},{7,1},{8,10},{10,12},{12... | collective-permute-start | bytes 1179656 | tf_op jit(solution)/shard_map/ppermute | solution.py:153
  119.8 16.2 %collective-permute-start.8 = (bf16[2,128,768]{2,1,0:T(8,128)(2,1)S(1)}, bf16[2,128,768]{2,1,0:T(8,128)(2,1)S(1)}, u32[]{:S(2)}, u32[]{:S(2)}) collective-permute-start(bf16[2,128,768]{2,1,0:T(8,128)(2,1)S(1)} %get-tuple-element.35), channel_id=1, source_target_pairs={{0,6},{2,0},{4,2},{6,4},{1,7},{3,1},{5,3},{7,5},{8,14},{10,8},{12,... | collective-permute-start | bytes 1179656 | tf_op jit(solution)/shard_map/ppermute | solution.py:153
  124.7 19.6 %collective-permute-start.4 = (bf16[2,128,768]{2,1,0:T(8,128)(2,1)S(1)}, bf16[2,128,768]{2,1,0:T(8,128)(2,1)S(1)}, u32[]{:S(2)}, u32[]{:S(2)}) collective-permute-start(bf16[2,128,768]{2,1,0:T(8,128)(2,1)S(1)} %collective-permute-done.3.refs_0_), channel_id=1, source_target_pairs={{0,2},{2,4},{4,6},{6,0},{1,3},{3,5},{5,7},{7,1},{8,10},{10,12},{12... | collective-permute-start | bytes 1179656 | tf_op jit(solution)/shard_map/ppermute | solution.py:153
  127.6 16.7 %collective-permute-start.6 = (bf16[2,128,768]{2,1,0:T(8,128)(2,1)S(1)}, bf16[2,128,768]{2,1,0:T(8,128)(2,1)S(1)}, u32[]{:S(2)}, u32[]{:S(2)}) collective-permute-start(bf16[2,128,768]{2,1,0:T(8,128)(2,1)S(1)} %collective-permute-done.5.refs_3_), channel_id=1, source_target_pairs={{0,6},{2,0},{4,2},{6,4},{1,7},{3,1},{5,3},{7,5},{8,14},{10,8},{12,... | collective-permute-start | bytes 1179656 | tf_op jit(solution)/shard_map/ppermute | solution.py:153
  136.1 1.4 copy-start.3
  142.5 0.9 copy-start.8
  143.4 0.9 copy-start.9
  148.2 0.9 copy-start.7
  149.1 22.9 %all-to-all-start.4 = ((bf16[4,128,768]{2,1,0:T(8,128)(2,1)}), bf16[4,128,768]{2,1,0:T(8,128)(2,1)}, u32[]{:S(2)}, u32[]{:S(2)}) async-start(bf16[4,128,768]{2,1,0:T(8,128)(2,1)} %copy-done.7), calls=%async_computation.4 | async-start | bytes 1572864 | tf_op jit(solution)/shard_map/all_to_all | solution.py:31
  153.3 16.2 %collective-permute-start.10 = (bf16[4,128,768]{2,1,0:T(8,128)(2,1)}, bf16[4,128,768]{2,1,0:T(8,128)(2,1)S(1)}, u32[]{:S(2)}, u32[]{:S(2)}) collective-permute-start(bf16[4,128,768]{2,1,0:T(8,128)(2,1)} %copy-done.9), channel_id=1, source_target_pairs={{0,2},{2,4},{4,6},{6,0},{1,3},{3,5},{5,7},{7,1},{8,10},{10,12},{12... | collective-permute-start | bytes 2359304 | tf_op jit(solution)/shard_map/ppermute | solution.py:153
  156.7 14.1 %collective-permute-start.9 = (bf16[4,128,768]{2,1,0:T(8,128)(2,1)}, bf16[4,128,768]{2,1,0:T(8,128)(2,1)S(1)}, u32[]{:S(2)}, u32[]{:S(2)}) collective-permute-start(bf16[4,128,768]{2,1,0:T(8,128)(2,1)} %copy-done.8), channel_id=1, source_target_pairs={{0,6},{2,0},{4,2},{6,4},{1,7},{3,1},{5,3},{7,5},{8,14},{10,8},{12,... | collective-permute-start | bytes 2359304 | tf_op jit(solution)/shard_map/ppermute | solution.py:153
  160.3 1.4 copy-start.4
  161.7 1.1 copy-start.6
  172.0 18.1 %all-to-all-start.3 = ((bf16[4,128,768]{2,1,0:T(8,128)(2,1)}), bf16[4,128,768]{2,1,0:T(8,128)(2,1)S(1)}, u32[]{:S(2)}, u32[]{:S(2)}) async-start(bf16[4,128,768]{2,1,0:T(8,128)(2,1)} %add_convert_fusion), calls=%async_computation.3 | async-start | bytes 1572864 | tf_op jit(solution)/shard_map/all_to_all | solution.py:31
  178.3 11.9 %collective-permute-start.11 = (bf16[128,768]{1,0:T(8,128)(2,1)S(1)}, bf16[128,768]{1,0:T(8,128)(2,1)S(1)}, u32[]{:S(2)}, u32[]{:S(2)}) collective-permute-start(bf16[128,768]{1,0:T(8,128)(2,1)S(1)} %reduce_sum.102), channel_id=1, source_target_pairs={{0,4},{2,6},{4,0},{6,2},{1,5},{3,7},{5,1},{7,3},{8,12},{10,14},{12... | collective-permute-start | bytes 589832 | tf_op jit(solution)/shard_map/ppermute | solution.py:153
  191.0 23.0 %all-to-all-start.5 = ((bf16[64,2,768]{2,1,0:T(2,128)(2,1)}), bf16[64,2,768]{2,1,0:T(2,128)(2,1)S(1)}, u32[]{:S(2)}, u32[]{:S(2)}) async-start(bf16[64,2,768]{2,1,0:T(2,128)(2,1)} %reshape.81), calls=%async_computation.5 | async-start | bytes 393216 | tf_op jit(solution)/shard_map/all_to_all | solution.py:31
